TPU v7x, 32 devices: a whole 2x2x4 slice. The times are simulated.
32 devices in a mesh: pair: 2 (over x), dp: 16 (over z, y, core).
Axes of the slice: x: 2, y: 2, z: 4, core: 2. Of those that a mesh axis runs over, the one named last changes fastest.
Arguments:
- token_shard: int32 [2, 16, 512, 1], P(None, 'dp'), may hold values from 0 to 15; in each aligned block of 512 rows (0 to 511, 512 to 1023, ..., all dimensions but the last counted through in order) at most 64 rows name the same one
- token_row: int32 [2, 16, 512], P(None, 'dp'), may hold values from 0 to 3143
- doc_ids: int32 [2, 16, 512], P(None, 'dp'), may hold values from 0 to 15, never falling along the last dimension, each value on 1 to 256 neighbouring positions
- loss_rows: int32 [2, 16, 16], P(None, 'dp'), may hold values from 0 to 510
- teacher_table: bfloat16 [50304, 768], P('dp'), may hold values from -0.41992188 to 0.41992188
- teacher_pos: bfloat16 [1024, 768], P('dp'), may hold values from -1.796875 to 1.796875
- teacher_attn_in: bfloat16 [768, 2304], P('dp'), may hold values from -0.21875 to 0.21875
- teacher_attn_out: bfloat16 [768, 768], P('dp'), may hold values from -0.875 to 0.875
- teacher_mlp_in: bfloat16 [768, 3072], P('dp'), may hold values from -0.21875 to 0.21875
- teacher_mlp_out: bfloat16 [3072, 768], P('dp'), may hold values from -0.21875 to 0.21875
- teacher_vecs: bfloat16 [14, 768], P(None, 'dp'), may hold values from -0.5 to 1.6, as said below
- table: float32 [50304, 768], P('dp'), may hold values from -0.42 to 0.42
- pos_table: float32 [1024, 768], P('dp'), may hold values from -1.8 to 1.8
- attn_in: float32 [768, 2304], P('dp'), may hold values from -0.21875 to 0.21875
- attn_out: float32 [768, 768], P('dp'), may hold values from -0.875 to 0.875
- mlp_in: float32 [768, 3072], P('dp'), may hold values from -0.21875 to 0.21875
- mlp_out: float32 [3072, 768], P('dp'), may hold values from -0.21875 to 0.21875
- vectors: float32 [14, 768], P(None, 'dp'), may hold values from -0.5 to 1.6, as said below
- table_m: float32 [50304, 768], P('dp'), may hold values from -1.8626451e-08 to 1.8626451e-08
- pos_m: float32 [1024, 768], P('dp'), may hold values from -1.9073486e-06 to 1.9073486e-06
- attn_in_m: float32 [768, 2304], P('dp'), may hold values from -1.9073486e-06 to 1.9073486e-06
- attn_out_m: float32 [768, 768], P('dp'), may hold values from -1.9073486e-06 to 1.9073486e-06
- mlp_in_m: float32 [768, 3072], P('dp'), may hold values from -1.9073486e-06 to 1.9073486e-06
- mlp_out_m: float32 [3072, 768], P('dp'), may hold values from -1.9073486e-06 to 1.9073486e-06
- vectors_m: float32 [14, 768], P(None, 'dp'), may hold values from -9.536743e-06 to 9.536743e-06
- table_v: float32 [50304, 768], P('dp'), may hold values from 8.60057e-15 to 3.440228e-14
- pos_v: float32 [1024, 768], P('dp'), may hold values from 8.60057e-15 to 3.440228e-14
- attn_in_v: float32 [768, 2304], P('dp'), may hold values from 8.60057e-15 to 3.440228e-14
- attn_out_v: float32 [768, 768], P('dp'), may hold values from 8.60057e-15 to 3.440228e-14
- mlp_in_v: float32 [768, 3072], P('dp'), may hold values from 8.60057e-15 to 3.440228e-14
- mlp_out_v: float32 [3072, 768], P('dp'), may hold values from 8.60057e-15 to 3.440228e-14
- vectors_v: float32 [14, 768], P(None, 'dp'), may hold values from 2.1501426e-13 to 8.6005703e-13
Outputs:
- table_new: float32 [50304, 768], P('dp')
- table_m_new: float32 [50304, 768], P('dp')
- table_v_new: float32 [50304, 768], P('dp')
- pos_new: float32 [1024, 768], P('dp')
- pos_m_new: float32 [1024, 768], P('dp')
- pos_v_new: float32 [1024, 768], P('dp')
- attn_in_new: float32 [768, 2304], P('dp')
- attn_in_m_new: float32 [768, 2304], P('dp')
- attn_in_v_new: float32 [768, 2304], P('dp')
- attn_out_new: float32 [768, 768], P('dp')
- attn_out_m_new: float32 [768, 768], P('dp')
- attn_out_v_new: float32 [768, 768], P('dp')
- mlp_in_new: float32 [768, 3072], P('dp')
- mlp_in_m_new: float32 [768, 3072], P('dp')
- mlp_in_v_new: float32 [768, 3072], P('dp')
- mlp_out_new: float32 [3072, 768], P('dp')
- mlp_out_m_new: float32 [3072, 768], P('dp')
- mlp_out_v_new: float32 [3072, 768], P('dp')
- vectors_new: float32 [14, 768], P(None, 'dp')
- vectors_m_new: float32 [14, 768], P(None, 'dp')
- vectors_v_new: float32 [14, 768], P(None, 'dp')
- grad_norm: float32 [], replicated
- kl_mean: float32 [], replicated
Inputs may be any that keep to these rules, and one draw needn't show every extreme that they name: `token_shard`: in each micro-batch at most 64 tokens of one device's sequence fall into one vocabulary shard. `doc_ids`: document ids never fall along a sequence; a document has at most 256 tokens. `loss_rows`: positions may repeat; each repeat counts again. `teacher_vecs`: rows 0, 2 and 4 hold norms' gains, the others biases. `vectors`: rows 0, 2 and 4 hold norms' gains, the others biases.
All inputs are finite; a program needn't handle non-finite values.
Results may differ from a plain program's by a relative error of at most 0.015.
The roundings to bfloat16 on the way count: a program that leaves them out, or rounds other values in their place, can miss the bound.
Values may be sent and summed in bfloat16 or wider, within the bound.
No kernel may reach another device: no remote copies, remote signals or barrier semaphores. Data moves between devices by JAX's collectives and lax.ppermute only.
A program may use at most 256 MiB of HBM per device.

v0:
```python
import jax
import jax.numpy as jnp
from jax import lax
from jax.sharding import PartitionSpec as P

H = 12
MB = 2
STEP = 10


learn_rate = 0.25
beta_one = 0.9
beta_two = 0.999
adam_eps = 1e-08
decay_rate = 0.1
clip_limit = 0.02
norm_eps = 1e-05
neg_big = -1000000000.0


def joined(value, axis, combine):
    everything = jax.tree.map(lambda part: lax.all_gather(part, axis), value)
    initial = jax.tree.map(lambda part: part[0], everything)

    def lap(k, so_far):
        return combine(so_far, jax.tree.map(lambda part: part[k], everything))

    return lax.fori_loop(1, lax.axis_size(axis), lap, initial)


def from_behind(block, axis, distance):
    devices = range(lax.axis_size(axis))
    route = [(i - distance, i) for i in devices if i - distance in devices]
    return lax.ppermute(block, axis, route)


def layer_norm(values, norm_gain, norm_shift):
    center = jnp.mean(values, axis=-1, keepdims=True)
    offsets = values - center
    spread = jnp.mean(offsets * offsets, axis=-1, keepdims=True)
    return offsets * lax.rsqrt(spread + norm_eps) * norm_gain + norm_shift


def gelu_tanh(values):
    return jax.nn.gelu(values, approximate=True)


def doc_positions(doc_row):
    indices = jnp.arange(doc_row.shape[0], dtype=jnp.int32)
    starts_here = jnp.concatenate([jnp.ones((1,), dtype=bool), doc_row[1:] != doc_row[:-1]])
    first_index = lax.cummax(jnp.where(starts_here, indices, 0), axis=0)
    return indices - first_index


def dot_plain(left_side, right_side):
    return jnp.dot(left_side, right_side, preferred_element_type=jnp.float32)


def dot_first(left_side, right_side):
    return lax.dot_general(
        left_side, right_side, (((0,), (0,)), ((), ())), preferred_element_type=jnp.float32
    )


def dot_last(left_side, right_side):
    return lax.dot_general(
        left_side, right_side, (((1,), (1,)), ((), ())), preferred_element_type=jnp.float32
    )


def block_masks(doc_row, begin_at, stop_at):
    indices = jnp.arange(doc_row.shape[0])
    same_doc = doc_row[begin_at:stop_at, None] == doc_row[None, :stop_at]
    return same_doc & (indices[None, :stop_at] <= indices[begin_at:stop_at, None])


def attention_forward(qkv_low, doc_row, head_count):
    length = qkv_low.shape[0]
    model_width = qkv_low.shape[1] // 3
    head_size = model_width // head_count
    split_parts = qkv_low.reshape(length, 3, head_count, head_size)
    queries, keys_all, values = (split_parts[:, 0], split_parts[:, 1], split_parts[:, 2])
    scaling = head_size ** (-0.5)
    block_rows = min(512, length)
    allowed = block_masks(doc_row, 0, block_rows)
    scores = (
        jnp.einsum("qhd,khd->hqk", queries, keys_all, preferred_element_type=jnp.float32) * scaling
    )
    scores = jnp.where(allowed[None], scores, neg_big)
    row_max = jnp.max(scores, axis=-1, keepdims=True)
    weights_exp = jnp.exp(scores - row_max)
    row_total = jnp.sum(weights_exp, axis=-1, keepdims=True)
    probs = (weights_exp / row_total).astype(jnp.bfloat16)
    results = jnp.einsum("hqk,khd->qhd", probs, values, preferred_element_type=jnp.float32)
    log_totals = (row_max + jnp.log(row_total))[..., 0]
    attended = results.reshape(length, model_width).astype(jnp.bfloat16)
    return (attended, log_totals)


def attention_backward(d_attended, qkv_low, doc_row, log_totals, head_count):
    length = qkv_low.shape[0]
    model_width = qkv_low.shape[1] // 3
    head_size = model_width // head_count
    split_parts = qkv_low.reshape(length, 3, head_count, head_size)
    queries, keys_all, values = (split_parts[:, 0], split_parts[:, 1], split_parts[:, 2])
    d_heads = d_attended.reshape(length, head_count, head_size)
    scaling = head_size ** (-0.5)
    block_rows = min(512, length)
    allowed = block_masks(doc_row, 0, block_rows)
    scores = (
        jnp.einsum("qhd,khd->hqk", queries, keys_all, preferred_element_type=jnp.float32) * scaling
    )
    scores = jnp.where(allowed[None], scores, neg_big)
    probs = jnp.exp(scores - log_totals[:, 0:block_rows, None])
    d_probs = jnp.einsum("qhd,khd->hqk", d_heads, values, preferred_element_type=jnp.float32)
    row_inner = jnp.sum(probs * d_probs, axis=-1, keepdims=True)
    d_scores = (probs * (d_probs - row_inner)).astype(jnp.bfloat16)
    query_grads = (
        jnp.einsum("hqk,khd->qhd", d_scores, keys_all, preferred_element_type=jnp.float32) * scaling
    )
    key_part = (
        jnp.einsum("hqk,qhd->khd", d_scores, queries, preferred_element_type=jnp.float32) * scaling
    )
    value_part = jnp.einsum(
        "hqk,qhd->khd", probs.astype(jnp.bfloat16), d_heads, preferred_element_type=jnp.float32
    )
    stacked = jnp.stack([query_grads, key_part, value_part], axis=1)
    return stacked.reshape(length, 3 * model_width).astype(jnp.bfloat16)


def layer_forward(embedded, positions, doc_row, weights):
    w_attn_in, w_attn_out, w_mlp_in, w_mlp_out, w_pos, w_vecs = weights
    vec_full = w_vecs.astype(jnp.float32)
    model_width = w_attn_out.shape[1]
    x_embed = embedded.astype(jnp.float32) + jnp.take(w_pos, positions, axis=0).astype(jnp.float32)
    normed_one = layer_norm(x_embed, vec_full[0], vec_full[1]).astype(jnp.bfloat16)
    qkv_bias = jnp.concatenate([vec_full[6], jnp.zeros((model_width,), jnp.float32), vec_full[7]])
    qkv_low = (dot_plain(normed_one, w_attn_in) + qkv_bias).astype(jnp.bfloat16)
    attended, log_totals = attention_forward(qkv_low, doc_row, H)
    x_mid = x_embed + dot_plain(attended, w_attn_out) + vec_full[8]
    normed_two = layer_norm(x_mid, vec_full[2], vec_full[3]).astype(jnp.bfloat16)
    pre_act = dot_plain(normed_two, w_mlp_in) + vec_full[10:].reshape(-1)
    activated = gelu_tanh(pre_act).astype(jnp.bfloat16)
    x_top = x_mid + dot_plain(activated, w_mlp_out) + vec_full[9]
    return (
        x_top,
        (x_embed, normed_one, qkv_low, attended, log_totals, x_mid, normed_two, pre_act, activated),
    )


def layer_backward(grad_top, weights, kept, positions, doc_row, final_pair):
    w_attn_in, w_attn_out, w_mlp_in, w_mlp_out, w_pos, w_vecs = weights
    vec_full = w_vecs.astype(jnp.float32)
    x_embed, normed_one, qkv_low, attended, log_totals, x_mid, normed_two, pre_act, activated = kept
    model_width = w_attn_out.shape[1]
    d_branch = grad_top.astype(jnp.bfloat16)
    g_mlp_out = dot_first(activated, d_branch)
    d_act = dot_last(d_branch, w_mlp_out)
    gelu_back = jax.vjp(gelu_tanh, pre_act)[1]
    d_pre = gelu_back(d_act)[0].astype(jnp.bfloat16)
    g_mlp_in = dot_first(normed_two, d_pre)
    d_normed_two = dot_last(d_pre, w_mlp_in)
    norm_two_back = jax.vjp(layer_norm, x_mid, vec_full[2], vec_full[3])[1]
    d_mid, d_gain_two, d_shift_two = norm_two_back(d_normed_two)
    d_mid = grad_top + d_mid
    d_attn_branch = d_mid.astype(jnp.bfloat16)
    g_attn_out = dot_first(attended, d_attn_branch)
    d_attended = dot_last(d_attn_branch, w_attn_out).astype(jnp.bfloat16)
    d_qkv = attention_backward(d_attended, qkv_low, doc_row, log_totals, H)
    g_attn_in = dot_first(normed_one, d_qkv)
    d_normed_one = dot_last(d_qkv, w_attn_in)
    norm_one_back = jax.vjp(layer_norm, x_embed, vec_full[0], vec_full[1])[1]
    d_embed, d_gain_one, d_shift_one = norm_one_back(d_normed_one)
    d_embed = d_mid + d_embed
    g_pos = jnp.zeros(w_pos.shape, jnp.float32).at[positions].add(d_embed)
    qkv_sums = jnp.sum(d_qkv, axis=0, dtype=jnp.float32)
    vector_part = jnp.stack(
        [
            d_gain_one,
            d_shift_one,
            d_gain_two,
            d_shift_two,
            final_pair[0],
            final_pair[1],
            qkv_sums[:model_width],
            qkv_sums[2 * model_width :],
            jnp.sum(d_attn_branch, axis=0, dtype=jnp.float32),
            jnp.sum(d_branch, axis=0, dtype=jnp.float32),
        ]
    )
    bias_part = jnp.sum(d_pre, axis=0, dtype=jnp.float32).reshape(-1, model_width)
    g_vecs = jnp.concatenate([vector_part, bias_part], axis=0)
    return (d_embed, (g_attn_in, g_attn_out, g_mlp_in, g_mlp_out, g_pos, g_vecs))


def combine_stats(first_pair, second_pair):
    joint_max = jnp.maximum(first_pair[0], second_pair[0])
    joint_sum = first_pair[1] * jnp.exp(first_pair[0] - joint_max) + second_pair[1] * jnp.exp(
        second_pair[0] - joint_max
    )
    return (joint_max, joint_sum)


def row_terms(d_low, table_low):
    return dot_plain(d_low, table_low)


def adam_update(master, moment_one, moment_two, gradient, factor):
    clipped = gradient * factor
    new_one = beta_one * moment_one + (1.0 - beta_one) * clipped
    new_two = beta_two * moment_two + (1.0 - beta_two) * clipped * clipped
    fixed_one = new_one / (1.0 - beta_one**STEP)
    fixed_two = new_two / (1.0 - beta_two**STEP)
    updated = master - learn_rate * (
        fixed_one / (jnp.sqrt(fixed_two) + adam_eps) + decay_rate * master
    )
    return (updated, new_one, new_two)


def shards(
    token_shard,
    token_row,
    doc_ids,
    loss_rows,
    teacher_table,
    teacher_pos,
    teacher_attn_in,
    teacher_attn_out,
    teacher_mlp_in,
    teacher_mlp_out,
    teacher_vecs,
    table,
    pos_table,
    attn_in,
    attn_out,
    mlp_in,
    mlp_out,
    vectors,
    table_m,
    pos_m,
    attn_in_m,
    attn_out_m,
    mlp_in_m,
    mlp_out_m,
    vectors_m,
    table_v,
    pos_v,
    attn_in_v,
    attn_out_v,
    mlp_in_v,
    mlp_out_v,
    vectors_v,
):
    is_student = lax.axis_index("pair") == 1
    student_weight = is_student.astype(jnp.float32)
    low_attn_in = jnp.where(is_student, attn_in.astype(jnp.bfloat16), teacher_attn_in)
    low_attn_out = jnp.where(is_student, attn_out.astype(jnp.bfloat16), teacher_attn_out)
    low_mlp_in = jnp.where(is_student, mlp_in.astype(jnp.bfloat16), teacher_mlp_in)
    low_mlp_out = jnp.where(is_student, mlp_out.astype(jnp.bfloat16), teacher_mlp_out)
    low_pos = jnp.where(is_student, pos_table.astype(jnp.bfloat16), teacher_pos)
    low_vecs = jnp.where(is_student, vectors.astype(jnp.bfloat16), teacher_vecs)
    table_low = jnp.where(is_student, table.astype(jnp.bfloat16), teacher_table)
    vocab_rows = table.shape[0]
    model_width = table.shape[1]
    devices = lax.axis_size("dp")
    vocab_offset = lax.axis_index("dp") * vocab_rows
    pick_count = loss_rows.shape[2]
    total_rows = MB * devices * pick_count
    vocab_iota = jnp.arange(vocab_rows, dtype=jnp.int32)
    table_grad = jnp.zeros((vocab_rows, model_width), jnp.float32)
    kl_local = jnp.zeros((), jnp.float32)
    reduced = None
    for micro_step in range(MB):
        gathered = (
            lax.all_gather(low_attn_in, "dp", axis=0, tiled=True),
            lax.all_gather(low_attn_out, "dp", axis=0, tiled=True),
            lax.all_gather(low_mlp_in, "dp", axis=0, tiled=True),
            lax.all_gather(low_mlp_out, "dp", axis=0, tiled=True),
            lax.all_gather(low_pos, "dp", axis=0, tiled=True),
            lax.all_gather(low_vecs, "dp", axis=1, tiled=True),
        )
        owners = token_shard[micro_step, 0, :, 0]
        shard_rows = token_row[micro_step, 0]
        doc_row = doc_ids[micro_step, 0]
        chosen = loss_rows[micro_step, 0]
        length = owners.shape[0]
        capacity = 2 * length // devices
        positions = doc_positions(doc_row)
        owner_hits = (owners[:, None] == jnp.arange(devices, dtype=jnp.int32)[None, :]).astype(
            jnp.int32
        )
        slot_index = jnp.sum(jnp.cumsum(owner_hits, axis=0) * owner_hits, axis=1) - 1
        request = (
            jnp.full((devices, capacity), vocab_rows, jnp.int32)
            .at[owners, slot_index]
            .set(shard_rows)
        )
        asked_here = lax.all_to_all(request, "dp", split_axis=0, concat_axis=0, tiled=True)
        present = asked_here < vocab_rows
        found_rows = jnp.take(table_low, jnp.minimum(asked_here, vocab_rows - 1), axis=0)
        found_rows = jnp.where(present[..., None], found_rows, jnp.zeros_like(found_rows))
        came_back = lax.all_to_all(found_rows, "dp", split_axis=0, concat_axis=0, tiled=True)
        embedded = came_back[owners, slot_index]
        x_top, kept = layer_forward(embedded, positions, doc_row, gathered)
        vec_full = gathered[5].astype(jnp.float32)
        final_in = x_top[chosen]
        normed_final, final_back = jax.vjp(layer_norm, final_in, vec_full[4], vec_full[5])
        next_ids = owners[chosen + 1] * vocab_rows + shard_rows[chosen + 1]
        hidden_all, target_all = (
            lax.all_gather(normed_final.astype(jnp.bfloat16), "dp", axis=0, tiled=True),
            lax.all_gather(next_ids, "dp", axis=0, tiled=True),
        )
        logits = dot_last(hidden_all, table_low)
        local_max = jnp.max(logits, axis=1)
        local_sum = jnp.sum(jnp.exp(logits - local_max[:, None]), axis=1)
        big_max, big_sum = joined((local_max, local_sum), "dp", combine_stats)
        log_total = big_max + jnp.log(big_sum)
        other_logits, other_total = from_behind((logits, log_total), "pair", 1)
        own_prob = jnp.exp(logits - log_total[:, None])
        other_log_prob = other_logits - other_total[:, None]
        other_prob = jnp.exp(other_log_prob)
        kl_rows = jnp.sum(other_prob * (other_log_prob - logits + log_total[:, None]), axis=1)
        kl_local = kl_local + student_weight * jnp.sum(kl_rows)
        target_hit = ((target_all - vocab_offset)[:, None] == vocab_iota[None, :]).astype(
            jnp.float32
        )
        d_logits = student_weight / total_rows * (2.0 * own_prob - target_hit - other_prob)
        d_low = d_logits.astype(jnp.bfloat16)
        d_final = lax.psum_scatter(
            row_terms(d_low, table_low), "dp", scatter_dimension=0, tiled=True
        )
        table_grad = table_grad + dot_first(d_low, hidden_all)
        d_final_in, d_gain_final, d_shift_final = final_back(d_final)
        grad_top = jnp.zeros_like(x_top).at[chosen].add(d_final_in)
        back_weights = (
            lax.all_gather(low_attn_in, "dp", axis=0, tiled=True),
            lax.all_gather(low_attn_out, "dp", axis=0, tiled=True),
            lax.all_gather(low_mlp_in, "dp", axis=0, tiled=True),
            lax.all_gather(low_mlp_out, "dp", axis=0, tiled=True),
            lax.all_gather(low_pos, "dp", axis=0, tiled=True),
            lax.all_gather(low_vecs, "dp", axis=1, tiled=True),
        )
        d_embed, grads = layer_backward(
            grad_top, back_weights, kept, positions, doc_row, (d_gain_final, d_shift_final)
        )
        sent_rows = (
            jnp.zeros((devices, capacity, model_width), jnp.bfloat16)
            .at[owners, slot_index]
            .set(d_embed.astype(jnp.bfloat16))
        )
        arrived = lax.all_to_all(sent_rows, "dp", split_axis=0, concat_axis=0, tiled=True)
        table_grad = table_grad.at[asked_here.reshape(-1)].add(
            arrived.reshape(-1, model_width).astype(jnp.float32), mode="drop"
        )
        shares = (
            lax.psum_scatter(grads[0], "dp", scatter_dimension=0, tiled=True),
            lax.psum_scatter(grads[1], "dp", scatter_dimension=0, tiled=True),
            lax.psum_scatter(grads[2], "dp", scatter_dimension=0, tiled=True),
            lax.psum_scatter(grads[3], "dp", scatter_dimension=0, tiled=True),
            lax.psum_scatter(grads[4], "dp", scatter_dimension=0, tiled=True),
            lax.psum_scatter(grads[5], "dp", scatter_dimension=1, tiled=True),
        )
        reduced = (
            shares
            if reduced is None
            else tuple((left_part + right_part for left_part, right_part in zip(reduced, shares)))
        )
    summed = lax.psum(
        (reduced[0], reduced[1], reduced[2], reduced[3], reduced[4], reduced[5], table_grad), "pair"
    )
    squares = jnp.zeros((), jnp.float32)
    for gradient in summed:
        squares = squares + jnp.sum(gradient * gradient)
    step_totals = lax.psum((student_weight * squares, kl_local), ("pair", "dp"))
    grad_norm = jnp.sqrt(step_totals[0])
    kl_mean = step_totals[1] / total_rows
    factor = jnp.minimum(1.0, clip_limit / (grad_norm + 1e-06))
    table_out = adam_update(table, table_m, table_v, summed[6], factor)
    pos_out = adam_update(pos_table, pos_m, pos_v, summed[4], factor)
    attn_in_out = adam_update(attn_in, attn_in_m, attn_in_v, summed[0], factor)
    attn_out_out = adam_update(attn_out, attn_out_m, attn_out_v, summed[1], factor)
    mlp_in_out = adam_update(mlp_in, mlp_in_m, mlp_in_v, summed[2], factor)
    mlp_out_out = adam_update(mlp_out, mlp_out_m, mlp_out_v, summed[3], factor)
    vectors_out = adam_update(vectors, vectors_m, vectors_v, summed[5], factor)
    return (
        table_out[0],
        table_out[1],
        table_out[2],
        pos_out[0],
        pos_out[1],
        pos_out[2],
        attn_in_out[0],
        attn_in_out[1],
        attn_in_out[2],
        attn_out_out[0],
        attn_out_out[1],
        attn_out_out[2],
        mlp_in_out[0],
        mlp_in_out[1],
        mlp_in_out[2],
        mlp_out_out[0],
        mlp_out_out[1],
        mlp_out_out[2],
        vectors_out[0],
        vectors_out[1],
        vectors_out[2],
        grad_norm,
        kl_mean,
    )


def solution(mesh):
    return jax.shard_map(
        shards,
        mesh=mesh,
        in_specs=(
            P(None, "dp", None, None),
            P(None, "dp", None),
            P(None, "dp", None),
            P(None, "dp", None),
            P("dp", None),
            P("dp", None),
            P("dp", None),
            P("dp", None),
            P("dp", None),
            P("dp", None),
            P(None, "dp"),
            P("dp", None),
            P("dp", None),
            P("dp", None),
            P("dp", None),
            P("dp", None),
            P("dp", None),
            P(None, "dp"),
            P("dp", None),
            P("dp", None),
            P("dp", None),
            P("dp", None),
            P("dp", None),
            P("dp", None),
            P(None, "dp"),
            P("dp", None),
            P("dp", None),
            P("dp", None),
            P("dp", None),
            P("dp", None),
            P("dp", None),
            P(None, "dp"),
        ),
        out_specs=(
            P("dp", None),
            P("dp", None),
            P("dp", None),
            P("dp", None),
            P("dp", None),
            P("dp", None),
            P("dp", None),
            P("dp", None),
            P("dp", None),
            P("dp", None),
            P("dp", None),
            P("dp", None),
            P("dp", None),
            P("dp", None),
            P("dp", None),
            P("dp", None),
            P("dp", None),
            P("dp", None),
            P(None, "dp"),
            P(None, "dp"),
            P(None, "dp"),
            P(),
            P(),
        ),
        check_vma=False,
    )
```

profile of v0, /device:TPU:0, one launch (start us, length us, event | category | flops | bytes accessed | tf_op | source)
XLA Modules:
  0.0 1861.7 jit_solution(17856079774361817829)
XLA Ops:
  18.4 70.8 %scatter_fusion.1 = s32[16,64]{1,0:T(8,128)} fusion(s32[16,64]{1,0:T(8,128)} %broadcast.660.clone, s32[512]{0:T(512)S(1)} %bitcast.316, s32[512]{0:T(512)S(1)} %bitcast.314), kind=kCustom, calls=%fused_computation.13 | custom fusion | bytes 10240 | tf_op jit(solution)/shard_map/scatter | solution.py:296
  98.2 70.7 %scatter_fusion = s32[16,64]{1,0:T(8,128)} fusion(s32[16,64]{1,0:T(8,128)} %broadcast.660.clone.1, s32[512]{0:T(512)S(1)} %bitcast.318, s32[512]{0:T(512)S(1)} %bitcast.312), kind=kCustom, calls=%fused_computation.12 | custom fusion | bytes 10240 | tf_op jit(solution)/shard_map/scatter | solution.py:296
  204.7 47.3 %all-gather.4 = bf16[16,48,14]{1,2,0:T(8,128)(2,1)S(1)} all-gather(bf16[1,48,14]{1,2,0:T(8,128)(2,1)S(1)} %select_bitcast_fusion), channel_id=1, replica_groups=mesh['pair'=2,'dp'=16] {'dp'}, dimensions={0}, use_global_device_ids=true | all-gather | bytes 22848 | tf_op jit(solution)/shard_map/all_gather | solution.py:280
  262.4 15.5 all-to-all-start.1
  278.6 38.1 %all-reduce.2 = (s32[256]{0:T(256)}, s32[256]{0:T(256)S(1)}) all-reduce(s32[256]{0:T(256)S(1)} %add_dynamic-update-slice_fusion.1, s32[256]{0:T(256)S(1)} %add_dynamic-update-slice_fusion), channel_id=1, replica_groups=mesh['pair'=2,'dp'=16] {'dp'}, use_global_device_ids=true, to_apply=%add | all-reduce | flops 512 | bytes 4096
  401.4 9.4 add_add_fusion.8
  428.8 20.6 %all_gather.76 = bf16[256,768]{1,0:T(8,128)(2,1)S(1)} all-gather(bf16[16,768]{1,0:T(8,128)(2,1)S(1)} %get-tuple-element.431), channel_id=1, replica_groups=mesh['pair'=2,'dp'=16] {'dp'}, dimensions={0}, use_global_device_ids=true | all-gather | bytes 417792 | tf_op jit(solution)/shard_map/all_gather | solution.py:310
  454.0 17.4 all-gather.6
  472.0 18.8 %all-gather.5 = f32[16,1,256]{2,1,0:T(1,128)S(1)} all-gather(f32[1,1,256]{2,1,0:T(1,128)S(1)} %bitcast.373), channel_id=2, replica_groups=mesh['pair'=2,'dp'=16] {'dp'}, dimensions={0}, use_global_device_ids=true | all-gather | bytes 17408 | tf_op jit(solution)/shard_map/all_gather | solution.py:22
  491.4 18.9 %all_gather.82 = bf16[256,768]{1,0:T(8,128)(2,1)S(1)} all-gather(bf16[16,768]{1,0:T(8,128)(2,1)S(1)} %get-tuple-element.430), channel_id=1, replica_groups=mesh['pair'=2,'dp'=16] {'dp'}, dimensions={0}, use_global_device_ids=true | all-gather | bytes 417792 | tf_op jit(solution)/shard_map/all_gather | solution.py:310
  516.2 18.8 %all-gather.8 = f32[16,1,256]{2,1,0:T(1,128)S(1)} all-gather(f32[1,1,256]{2,1,0:T(1,128)S(1)} %bitcast.380), channel_id=5, replica_groups=mesh['pair'=2,'dp'=16] {'dp'}, dimensions={0}, use_global_device_ids=true | all-gather | bytes 17408 | tf_op jit(solution)/shard_map/all_gather | solution.py:22
  535.6 17.4 all-gather.7
  559.6 11.3 while.34
  570.9 11.4 while.35
  584.9 108.9 %collective-permute-done.3 = f32[256]{0:T(256)S(1)} collective-permute-done((f32[256]{0:T(256)S(1)}, f32[256]{0:T(256)S(1)}, u32[]{:S(2)}, u32[]{:S(2)}) %collective-permute-start.3) | collective-permute-done | bytes 1056 | tf_op jit(solution)/shard_map/ppermute | solution.py:34
  717.2 44.2 %reduce-scatter.13.cloned.1.call-done = f32[16,768]{1,0:T(8,128)} async-done(((f32[256,768]{1,0:T(8,128)}), f32[16,768]{1,0:T(8,128)}) %reduce-scatter.13.cloned.1.call-update) | async-done | bytes 49168 | tf_op jit(solution)/shard_map/reduce_scatter | solution.py:329
  761.4 59.5 %reduce-scatter.11.cloned.1.call-done = f32[16,768]{1,0:T(8,128)} async-done(((f32[256,768]{1,0:T(8,128)}), f32[16,768]{1,0:T(8,128)}) %reduce-scatter.11.cloned.1.call-update) | async-done | bytes 49168 | tf_op jit(solution)/shard_map/reduce_scatter | solution.py:329
  827.2 10.2 convert_reduce_fusion
  837.4 10.7 convert_reduce_fusion.1
  872.5 9.8 multiply_reduce_fusion
  908.6 9.7 multiply_reduce_fusion.1
  990.5 10.4 convolution_add_fusion.2
  1014.5 69.0 %scatter_fusion.2 = bf16[16,64,768]{2,1,0:T(8,128)(2,1)} fusion(bf16[16,64,768]{2,1,0:T(8,128)(2,1)} %broadcast.668.clone, s32[512]{0:T(512)S(1)} %bitcast.319, bf16[512,768]{1,0:T(8,128)(2,1)S(1)} %copy-done.56), kind=kCustom, calls=%fused_computation.15 | custom fusion | bytes 2363392 | tf_op jit(solution)/shard_map/scatter | solution.py:349
  1088.8 68.5 %scatter_fusion.3 = bf16[16,64,768]{2,1,0:T(8,128)(2,1)} fusion(bf16[16,64,768]{2,1,0:T(8,128)(2,1)} %broadcast.668.clone.1, s32[512]{0:T(512)S(1)} %bitcast.317, bf16[512,768]{1,0:T(8,128)(2,1)S(1)} %copy-done.57), kind=kCustom, calls=%fused_computation.18 | custom fusion | bytes 2363392 | tf_op jit(solution)/shard_map/scatter | solution.py:349
  1181.5 14.9 scatter_custom_fusion.4
  1204.5 16.5 scatter_custom_fusion.7
  1221.1 86.1 %reduce-scatter.21.cloned.1.call-done = f32[192,768]{1,0:T(8,128)} async-done(((f32[3072,768]{1,0:T(8,128)}), f32[192,768]{1,0:T(8,128)}) %reduce-scatter.21.cloned.1.call-update) | async-done | bytes 589840 | tf_op jit(solution)/shard_map/reduce_scatter | solution.py:359
  1307.1 116.2 %reduce-scatter.19.cloned.1.call-done = f32[48,3072]{1,0:T(8,128)} async-done(((f32[768,3072]{1,0:T(8,128)}), f32[48,3072]{1,0:T(8,128)}) %reduce-scatter.19.cloned.1.call-update) | async-done | bytes 589840 | tf_op jit(solution)/shard_map/reduce_scatter | solution.py:358
  1424.7 58.1 %reduce-scatter.25.cloned.1.call-done = f32[48,14]{1,0:T(8,128)} async-done(((f32[768,14]{1,0:T(8,128)}), f32[48,14]{1,0:T(8,128)}) %reduce-scatter.25.cloned.1.call-update) | async-done | bytes 2704
  1489.2 266.7 %all-reduce.7.cloned.1.call-done = (f32[3144,768]{1,0:T(8,128)}, f32[48,2304]{1,0:T(8,128)}, f32[48,768]{1,0:T(8,128)}, f32[48,3072]{1,0:T(8,128)}, f32[192,768]{1,0:T(8,128)}, /*index=5*/f32[64,768]{1,0:T(8,128)}) async-done(((f32[3144,768]{1,0:T(8,128)}, f32[48,2304]{1,0:T(8,128)}, f32[48,768]{1,0:T(8,128)}, f32[48,3072]{1,0:T(8,128)}, f32[192,768]{1,0:T(8,128)}, /*index=5*/f32[64,768]{1,0:T(8,128)}), ...) | async-done | bytes 11624464 | tf_op jit(solution)/shard_map/psum | solution.py:368
  1776.0 40.1 %all-reduce.3 = (f32[]{:T(128)}, f32[]{:T(128)}) all-reduce(f32[]{:T(128)S(6)} %mul.980, f32[]{:T(128)S(6)} %add.885), channel_id=1, replica_groups=mesh['pair'=2,'dp'=16] {'pair','dp'}, use_global_device_ids=true, to_apply=%region_106.109 | all-reduce | flops 2 | bytes 16 | tf_op jit(solution)/shard_map/psum | solution.py:374
  1828.3 24.4 %multiply_subtract_fusion = (f32[3144,768]{1,0:T(8,128)}, f32[3144,768]{1,0:T(8,128)}, f32[3144,768]{1,0:T(8,128)}) fusion(f32[3144,768]{1,0:T(8,128)} %param.51, f32[3144,768]{1,0:T(8,128)} %get-tuple-element.349, f32[]{:T(128)S(6)} %min.19, f32[3144,768]{1,0:T(8,128)} %param.58, f32[3144,768]{1,0:T(8,128)} %param.65), kind=kLoop, calls=%fused_computation.44 | loop fusion | flops 38633472 | bytes 67608576 | tf_op jit(solution)/shard_map/sub | solution.py:214
  (747 shorter events, 446.7 us)
Async XLA Ops:
  7.2 312.6 %all-gather.15.cloned.1.call-start = ((), (), s32[]{:S(2)}) async-start(), calls=%async_computation.14 | async-start | bytes 1671168 | tf_op jit(solution)/shard_map/all_gather | solution.py:279
  8.9 333.0 %all-gather.17.cloned.1.call-start = ((), (), s32[]{:S(2)}) async-start(), calls=%async_computation.15 | async-start | bytes 3760128 | tf_op jit(solution)/shard_map/all_gather | solution.py:275
  10.9 365.7 %all-gather.19.cloned.1.call-start = ((), (), s32[]{:S(2)}) async-start(), calls=%async_computation.16 | async-start | bytes 1253376 | tf_op jit(solution)/shard_map/all_gather | solution.py:276
  12.6 381.5 %all-gather.21.cloned.1.call-start = ((), (), s32[]{:S(2)}) async-start(), calls=%async_computation.17 | async-start | bytes 5013504 | tf_op jit(solution)/shard_map/all_gather | solution.py:277
  17.8 151.2 %copy-start.2 = (s32[512,1]{0,1:T(1,128)}, s32[512,1]{0,1:T(1,128)S(1)}, u32[]{:S(2)}) copy-start(s32[512,1]{0,1:T(1,128)S(1)} %get-tuple-element.406) | copy-start | bytes 6148
  17.8 151.2 %copy-start.4 = (s32[512,1]{0,1:T(1,128)}, s32[512,1]{0,1:T(1,128)S(1)}, u32[]{:S(2)}) copy-start(s32[512,1]{0,1:T(1,128)S(1)} %get-tuple-element.449) | copy-start | bytes 6148
  89.1 79.8 %all-to-all-start.2 = ((s32[16,1,64]{2,1,0:T(1,128)}), s32[16,1,64]{2,1,0:T(1,128)S(1)}, u32[]{:S(2)}, u32[]{:S(2)}) async-start(s32[16,1,64]{2,1,0:T(1,128)} %bitcast.48), calls=%async_computation.2 | async-start | bytes 16384 | tf_op jit(solution)/shard_map/all_to_all | solution.py:298
  96.8 304.6 %all-gather.23.cloned.1.call-start = ((), (), s32[]{:S(2)}) async-start(), calls=%async_computation.18 | async-start | bytes 5013504 | tf_op jit(solution)/shard_map/all_gather | solution.py:278
  168.9 14.1 all-to-all-start
  193.8 68.6 %all-to-all-start.3 = ((bf16[16,64,768]{2,1,0:T(8,128)(2,1)}), bf16[16,64,768]{2,1,0:T(8,128)(2,1)S(1)}, u32[]{:S(2)}, u32[]{:S(2)}) async-start(bf16[16,64,768]{2,1,0:T(8,128)(2,1)} %select_select_fusion), calls=%async_computation.3 | async-start | bytes 3145728 | tf_op jit(solution)/shard_map/all_to_all | solution.py:302
  200.1 116.8 %copy-start.164 = (s32[16]{0:T(128)}, s32[16]{0:T(128)S(1)}, u32[]{:S(2)}) copy-start(s32[16]{0:T(128)S(1)} %get-tuple-element.459) | copy-start | bytes 196
  200.1 116.8 %copy-start.165 = (s32[16]{0:T(128)}, s32[16]{0:T(128)S(1)}, u32[]{:S(2)}) copy-start(s32[16]{0:T(128)S(1)} %get-tuple-element.460) | copy-start | bytes 196
  262.4 70.8 %all-to-all-start.1 = ((bf16[16,64,768]{2,1,0:T(8,128)(2,1)}), bf16[16,64,768]{2,1,0:T(8,128)(2,1)}, u32[]{:S(2)}, u32[]{:S(2)}) async-start(bf16[16,64,768]{2,1,0:T(8,128)(2,1)} %select_select_fusion.1), calls=%async_computation.1 | async-start | bytes 3145728 | tf_op jit(solution)/shard_map/all_to_all | solution.py:302
  277.9 483.6 %reduce-scatter.13.cloned.1.call-start = ((), (), s32[]{:S(2)}) async-start(), calls=%async_computation.20 | async-start | bytes 835584 | tf_op jit(solution)/shard_map/reduce_scatter | solution.py:329
  278.6 122.8 %copy-start.136 = (f32[3072]{0:T(1024)}, f32[3072]{0:T(1024)S(1)}, u32[]{:S(2)}) copy-start(f32[3072]{0:T(1024)S(1)} %add.782) | copy-start | bytes 36868
  553.6 140.2 %collective-permute-start.2 = (f32[256,3144]{0,1:T(8,128)}, f32[256,3144]{0,1:T(8,128)}, u32[]{:S(2)}, u32[]{:S(2)}) collective-permute-start(f32[256,3144]{0,1:T(8,128)} %get-tuple-element.474), channel_id=1, source_target_pairs={{0,16},{1,17},{2,18},{3,19},{4,20},{5,21},{6,22},{7,23},{8,24},{9,... | collective-permute-start | bytes 9658376 | tf_op jit(solution)/shard_map/ppermute | solution.py:34
  556.6 148.7 %collective-permute-start = (f32[256,3144]{0,1:T(8,128)S(1)}, f32[256,3144]{0,1:T(8,128)}, u32[]{:S(2)}, u32[]{:S(2)}) collective-permute-start(f32[256,3144]{0,1:T(8,128)S(1)} %get-tuple-element.472), channel_id=1, source_target_pairs={{0,16},{1,17},{2,18},{3,19},{4,20},{5,21},{6,22},{7,23},{8,24},{9,... | collective-permute-start | bytes 9658376 | tf_op jit(solution)/shard_map/ppermute | solution.py:34
  582.3 111.5 %collective-permute-start.3 = (f32[256]{0:T(256)S(1)}, f32[256]{0:T(256)S(1)}, u32[]{:S(2)}, u32[]{:S(2)}) collective-permute-start(f32[256]{0:T(256)S(1)} %log_add_fusion.2), channel_id=1, source_target_pairs={{0,16},{1,17},{2,18},{3,19},{4,20},{5,21},{6,22},{7,23},{8,24},{9,... | collective-permute-start | bytes 3080 | tf_op jit(solution)/shard_map/ppermute | solution.py:34
  583.6 121.7 %collective-permute-start.1 = (f32[256]{0:T(256)S(1)}, f32[256]{0:T(256)S(1)}, u32[]{:S(2)}, u32[]{:S(2)}) collective-permute-start(f32[256]{0:T(256)S(1)} %log_add_fusion.3), channel_id=1, source_target_pairs={{0,16},{1,17},{2,18},{3,19},{4,20},{5,21},{6,22},{7,23},{8,24},{9,... | collective-permute-start | bytes 3080 | tf_op jit(solution)/shard_map/ppermute | solution.py:34
  705.3 115.7 %reduce-scatter.11.cloned.1.call-start = ((), (), s32[]{:S(2)}) async-start(), calls=%async_computation.19 | async-start | bytes 835584 | tf_op jit(solution)/shard_map/reduce_scatter | solution.py:329
  710.9 110.1 %copy-start.66 = (f32[16,768]{1,0:T(8,128)S(1)}, f32[16,768]{1,0:T(8,128)}, u32[]{:S(2)}) copy-start(f32[16,768]{1,0:T(8,128)} %copy-done.65) | copy-start | bytes 147460
  711.0 111.6 %copy-start.171 = (f32[16]{0:T(128)S(1)}, f32[16]{0:T(128)}, u32[]{:S(2)}) copy-start(f32[16]{0:T(128)} %copy-done.170) | copy-start | bytes 196
  711.0 111.6 %copy-start.169 = (f32[16]{0:T(128)S(1)}, f32[16]{0:T(128)}, u32[]{:S(2)}) copy-start(f32[16]{0:T(128)} %copy-done.168) | copy-start | bytes 196
  715.9 505.1 %reduce-scatter.17.cloned.1.call-start = ((), (), s32[]{:S(2)}) async-start(), calls=%async_computation.22 | async-start | bytes 2506752 | tf_op jit(solution)/shard_map/reduce_scatter | solution.py:357
  932.6 288.4 %reduce-scatter.23.cloned.1.call-start = ((), (), s32[]{:S(2)}) async-start(), calls=%async_computation.25 | async-start | bytes 3342336 | tf_op jit(solution)/shard_map/reduce_scatter | solution.py:360
  971.9 249.1 %reduce-scatter.15.cloned.1.call-start = ((), (), s32[]{:S(2)}) async-start(), calls=%async_computation.21 | async-start | bytes 7520256 | tf_op jit(solution)/shard_map/reduce_scatter | solution.py:356
  983.0 324.2 %reduce-scatter.21.cloned.1.call-start = ((), (), s32[]{:S(2)}) async-start(), calls=%async_computation.24 | async-start | bytes 10027008 | tf_op jit(solution)/shard_map/reduce_scatter | solution.py:359
  1000.9 422.5 %reduce-scatter.19.cloned.1.call-start = ((), (), s32[]{:S(2)}) async-start(), calls=%async_computation.23 | async-start | bytes 10027008 | tf_op jit(solution)/shard_map/reduce_scatter | solution.py:358
  1083.5 73.8 %all-to-all-start.4 = ((bf16[16,64,768]{2,1,0:T(8,128)(2,1)}), bf16[16,64,768]{2,1,0:T(8,128)(2,1)S(1)}, u32[]{:S(2)}, u32[]{:S(2)}) async-start(bf16[16,64,768]{2,1,0:T(8,128)(2,1)} %scatter_fusion.2), calls=%async_computation.5 | async-start | bytes 3145728 | tf_op jit(solution)/shard_map/all_to_all | solution.py:351
  1157.3 47.2 %all-to-all-start.5 = ((bf16[16,64,768]{2,1,0:T(8,128)(2,1)}), bf16[16,64,768]{2,1,0:T(8,128)(2,1)}, u32[]{:S(2)}, u32[]{:S(2)}) async-start(bf16[16,64,768]{2,1,0:T(8,128)(2,1)} %scatter_fusion.3), calls=%async_computation.7 | async-start | bytes 3145728 | tf_op jit(solution)/shard_map/all_to_all | solution.py:351
  1163.6 319.2 %reduce-scatter.25.cloned.1.call-start = ((), (), s32[]{:S(2)}) async-start(), calls=%async_computation.26 | async-start | bytes 417792
  1172.2 583.7 %all-reduce.7.cloned.1.call-start = ((), (), s32[]{:S(2)}) async-start(), calls=%async_computation.27 | async-start | bytes 23248896 | tf_op jit(solution)/shard_map/psum | solution.py:368
  (183 other events, 2829.9 us)
Sparse Core Ops, SparseCore 0:
  10.9 42.3 all-gather.14
  56.2 45.8 all-gather.16
  104.9 37.4 all-gather.18
  145.1 52.3 all-gather.20
  200.3 69.9 all-gather.22
  705.4 56.0 reduce-scatter.12
  765.4 55.5 reduce-scatter.10
  932.8 62.0 reduce-scatter.16
  999.1 65.2 reduce-scatter.22
  1068.8 121.2 reduce-scatter.14
  1194.7 112.3 reduce-scatter.20
  1312.2 111.1 reduce-scatter.18
  1427.4 55.3 reduce-scatter.24
  1486.4 269.3 all-reduce.6
where the time goes:
time: 1880 us; the launch traced here: 1860 us
  waiting for transfers between devices  748 us (40%)
  local copies, waits for them, and re-layouts  384 us (20%)
  blocking collectives  242 us (13%)
  matrix products  219 us (12%)
  other arithmetic  186 us (10%)
  starting transfers between devices  55.3 us (3%)
  between operations  27.1 us (1%)
    psum x1, waiting for transfers between devices, shards(): lax.psum((reduced[0], reduced[1], reduced[2], reduced[3], reduced[4], red...  267 us
    scatter x2, local copies, waits for them, and re-layouts, shards(): request = jnp.full((devices, capacity), vocab_rows, jnp.int32).at[owners,...  141 us
    scatter x2, local copies, waits for them, and re-layouts, shards(): sent_rows = jnp.zeros((devices, capacity, model_width), jnp.bfloat16).at[...  137 us
    reduce_scatter x1, waiting for transfers between devices, shards(): lax.psum_scatter(grads[2], 'dp', scatter_dimension=0, tiled=True)  116 us
    ppermute x4, waiting for transfers between devices, from_behind(): return lax.ppermute(block, axis, route)  109 us
    reduce_scatter x2, waiting for transfers between devices, shards(): lax.psum_scatter(row_terms(d_low, table_low), 'dp', scatter_dimension=0,...  104 us
    reduce_scatter x1, waiting for transfers between devices, shards(): lax.psum_scatter(grads[3], 'dp', scatter_dimension=0, tiled=True)  86.1 us
    all_gather x4, blocking collectives, joined(): everything = jax.tree.map(lambda part: lax.all_gather(part, axis), value)  72.4 us
  transfers between devices with their start and end apart: 24, of which 8 were waited for; matrix products, arithmetic and copies ran while one was open for 31% of the time, Pallas kernels for 0%

commit v1 on v0

v1 whole, which is shorter than its diff:
```python
import jax
import jax.numpy as jnp
from jax import lax
from jax.sharding import PartitionSpec as P

H = 12
MB = 2
STEP = 10
LONGEST = 256
LANES = 128


learn_rate = 0.25
beta_one = 0.9
beta_two = 0.999
adam_eps = 1e-08
decay_rate = 0.1
clip_limit = 0.02
norm_eps = 1e-05
neg_big = -1000000000.0

low = jnp.bfloat16
wide = jnp.float32


def layer_norm(values, norm_gain, norm_shift):
    center = jnp.mean(values, axis=-1, keepdims=True)
    offsets = values - center
    spread = jnp.mean(offsets * offsets, axis=-1, keepdims=True)
    return offsets * lax.rsqrt(spread + norm_eps) * norm_gain + norm_shift


def gelu_tanh(values):
    return jax.nn.gelu(values, approximate=True)


def dot_plain(left_side, right_side):
    return jnp.dot(left_side, right_side, preferred_element_type=wide)


def dot_first(left_side, right_side):
    return lax.dot_general(
        left_side, right_side, (((0,), (0,)), ((), ())), preferred_element_type=wide
    )


def dot_last(left_side, right_side):
    return lax.dot_general(
        left_side, right_side, (((1,), (1,)), ((), ())), preferred_element_type=wide
    )


def exact_rows(one_hot, values):
    return lax.dot_general(
        one_hot.astype(wide),
        values,
        (((1,), (0,)), ((), ())),
        precision=lax.Precision.HIGHEST,
        preferred_element_type=wide,
    )


def chip_ring(chips):
    if chips % 8:
        return list(range(chips))
    if chips == 8:
        return [0, 2, 4, 6, 7, 5, 3, 1]
    lines = chips // 4
    order = list(range(lines))
    for k in range(0, lines - 3, 4):
        order[k + 2], order[k + 3] = order[k + 3], order[k + 2]
    ring = [order[0] * 4]
    for k, line in enumerate(order):
        columns = (1, 2, 3) if k % 2 == 0 else (3, 2, 1)
        ring = ring + [line * 4 + column for column in columns]
    return ring + [line * 4 for line in reversed(order[1:])]


def ring_gather(block):
    devices = lax.axis_size("dp")
    if devices % 4:
        return lax.all_gather(block, "dp", axis=0)
    chips = devices // 2
    ring = chip_ring(chips)
    place_of = [ring.index(chip) for chip in range(chips)]
    me = lax.axis_index("dp")
    core = me % 2
    place = jnp.asarray(place_of, jnp.int32)[me // 2]
    onward = [(2 * ring[k] + c, 2 * ring[(k + 1) % chips] + c) for k in range(chips) for c in (0, 1)]
    backward = [(there, here) for here, there in onward]
    across = [(d, d ^ 1) for d in range(devices)]
    half_rows = block.shape[0] // 2
    whole = jnp.zeros((devices,) + block.shape, block.dtype)

    def keep(whole, piece, distance):
        chip = jnp.asarray(ring, jnp.int32)[(place + distance) % chips]
        partner = lax.ppermute(piece, "dp", across)
        whole = lax.dynamic_update_slice(whole, piece[None], (2 * chip + core, 0, 0))
        return lax.dynamic_update_slice(whole, partner[None], (2 * chip + 1 - core, 0, 0))

    ahead, behind = block, block
    whole = keep(whole, block, 0)
    for distance in range(1, chips // 2):
        ahead = lax.ppermute(ahead, "dp", onward)
        behind = lax.ppermute(behind, "dp", backward)
        whole = keep(whole, ahead, -distance)
        whole = keep(whole, behind, distance)
    first = lax.ppermute(ahead[:half_rows], "dp", onward)
    second = lax.ppermute(behind[half_rows:], "dp", backward)
    return keep(whole, jnp.concatenate([first, second], axis=0), chips // 2)


def pack(attn_in, attn_out, mlp_in, mlp_out, pos, vecs):
    rows = attn_in.shape[0]
    width = attn_out.shape[1]
    folds = mlp_out.shape[0] // rows
    folded = mlp_out.reshape(folds, rows, width).transpose(1, 0, 2).reshape(rows, folds * width)
    turned = jnp.pad(vecs.T, ((0, 0), (0, LANES - vecs.shape[0])))
    return jnp.concatenate([attn_in, attn_out, mlp_in, folded, pos.reshape(rows, -1), turned], axis=1)


def unpack(whole, width, hidden, vec_count):
    devices, rows = whole.shape[:2]
    folds = hidden // width
    flat = whole.reshape(devices * rows, -1)
    cuts = [3 * width, width, hidden, hidden]
    starts = [0, 3 * width, 4 * width, 4 * width + hidden]
    attn_in, attn_out, mlp_in, folded = [
        flat[:, start : start + cut] for start, cut in zip(starts, cuts)
    ]
    mlp_out = folded.reshape(devices, rows, folds, width).transpose(0, 2, 1, 3).reshape(hidden, width)
    pos_start = 4 * width + 2 * hidden
    pos_width = flat.shape[1] - pos_start - LANES
    pos_rows = LONGEST * width // pos_width
    pos = flat[:pos_rows, pos_start : pos_start + pos_width].reshape(LONGEST, width)
    vecs = flat[:, flat.shape[1] - LANES :][:, :vec_count].T
    return attn_in, attn_out, mlp_in, mlp_out, pos, vecs


def head_marks(width):
    size = width // H
    columns = jnp.arange(width, dtype=jnp.int32) // size
    return columns[None, None, :] == jnp.arange(H, dtype=jnp.int32)[:, None, None]


def by_head(rows, marks):
    spread = jnp.where(marks, rows[None], jnp.zeros((), rows.dtype))
    return spread.reshape(-1, rows.shape[1])


def from_heads(spread, marks):
    parts = spread.reshape(H, -1, spread.shape[1])
    return jnp.sum(jnp.where(marks, parts, 0.0), axis=0)


def attend(queries, keys_all, values, allowed, marks):
    scaling = (queries.shape[1] // H) ** (-0.5)
    scores = dot_last(by_head(queries, marks), keys_all) * scaling
    scores = jnp.where(allowed, scores, neg_big)
    row_max = jnp.max(scores, axis=-1, keepdims=True)
    weights_exp = jnp.exp(scores - row_max)
    probs = weights_exp / jnp.sum(weights_exp, axis=-1, keepdims=True)
    attended = from_heads(dot_plain(probs.astype(low), values), marks).astype(low)
    return attended, probs


def attend_back(d_attended, queries, keys_all, values, probs, marks):
    scaling = (queries.shape[1] // H) ** (-0.5)
    d_spread = by_head(d_attended, marks)
    d_probs = dot_last(d_spread, values)
    row_inner = jnp.sum(probs * d_probs, axis=-1, keepdims=True)
    d_scores = (probs * (d_probs - row_inner)).astype(low)
    query_grads = from_heads(dot_plain(d_scores, keys_all), marks) * scaling
    key_grads = dot_first(d_scores, by_head(queries, marks)) * scaling
    value_grads = dot_first(probs.astype(low), d_spread)
    return query_grads.astype(low), key_grads.astype(low), value_grads.astype(low)


def adam_update(master, moment_one, moment_two, gradient, factor):
    clipped = gradient * factor
    new_one = beta_one * moment_one + (1.0 - beta_one) * clipped
    new_two = beta_two * moment_two + (1.0 - beta_two) * clipped * clipped
    fixed_one = new_one / (1.0 - beta_one**STEP)
    fixed_two = new_two / (1.0 - beta_two**STEP)
    updated = master - learn_rate * (
        fixed_one / (jnp.sqrt(fixed_two) + adam_eps) + decay_rate * master
    )
    return (updated, new_one, new_two)


def to_all(value, axis):
    copies = lax.axis_size(axis)
    spread = jnp.broadcast_to(value[None], (copies,) + value.shape)
    return lax.all_to_all(spread, axis, split_axis=0, concat_axis=0, tiled=True)


def shards(
    token_shard,
    token_row,
    doc_ids,
    loss_rows,
    teacher_table,
    teacher_pos,
    teacher_attn_in,
    teacher_attn_out,
    teacher_mlp_in,
    teacher_mlp_out,
    teacher_vecs,
    table,
    pos_table,
    attn_in,
    attn_out,
    mlp_in,
    mlp_out,
    vectors,
    table_m,
    pos_m,
    attn_in_m,
    attn_out_m,
    mlp_in_m,
    mlp_out_m,
    vectors_m,
    table_v,
    pos_v,
    attn_in_v,
    attn_out_v,
    mlp_in_v,
    mlp_out_v,
    vectors_v,
):
    part = lax.axis_index("pair")
    is_student = part == 1
    me = lax.axis_index("dp")
    devices = lax.axis_size("dp")
    vocab_rows, width = table.shape
    hidden = mlp_in.shape[1]
    rows = attn_in.shape[0]
    vec_count = vectors.shape[0]
    pos_count = pos_table.shape[0]
    swap = [(0, 1), (1, 0)]
    to_teacher = [(1, 0)]
    to_student = [(0, 1)]

    own_block = jnp.where(
        is_student,
        pack(*[w.astype(low) for w in (attn_in, attn_out, mlp_in, mlp_out, pos_table, vectors)]),
        pack(
            teacher_attn_in,
            teacher_attn_out,
            teacher_mlp_in,
            teacher_mlp_out,
            teacher_pos,
            teacher_vecs,
        ),
    )
    whole = ring_gather(own_block)
    w_attn_in, w_attn_out, w_mlp_in, w_mlp_out, w_pos, w_vecs = unpack(
        whole, width, hidden, vec_count
    )
    vec = w_vecs.astype(wide)

    owners = token_shard[:, 0, :, 0]
    shard_rows = token_row[:, 0]
    docs = doc_ids[:, 0]
    chosen = loss_rows[:, 0]
    length = owners.shape[1]
    picks = chosen.shape[1]
    capacity = 2 * length // devices
    total_rows = MB * devices * picks
    indices = jnp.arange(length, dtype=jnp.int32)
    before = indices[None, :] < indices[:, None]
    same_owner = owners[:, :, None] == owners[:, None, :]
    slot = owners * capacity + jnp.sum(same_owner & before, axis=-1, dtype=jnp.int32)
    positions = indices - jnp.sum(docs[:, None, :] < docs[:, :, None], axis=-1, dtype=jnp.int32)
    slots = jnp.arange(devices * capacity, dtype=jnp.int32)
    filled = slots[None, :, None] == slot[:, None, :]
    request = vocab_rows + jnp.sum(
        jnp.where(filled, shard_rows[:, None, :] - vocab_rows, 0), axis=-1
    )
    request = request.reshape(MB, devices, capacity).transpose(1, 0, 2).reshape(devices, -1)
    is_next = indices[None, None, :] == (chosen + 1)[:, :, None]
    next_ids = jnp.sum(
        jnp.where(is_next, (owners * vocab_rows + shard_rows)[:, None, :], 0), axis=-1
    )
    notes = jnp.broadcast_to(next_ids.reshape(1, -1), (devices, MB * picks))
    arrived_notes = lax.all_to_all(
        jnp.concatenate([request, notes], axis=1), "dp", split_axis=0, concat_axis=0, tiled=True
    )
    asked = arrived_notes[:, : MB * capacity].reshape(devices, MB, capacity).transpose(1, 0, 2)
    asked = asked.reshape(MB, devices * capacity)
    targets = arrived_notes[:, MB * capacity :].reshape(devices, MB, picks).transpose(1, 0, 2)
    targets = targets.reshape(MB, devices * picks)[part]

    safe = jnp.minimum(asked, vocab_rows - 1)
    found = lax.cond(
        is_student,
        lambda at: jnp.take(table, at, axis=0).astype(low),
        lambda at: jnp.take(teacher_table, at, axis=0),
        safe,
    )
    marks = head_marks(width)
    kept = []
    for m in range(MB):
        back = lax.all_to_all(
            found[m].reshape(devices, capacity, width),
            "dp",
            split_axis=0,
            concat_axis=0,
            tiled=True,
        ).reshape(devices * capacity, width)
        sources = jnp.concatenate([back, w_pos], axis=0)
        spots = jnp.arange(LONGEST, dtype=jnp.int32)
        pick_row = jnp.concatenate(
            [slot[m][:, None] == slots[None, :], positions[m][:, None] == spots[None, :]], axis=1
        ).astype(low)
        is_chosen = chosen[m][:, None] == indices[None, :]
        slot_c = jnp.sum(jnp.where(is_chosen, slot[m][None], 0), axis=1)
        position_c = jnp.sum(jnp.where(is_chosen, positions[m][None], 0), axis=1)
        doc_c = jnp.sum(jnp.where(is_chosen, docs[m][None], 0), axis=1)
        pick_c = jnp.concatenate(
            [slot_c[:, None] == slots[None, :], position_c[:, None] == spots[None, :]], axis=1
        ).astype(low)
        x_embed = dot_plain(pick_row, sources)
        x_embed_c = dot_plain(pick_c, sources)
        normed_one = layer_norm(x_embed, vec[0], vec[1]).astype(low)
        normed_one_c = layer_norm(x_embed_c, vec[0], vec[1]).astype(low)
        kv_bias = jnp.concatenate([jnp.zeros((width,), wide), vec[7]])
        kv_low = (dot_plain(normed_one, w_attn_in[:, width:]) + kv_bias).astype(low)
        queries = (dot_plain(normed_one_c, w_attn_in[:, :width]) + vec[6]).astype(low)
        allowed = (doc_c[:, None] == docs[m][None, :]) & (indices[None, :] <= chosen[m][:, None])
        allowed = jnp.broadcast_to(allowed[None], (H,) + allowed.shape).reshape(-1, length)
        attended, probs = attend(queries, kv_low[:, :width], kv_low[:, width:], allowed, marks)
        kept.append(
            (x_embed, x_embed_c, normed_one, kv_low, queries, attended, probs, pick_row, is_chosen)
        )

    x_embed_c = jnp.concatenate([k[1] for k in kept], axis=0)
    attended = jnp.concatenate([k[5] for k in kept], axis=0)
    x_mid = x_embed_c + dot_plain(attended, w_attn_out) + vec[8]
    normed_two = layer_norm(x_mid, vec[2], vec[3]).astype(low)
    pre_act = dot_plain(normed_two, w_mlp_in) + vec[10:].reshape(-1)
    activated = gelu_tanh(pre_act).astype(low)
    x_top = x_mid + dot_plain(activated, w_mlp_out) + vec[9]
    final = layer_norm(x_top, vec[4], vec[5]).astype(low).reshape(MB, picks, width)

    other_final = lax.ppermute(final[1 - part], "pair", swap)
    own_final = final[part]
    both = jnp.stack(
        [
            jnp.where(is_student, other_final, own_final),
            jnp.where(is_student, own_final, other_final),
        ]
    )
    every = lax.all_gather(both.reshape(2 * picks, width), "dp", axis=0)
    every = every.reshape(devices, 2, picks, width).transpose(1, 0, 2, 3)
    every = every.reshape(2, devices * picks, width)
    teacher_rows, student_rows = every[0], every[1]
    table_low = table.astype(low)
    teacher_logits = dot_last(teacher_rows, teacher_table)
    logits = dot_last(student_rows, table_low)
    teacher_max = jnp.max(teacher_logits, axis=1)
    teacher_sum = jnp.sum(jnp.exp(teacher_logits - teacher_max[:, None]), axis=1)
    own_max = jnp.max(logits, axis=1)
    own_sum = jnp.sum(jnp.exp(logits - own_max[:, None]), axis=1)
    stats = to_all(jnp.stack([teacher_max, teacher_sum, own_max, own_sum]), "dp")

    def log_total(maxima, sums):
        big = jnp.max(maxima, axis=0)
        return big + jnp.log(jnp.sum(sums * jnp.exp(maxima - big[None]), axis=0))

    teacher_total = log_total(stats[:, 0], stats[:, 1])[:, None]
    own_total = log_total(stats[:, 2], stats[:, 3])[:, None]
    teacher_log = teacher_logits - teacher_total
    teacher_prob = jnp.exp(teacher_log)
    own_log = logits - own_total
    own_prob = jnp.exp(own_log)
    kl_local = jnp.sum(teacher_prob * (teacher_log - own_log))
    vocab_iota = jnp.arange(vocab_rows, dtype=jnp.int32)
    target_hit = (targets - me * vocab_rows)[:, None] == vocab_iota[None, :]
    d_logits = (2.0 * own_prob - target_hit.astype(wide) - teacher_prob) * (1.0 / total_rows)
    d_low = d_logits.astype(low)
    d_final_parts = dot_plain(d_low, table_low).astype(low).reshape(devices, picks, width)
    d_final_parts = lax.all_to_all(d_final_parts, "dp", split_axis=0, concat_axis=0, tiled=True)
    d_final = jnp.sum(d_final_parts.astype(wide), axis=0)
    d_final_first = lax.ppermute(d_final, "pair", to_student)
    d_final = jnp.concatenate([d_final_first, d_final], axis=0)
    d_low_other = lax.ppermute(d_low, "pair", swap)
    student_rows_other = lax.ppermute(student_rows, "pair", swap)

    final_back = jax.vjp(layer_norm, x_top, vec[4], vec[5])[1]
    d_top, d_gain_final, d_shift_final = final_back(d_final)
    d_branch = d_top.astype(low)
    d_act = dot_last(d_branch, w_mlp_out)
    d_pre = jax.vjp(gelu_tanh, pre_act)[1](d_act)[0].astype(low)
    d_normed_two = dot_last(d_pre, w_mlp_in)
    d_mid, d_gain_two, d_shift_two = jax.vjp(layer_norm, x_mid, vec[2], vec[3])[1](d_normed_two)
    d_mid = d_top + d_mid
    d_attn_branch = d_mid.astype(low)
    d_attended = dot_last(d_attn_branch, w_attn_out).astype(low)

    def column_blocks(values):
        return values.reshape(values.shape[0], devices, -1).transpose(1, 0, 2)

    lefts = jnp.concatenate(
        [column_blocks(activated), column_blocks(normed_two), column_blocks(attended)], axis=2
    )
    rights = jnp.concatenate([d_branch, d_pre, d_attn_branch], axis=1)
    lefts = lax.ppermute(lefts, "pair", to_teacher) + jnp.where(is_student, lefts, 0)
    rights = lax.ppermute(rights, "pair", to_teacher) + jnp.where(is_student, rights, 0)
    lefts = lax.all_to_all(lefts, "dp", split_axis=0, concat_axis=0, tiled=True)
    lefts = lefts.reshape(-1, lefts.shape[2])
    rights = lax.all_gather(rights, "dp", axis=0, tiled=True)
    fold_rows = mlp_out.shape[0]
    g_mlp_out = dot_first(lefts[:, :fold_rows], rights[:, :width])
    g_mlp_in = dot_first(lefts[:, fold_rows : fold_rows + rows], rights[:, width : width + hidden])
    g_attn_out = dot_first(lefts[:, fold_rows + rows :], rights[:, width + hidden :])

    g_attn_in = jnp.zeros((width, 3 * width), wide)
    g_pos = jnp.zeros((LONGEST, width), wide)
    d_gain_one = jnp.zeros((width,), wide)
    d_shift_one = jnp.zeros((width,), wide)
    qkv_sums = jnp.zeros((3 * width,), wide)
    sent = []
    for m in range(MB):
        x_embed, _, normed_one, kv_low, queries, _, probs, pick_row, is_chosen = kept[m]
        d_query_c, d_keys, d_values = attend_back(
            d_attended[m * picks : (m + 1) * picks],
            queries,
            kv_low[:, :width],
            kv_low[:, width:],
            probs,
            marks,
        )
        to_chosen = is_chosen.T
        d_queries = dot_plain(to_chosen.astype(low), d_query_c).astype(low)
        d_qkv = jnp.concatenate([d_queries, d_keys, d_values], axis=1)
        g_attn_in = g_attn_in + dot_first(normed_one, d_qkv)
        qkv_sums = qkv_sums + jnp.sum(d_qkv, axis=0, dtype=wide)
        d_normed_one = dot_last(d_qkv, w_attn_in)
        norm_one_back = jax.vjp(layer_norm, x_embed, vec[0], vec[1])[1]
        d_embed, d_gain, d_shift = norm_one_back(d_normed_one)
        d_gain_one = d_gain_one + d_gain
        d_shift_one = d_shift_one + d_shift
        d_embed = d_embed + exact_rows(to_chosen, d_mid[m * picks : (m + 1) * picks])
        d_embed = d_embed.astype(low)
        slot_count = devices * capacity
        g_pos = g_pos + dot_first(pick_row[:, slot_count:], d_embed)
        here = lax.ppermute(d_embed, "pair", to_teacher) + jnp.where(is_student, d_embed, 0)
        out_rows = dot_first(pick_row[:, :slot_count], here).astype(low)
        sent.append(
            lax.all_to_all(
                out_rows.reshape(devices, capacity, width),
                "dp",
                split_axis=0,
                concat_axis=0,
                tiled=True,
            ).reshape(slot_count, width)
        )

    vector_part = jnp.stack(
        [
            d_gain_one,
            d_shift_one,
            d_gain_two,
            d_shift_two,
            d_gain_final,
            d_shift_final,
            qkv_sums[:width],
            qkv_sums[2 * width :],
            jnp.sum(d_attn_branch, axis=0, dtype=wide),
            jnp.sum(d_branch, axis=0, dtype=wide),
        ]
    )
    bias_part = jnp.sum(d_pre, axis=0, dtype=wide).reshape(-1, width)
    g_vecs = jnp.concatenate([vector_part, bias_part], axis=0)
    g_vecs = jnp.pad(g_vecs.T, ((0, 0), (0, LANES - vec_count)))
    pos_share = LONGEST // devices
    shared = jnp.concatenate([g_attn_in, g_vecs, g_pos.reshape(width, -1)], axis=1).astype(low)
    shared = lax.psum_scatter(shared, "dp", scatter_dimension=0, tiled=True)
    shared = lax.ppermute(shared, "pair", to_teacher) + jnp.where(is_student, shared, 0)
    shared = shared.astype(wide)
    g_attn_in = shared[:, : 3 * width]
    g_vecs = shared[:, 3 * width : 3 * width + vec_count].T
    pos_near = shared[:, 3 * width + LANES :].reshape(pos_share, width).astype(low)
    pos_near = lax.all_gather(pos_near, "dp", axis=0, tiled=True).astype(wide)
    pos_all = jnp.concatenate([pos_near, jnp.zeros((pos_count, width), wide)], axis=0)
    g_pos = lax.dynamic_slice(
        pos_all, (jnp.minimum(me * pos_count, LONGEST), 0), (pos_count, width)
    )

    d_low_all = jnp.concatenate(
        [jnp.where(is_student, d_low_other, d_low), jnp.where(is_student, d_low, d_low_other)],
        axis=0,
    )
    rows_all = jnp.concatenate(
        [
            jnp.where(is_student, student_rows_other, student_rows),
            jnp.where(is_student, student_rows, student_rows_other),
        ],
        axis=0,
    )
    arrived = jnp.concatenate(sent, axis=0)
    wanted = (asked.reshape(-1)[:, None] == vocab_iota[None, :]).astype(low)
    g_table = dot_first(d_low_all, rows_all) + dot_first(wanted, arrived)

    summed = (g_attn_in, g_attn_out, g_mlp_in, g_mlp_out, g_pos, g_vecs, g_table)
    squares = jnp.zeros((), wide)
    for gradient in summed:
        squares = squares + jnp.sum(gradient * gradient)
    lane = jnp.arange(LANES, dtype=jnp.int32)[None, :]
    totals = to_all(
        jnp.where(lane == 0, squares, jnp.where(lane == 1, kl_local, 0.0)), ("pair", "dp")
    )
    grad_norm = jnp.sqrt(jnp.sum(totals[devices:, 0, 0]))
    kl_mean = jnp.sum(totals[:, 0, 1]) / total_rows
    factor = jnp.minimum(1.0, clip_limit / (grad_norm + 1e-06))
    table_out = adam_update(table, table_m, table_v, summed[6], factor)
    pos_out = adam_update(pos_table, pos_m, pos_v, summed[4], factor)
    attn_in_out = adam_update(attn_in, attn_in_m, attn_in_v, summed[0], factor)
    attn_out_out = adam_update(attn_out, attn_out_m, attn_out_v, summed[1], factor)
    mlp_in_out = adam_update(mlp_in, mlp_in_m, mlp_in_v, summed[2], factor)
    mlp_out_out = adam_update(mlp_out, mlp_out_m, mlp_out_v, summed[3], factor)
    vectors_out = adam_update(vectors, vectors_m, vectors_v, summed[5], factor)
    return (
        *table_out,
        *pos_out,
        *attn_in_out,
        *attn_out_out,
        *mlp_in_out,
        *mlp_out_out,
        *vectors_out,
        grad_norm,
        kl_mean,
    )


def solution(mesh):
    return jax.shard_map(
        shards,
        mesh=mesh,
        in_specs=(
            P(None, "dp", None, None),
            P(None, "dp", None),
            P(None, "dp", None),
            P(None, "dp", None),
            P("dp", None),
            P("dp", None),
            P("dp", None),
            P("dp", None),
            P("dp", None),
            P("dp", None),
            P(None, "dp"),
            P("dp", None),
            P("dp", None),
            P("dp", None),
            P("dp", None),
            P("dp", None),
            P("dp", None),
            P(None, "dp"),
            P("dp", None),
            P("dp", None),
            P("dp", None),
            P("dp", None),
            P("dp", None),
            P("dp", None),
            P(None, "dp"),
            P("dp", None),
            P("dp", None),
            P("dp", None),
            P("dp", None),
            P("dp", None),
            P("dp", None),
            P(None, "dp"),
        ),
        out_specs=(
            P("dp", None),
            P("dp", None),
            P("dp", None),
            P("dp", None),
            P("dp", None),
            P("dp", None),
            P("dp", None),
            P("dp", None),
            P("dp", None),
            P("dp", None),
            P("dp", None),
            P("dp", None),
            P("dp", None),
            P("dp", None),
            P("dp", None),
            P("dp", None),
            P("dp", None),
            P("dp", None),
            P(None, "dp"),
            P(None, "dp"),
            P(None, "dp"),
            P(),
            P(),
        ),
        check_vma=False,
    )
```

time: 1880 us -> 736 us (0.39)
  waiting for transfers between devices: 748 us -> 198 us
  local copies, waits for them, and re-layouts: 384 us -> 120 us
  blocking collectives: 242 us -> 64.6 us
  other arithmetic: 186 us -> 91.6 us
  matrix products: 219 us -> 128 us
  starting transfers between devices: 55.3 us -> 83.7 us
    reduce_scatter x7 -> x1, waiting for transfers between devices: 306 us -> 0.01 us  [shards(): shared = lax.psum_scatter(shared, 'dp', scatter_dimension=0, tiled=True)]
    scatter x4 -> x0, local copies, waits for them, and re-layouts: 279 us -> none  [the longest x2 141 us: shards(): request = jnp.full((devices, capacity), vocab_rows, jnp.int32).at[owners,...]
    psum x1 -> x0, waiting for transfers between devices: 267 us -> none  [shards(): lax.psum((reduced[0], reduced[1], reduced[2], reduced[3], reduced[4], red...]
    all_gather x7 -> x2, blocking collectives: 159 us -> 49.8 us  [the longest x1 26.9 us: shards(): every = lax.all_gather(both.reshape(2 * picks, width), 'dp', axis=0)]
    dot_general x22 -> x20, matrix products: 117 us -> 37.8 us  [the longest x18 33.8 us: dot_plain(): return jnp.dot(left_side, right_side, preferred_element_type=wide)]
    unnamed x15 -> x2, waiting for transfers between devices: 58.3 us -> 0.03 us
    scatter-add x6 -> x0, other arithmetic: 47.6 us -> none  [the longest x2 31.3 us: shards(): table_grad.at[asked_here.reshape(-1)]]
    psum x2 -> x0, blocking collectives: 45.1 us -> none  [the longest x1 40.1 us: shards(): step_totals = lax.psum((student_weight * squares, kl_local), ('pair', 'dp'))]
  transfers between devices with their start and end apart: 24 -> 35, of which waited for: 8 -> 15; matrix products, arithmetic and copies ran while one was open for 31% -> 19% of each run, Pallas kernels for 0% -> 0%
where the time goes in v1:
time: 736 us; the launch traced here: 724 us
  waiting for transfers between devices  198 us (27%)
  matrix products  128 us (17%)
  local copies, waits for them, and re-layouts  120 us (16%)
  other arithmetic  91.6 us (12%)
  starting transfers between devices  83.7 us (11%)
  blocking collectives  64.6 us (9%)
  between operations  37.1 us (5%)
    dot_general x15, matrix products, dot_first(): lax.dot_general(left_side, right_side, (((0,), (0,)), ((), ())), preferre...  62.3 us
    ppermute x3, waiting for transfers between devices, ring_gather(): ahead = lax.ppermute(ahead, 'dp', onward)  57.3 us
    ppermute x2, waiting for transfers between devices, shards(): lax.ppermute(d_embed, 'pair', to_teacher)  40 us
    ppermute x1, waiting for transfers between devices, shards(): lax.ppermute(lefts, 'pair', to_teacher) + jnp.where(is_student, lefts, 0)  38.9 us
    sub x7, other arithmetic, adam_update(): master - learn_rate * (fixed_one / (jnp.sqrt(fixed_two) + adam_eps) + dec...  34.9 us
    dot_general x18, matrix products, dot_plain(): return jnp.dot(left_side, right_side, preferred_element_type=wide)  33.8 us
    unnamed x336, local copies, waits for them, and re-layouts  29.9 us
    dot_general x11, matrix products, dot_last(): lax.dot_general(left_side, right_side, (((1,), (1,)), ((), ())), preferre...  28.4 us
  transfers between devices with their start and end apart: 35, of which 15 were waited for; matrix products, arithmetic and copies ran while one was open for 19% of the time, Pallas kernels for 0%

profile of v1, /device:TPU:0, one launch (start us, length us, event | category | flops | bytes accessed | tf_op | source)
XLA Modules:
  0.0 724.4 jit_solution(1183843522432422965)
XLA Ops:
  31.1 6.4 all-to-all-start
  63.3 5.7 broadcast_in_dim.428
  78.2 15.2 %conditional.1 = (bf16[2,1024,768]{2,1,0:T(8,128)(2,1)S(1)}) conditional(s32[]{:T(128)} %convert_element_type.209, (s32[2,1024]{1,0:T(2,128)S(1)}, bf16[3144,768]{1,0:T(8,128)(2,1)}) %tuple.14, (s32[2,1024]{1,0:T(2,128)S(1)}, f32[3144,768]{1,0:T(8,128)}) %tuple.15), branch_computations={%region_6.7_spmd, %region_7.8_spmd} | conditional | flops 1593344 | bytes 12636168 | solution.py:295
  78.2 13.1 %gather_fusion = bf16[2048,768]{1,0:T(8,128)(2,1)} fusion(bf16[3144,768]{1,0:T(8,128)(2,1)} %get-tuple-element.12, s32[2048]{0:T(1024)S(1)} %bitcast_clamp_fusion), kind=kCustom, calls=%fused_computation | custom fusion | bytes 6299648 | tf_op jit(solution)/shard_map/cond/branch_0_fun/jit(_take)/gather | solution.py:298
  95.3 5.9 all-to-all-start.1
  108.3 40.9 %collective-permute-done.5 = bf16[48,10368]{1,0:T(8,128)(2,1)S(1)} collective-permute-done((bf16[48,10368]{1,0:T(8,128)(2,1)}, bf16[48,10368]{1,0:T(8,128)(2,1)S(1)}, u32[]{:S(2)}, u32[]{:S(2)}) %collective-permute-start.5) | collective-permute-done | bytes 995360 | tf_op jit(solution)/shard_map/ppermute | solution.py:104
  149.2 10.0 %collective-permute-start.9 = (bf16[48,10368]{1,0:T(8,128)(2,1)S(1)}, bf16[48,10368]{1,0:T(8,128)(2,1)S(1)}, u32[]{:S(2)}, u32[]{:S(2)}) collective-permute-start(bf16[48,10368]{1,0:T(8,128)(2,1)S(1)} %collective-permute-done.5), channel_id=1, source_target_pairs={{0,4},{1,5},{4,8},{5,9},{8,12},{9,13},{12,14},{13,15},{14,10},{15,... | collective-permute-start | bytes 2985992 | tf_op jit(solution)/shard_map/ppermute | solution.py:104
  164.8 16.4 %collective-permute-done.9 = bf16[48,10368]{1,0:T(8,128)(2,1)S(1)} collective-permute-done((bf16[48,10368]{1,0:T(8,128)(2,1)S(1)}, bf16[48,10368]{1,0:T(8,128)(2,1)S(1)}, u32[]{:S(2)}, u32[]{:S(2)}) %collective-permute-start.9) | collective-permute-done | bytes 995360 | tf_op jit(solution)/shard_map/ppermute | solution.py:104
  190.3 6.5 collective-permute-done.13
  201.9 4.9 all-to-all-start.2
  210.1 4.8 slice.314
  223.3 15.6 %all-to-all-done.2 = bf16[16,64,768]{2,1,0:T(8,128)(2,1)} async-done(((bf16[16,64,768]{2,1,0:T(8,128)(2,1)}), bf16[16,64,768]{2,1,0:T(8,128)(2,1)}, u32[]{:S(2)}, u32[]{:S(2)}) %all-to-all-start.2) | async-done | bytes 1572896 | tf_op jit(solution)/shard_map/all_to_all | solution.py:304
  262.5 10.0 %reshape.833 = bf16[16,48,4,768]{3,2,1,0:T(4,128)(2,1)} reshape(bf16[768,3072]{1,0:T(8,128)(2,1)} %slice.314) | data formatting | bytes 9437184 | tf_op jit(solution)/shard_map/reshape | solution.py:131
  275.9 5.6 multiply_convert_fusion.5
  288.8 26.9 %all_gather.9 = bf16[16,32,768]{2,1,0:T(8,128)(2,1)S(1)} all-gather(bf16[1,32,768]{2,1,0:T(8,128)(2,1)S(1)} %bitcast.276), channel_id=1, replica_groups=mesh['pair'=2,'dp'=16] {'dp'}, dimensions={0}, use_global_device_ids=true | all-gather | bytes 835584 | tf_op jit(solution)/shard_map/all_gather | solution.py:354
  319.8 5.3 fusion.219
  331.2 6.6 all-to-all-done.3
  342.3 5.9 fusion.47
  348.2 14.8 %all_to_all.52 = bf16[16,16,768]{2,1,0:T(8,128)(2,1)S(1)} all-to-all(bf16[16,16,768]{2,1,0:T(8,128)(2,1)S(1)} %bitcast.252), channel_id=1, replica_groups=mesh['pair'=2,'dp'=16] {'dp'}, dimensions={0} | all-to-all | bytes 786432 | tf_op jit(solution)/shard_map/all_to_all | solution.py:383
  391.7 5.2 fusion.178
  424.9 6.0 add_convert_fusion
  436.8 19.7 %collective-permute-done.21 = bf16[512,768]{1,0:T(8,128)(2,1)S(1)} collective-permute-done((bf16[512,768]{1,0:T(8,128)(2,1)S(1)}, bf16[512,768]{1,0:T(8,128)(2,1)S(1)}, u32[]{:S(2)}, u32[]{:S(2)}) %collective-permute-start.21) | collective-permute-done | bytes 786464 | tf_op jit(solution)/shard_map/ppermute | solution.py:448
  465.6 20.3 %collective-permute-done.20 = bf16[512,768]{1,0:T(8,128)(2,1)S(1)} collective-permute-done((bf16[512,768]{1,0:T(8,128)(2,1)S(1)}, bf16[512,768]{1,0:T(8,128)(2,1)S(1)}, u32[]{:S(2)}, u32[]{:S(2)}) %collective-permute-start.20) | collective-permute-done | bytes 786464 | tf_op jit(solution)/shard_map/ppermute | solution.py:448
  488.2 21.2 %all-to-all-done.6 = bf16[16,64,768]{2,1,0:T(8,128)(2,1)} async-done(((bf16[16,64,768]{2,1,0:T(8,128)(2,1)}), bf16[16,64,768]{2,1,0:T(8,128)(2,1)}, u32[]{:S(2)}, u32[]{:S(2)}) %all-to-all-start.6) | async-done | bytes 1572896 | tf_op jit(solution)/shard_map/all_to_all | solution.py:451
  509.4 8.8 %all-to-all-start.5 = ((bf16[16,64,768]{2,1,0:T(8,128)(2,1)}), bf16[16,64,768]{2,1,0:T(8,128)(2,1)}, u32[]{:S(2)}, u32[]{:S(2)}) async-start(bf16[16,64,768]{2,1,0:T(8,128)(2,1)} %bitcast.256), calls=%async_computation.5 | async-start | bytes 3145728 | tf_op jit(solution)/shard_map/all_to_all | solution.py:451
  525.9 38.9 %collective-permute-done.23 = bf16[16,32,288]{2,1,0:T(8,128)(2,1)} collective-permute-done((bf16[16,32,288]{2,1,0:T(8,128)(2,1)S(1)}, bf16[16,32,288]{2,1,0:T(8,128)(2,1)}, u32[]{:S(2)}, u32[]{:S(2)}) %collective-permute-start.23) | collective-permute-done | bytes 294944 | tf_op jit(solution)/shard_map/ppermute | solution.py:408
  566.8 5.7 collective-permute-done.18
  576.3 6.0 all-to-all-start.7
  582.4 24.8 %fusion.2 = f32[3144,768]{1,0:T(8,128)} fusion(s32[2048]{0:T(1024)S(1)} %eq.386, bf16[1024,768]{1,0:T(8,128)(2,1)} %bitcast.95, bf16[1024,768]{1,0:T(8,128)(2,1)} %bitcast.91), kind=kOutput, calls=%fused_computation.13 | convolution fusion | flops 9902899200 | bytes 12812288 | tf_op jit(solution)/shard_map/dot_general | solution.py:42
  608.5 9.2 %multiply_reduce_fusion = (f32[]{:T(128)}, f32[3144,768]{1,0:T(8,128)}) fusion(f32[3144,768]{1,0:T(8,128)} %fusion.2, bf16[256,768]{1,0:T(8,128)(2,1)} %get-tuple-element.325, bf16[256,768]{1,0:T(8,128)(2,1)} %get-tuple-element.324, bf16[256,3144]{0,1:T(8,128)(2,1)S(1)} %copy-done.4, bf16[256,3144]{0,1:T(8,128)(2,1)S(1)} %get-tuple-element.320), kind=kOutput, calls=%fused_computation.21 | convolution fusion | flops 2487797760 | bytes 23322628 | tf_op jit(solution)/shard_map/dot_general | solution.py:42
  619.8 22.9 %all_gather.11 = bf16[256,768]{1,0:T(8,128)(2,1)S(1)} all-gather(bf16[16,768]{1,0:T(8,128)(2,1)S(1)} %convert_element_type.264), channel_id=1, replica_groups=mesh['pair'=2,'dp'=16] {'dp'}, dimensions={0}, use_global_device_ids=true | all-gather | bytes 417792 | tf_op jit(solution)/shard_map/all_gather | solution.py:485
  686.4 24.5 %multiply_subtract_fusion = (f32[3144,768]{1,0:T(8,128)}, f32[3144,768]{1,0:T(8,128)}, f32[3144,768]{1,0:T(8,128)}) fusion(f32[3144,768]{1,0:T(8,128)} %param.54, f32[3144,768]{1,0:T(8,128)} %get-tuple-element.404, f32[]{:T(128)S(6)} %min.19, f32[3144,768]{1,0:T(8,128)} %param.61, f32[3144,768]{1,0:T(8,128)} %param.68), kind=kLoop, calls=%fused_computation.19 | loop fusion | flops 38633472 | bytes 67608576 | tf_op jit(solution)/shard_map/sub | solution.py:185
  (648 shorter events, 268.6 us)
Async XLA Ops:
  24.8 78.9 %collective-permute-start = (bf16[48,10368]{1,0:T(8,128)(2,1)}, bf16[48,10368]{1,0:T(8,128)(2,1)}, u32[]{:S(2)}, u32[]{:S(2)}) collective-permute-start(bf16[48,10368]{1,0:T(8,128)(2,1)} %broadcast_select_fusion.3), channel_id=1, source_target_pairs={{0,1},{1,0},{2,3},{3,2},{4,5},{5,4},{6,7},{7,6},{8,9},{9,8},{10,11... | collective-permute-start | bytes 2985992 | tf_op jit(solution)/shard_map/ppermute | solution.py:97
  25.3 75.9 %collective-permute-start.1 = (bf16[48,10368]{1,0:T(8,128)(2,1)}, bf16[48,10368]{1,0:T(8,128)(2,1)}, u32[]{:S(2)}, u32[]{:S(2)}) collective-permute-start(bf16[48,10368]{1,0:T(8,128)(2,1)} %broadcast_select_fusion.3), channel_id=1, source_target_pairs={{0,4},{1,5},{4,8},{5,9},{8,12},{9,13},{12,14},{13,15},{14,10},{15,... | collective-permute-start | bytes 2985992 | tf_op jit(solution)/shard_map/ppermute | solution.py:104
  27.9 75.5 %collective-permute-start.3 = (bf16[48,10368]{1,0:T(8,128)(2,1)}, bf16[48,10368]{1,0:T(8,128)(2,1)}, u32[]{:S(2)}, u32[]{:S(2)}) collective-permute-start(bf16[48,10368]{1,0:T(8,128)(2,1)} %broadcast_select_fusion.3), channel_id=1, source_target_pairs={{4,0},{5,1},{8,4},{9,5},{12,8},{13,9},{14,12},{15,13},{10,14},{11,... | collective-permute-start | bytes 2985992 | tf_op jit(solution)/shard_map/ppermute | solution.py:105
  31.1 45.1 %all-to-all-start = ((s32[16,1,160]{2,1,0:T(1,128)}), s32[16,1,160]{2,1,0:T(1,128)}, u32[]{:S(2)}, u32[]{:S(2)}) async-start(s32[16,1,160]{2,1,0:T(1,128)} %copy.281), calls=%async_computation | async-start | bytes 32768 | tf_op jit(solution)/shard_map/all_to_all | solution.py:286
  95.3 106.6 %all-to-all-start.1 = ((bf16[16,64,768]{2,1,0:T(8,128)(2,1)}), bf16[16,64,768]{2,1,0:T(8,128)(2,1)S(1)}, u32[]{:S(2)}, u32[]{:S(2)}) async-start(bf16[16,64,768]{2,1,0:T(8,128)(2,1)} %bitcast.242), calls=%async_computation.1 | async-start | bytes 3145728 | tf_op jit(solution)/shard_map/all_to_all | solution.py:304
  101.2 58.2 %collective-permute-start.2 = (bf16[48,10368]{1,0:T(8,128)(2,1)}, bf16[48,10368]{1,0:T(8,128)(2,1)S(1)}, u32[]{:S(2)}, u32[]{:S(2)}) collective-permute-start(bf16[48,10368]{1,0:T(8,128)(2,1)} %collective-permute-done.1), channel_id=1, source_target_pairs={{0,1},{1,0},{2,3},{3,2},{4,5},{5,4},{6,7},{7,6},{8,9},{9,8},{10,11... | collective-permute-start | bytes 2985992 | tf_op jit(solution)/shard_map/ppermute | solution.py:97
  101.7 47.5 %collective-permute-start.5 = (bf16[48,10368]{1,0:T(8,128)(2,1)}, bf16[48,10368]{1,0:T(8,128)(2,1)S(1)}, u32[]{:S(2)}, u32[]{:S(2)}) collective-permute-start(bf16[48,10368]{1,0:T(8,128)(2,1)} %collective-permute-done.1), channel_id=1, source_target_pairs={{0,4},{1,5},{4,8},{5,9},{8,12},{9,13},{12,14},{13,15},{14,10},{15,... | collective-permute-start | bytes 2985992 | tf_op jit(solution)/shard_map/ppermute | solution.py:104
  103.4 59.3 %collective-permute-start.4 = (bf16[48,10368]{1,0:T(8,128)(2,1)}, bf16[48,10368]{1,0:T(8,128)(2,1)S(1)}, u32[]{:S(2)}, u32[]{:S(2)}) collective-permute-start(bf16[48,10368]{1,0:T(8,128)(2,1)} %collective-permute-done.3), channel_id=1, source_target_pairs={{0,1},{1,0},{2,3},{3,2},{4,5},{5,4},{6,7},{7,6},{8,9},{9,8},{10,11... | collective-permute-start | bytes 2985992 | tf_op jit(solution)/shard_map/ppermute | solution.py:97
  103.5 55.8 %collective-permute-start.7 = (bf16[48,10368]{1,0:T(8,128)(2,1)}, bf16[48,10368]{1,0:T(8,128)(2,1)S(1)}, u32[]{:S(2)}, u32[]{:S(2)}) collective-permute-start(bf16[48,10368]{1,0:T(8,128)(2,1)} %collective-permute-done.3), channel_id=1, source_target_pairs={{4,0},{5,1},{8,4},{9,5},{12,8},{13,9},{14,12},{15,13},{10,14},{11,... | collective-permute-start | bytes 2985992 | tf_op jit(solution)/shard_map/ppermute | solution.py:105
  149.2 36.5 %collective-permute-start.6 = (bf16[48,10368]{1,0:T(8,128)(2,1)S(1)}, bf16[48,10368]{1,0:T(8,128)(2,1)S(1)}, u32[]{:S(2)}, u32[]{:S(2)}) collective-permute-start(bf16[48,10368]{1,0:T(8,128)(2,1)S(1)} %collective-permute-done.5), channel_id=1, source_target_pairs={{0,1},{1,0},{2,3},{3,2},{4,5},{5,4},{6,7},{7,6},{8,9},{9,8},{10,11... | collective-permute-start | bytes 2985992 | tf_op jit(solution)/shard_map/ppermute | solution.py:97
  149.2 32.0 %collective-permute-start.9 = (bf16[48,10368]{1,0:T(8,128)(2,1)S(1)}, bf16[48,10368]{1,0:T(8,128)(2,1)S(1)}, u32[]{:S(2)}, u32[]{:S(2)}) collective-permute-start(bf16[48,10368]{1,0:T(8,128)(2,1)S(1)} %collective-permute-done.5), channel_id=1, source_target_pairs={{0,4},{1,5},{4,8},{5,9},{8,12},{9,13},{12,14},{13,15},{14,10},{15,... | collective-permute-start | bytes 2985992 | tf_op jit(solution)/shard_map/ppermute | solution.py:104
  159.2 29.0 %collective-permute-start.8 = (bf16[48,10368]{1,0:T(8,128)(2,1)S(1)}, bf16[48,10368]{1,0:T(8,128)(2,1)S(1)}, u32[]{:S(2)}, u32[]{:S(2)}) collective-permute-start(bf16[48,10368]{1,0:T(8,128)(2,1)S(1)} %collective-permute-done.7), channel_id=1, source_target_pairs={{0,1},{1,0},{2,3},{3,2},{4,5},{5,4},{6,7},{7,6},{8,9},{9,8},{10,11... | collective-permute-start | bytes 2985992 | tf_op jit(solution)/shard_map/ppermute | solution.py:97
  159.5 24.8 %collective-permute-start.11 = (bf16[48,10368]{1,0:T(8,128)(2,1)S(1)}, bf16[48,10368]{1,0:T(8,128)(2,1)S(1)}, u32[]{:S(2)}, u32[]{:S(2)}) collective-permute-start(bf16[48,10368]{1,0:T(8,128)(2,1)S(1)} %collective-permute-done.7), channel_id=1, source_target_pairs={{4,0},{5,1},{8,4},{9,5},{12,8},{13,9},{14,12},{15,13},{10,14},{11,... | collective-permute-start | bytes 2985992 | tf_op jit(solution)/shard_map/ppermute | solution.py:105
  181.2 15.6 %collective-permute-start.13 = (bf16[24,10368]{1,0:T(8,128)(2,1)S(1)}, bf16[24,10368]{1,0:T(8,128)(2,1)S(1)}, u32[]{:S(2)}, u32[]{:S(2)}) collective-permute-start(bf16[24,10368]{1,0:T(8,128)(2,1)S(1)} %slice.291), channel_id=1, source_target_pairs={{0,4},{1,5},{4,8},{5,9},{8,12},{9,13},{12,14},{13,15},{14,10},{15,... | collective-permute-start | bytes 1493000 | tf_op jit(solution)/shard_map/ppermute | solution.py:108
  184.3 13.3 %collective-permute-start.14 = (bf16[24,10368]{1,0:T(8,128)(2,1)S(1)}, bf16[24,10368]{1,0:T(8,128)(2,1)S(1)}, u32[]{:S(2)}, u32[]{:S(2)}) collective-permute-start(bf16[24,10368]{1,0:T(8,128)(2,1)S(1)} %slice.292), channel_id=1, source_target_pairs={{4,0},{5,1},{8,4},{9,5},{12,8},{13,9},{14,12},{15,13},{10,14},{11,... | collective-permute-start | bytes 1493000 | tf_op jit(solution)/shard_map/ppermute | solution.py:109
  185.6 12.1 %collective-permute-start.10 = (bf16[48,10368]{1,0:T(8,128)(2,1)S(1)}, bf16[48,10368]{1,0:T(8,128)(2,1)S(1)}, u32[]{:S(2)}, u32[]{:S(2)}) collective-permute-start(bf16[48,10368]{1,0:T(8,128)(2,1)S(1)} %collective-permute-done.9), channel_id=1, source_target_pairs={{0,1},{1,0},{2,3},{3,2},{4,5},{5,4},{6,7},{7,6},{8,9},{9,8},{10,11... | collective-permute-start | bytes 2985992 | tf_op jit(solution)/shard_map/ppermute | solution.py:97
  185.6 14.2 %collective-permute-start.12 = (bf16[48,10368]{1,0:T(8,128)(2,1)S(1)}, bf16[48,10368]{1,0:T(8,128)(2,1)S(1)}, u32[]{:S(2)}, u32[]{:S(2)}) collective-permute-start(bf16[48,10368]{1,0:T(8,128)(2,1)S(1)} %collective-permute-done.11), channel_id=1, source_target_pairs={{0,1},{1,0},{2,3},{3,2},{4,5},{5,4},{6,7},{7,6},{8,9},{9,8},{10,11... | collective-permute-start | bytes 2985992 | tf_op jit(solution)/shard_map/ppermute | solution.py:97
  201.9 37.0 %all-to-all-start.2 = ((bf16[16,64,768]{2,1,0:T(8,128)(2,1)}), bf16[16,64,768]{2,1,0:T(8,128)(2,1)}, u32[]{:S(2)}, u32[]{:S(2)}) async-start(bf16[16,64,768]{2,1,0:T(8,128)(2,1)} %bitcast.55), calls=%async_computation.2 | async-start | bytes 3145728 | tf_op jit(solution)/shard_map/all_to_all | solution.py:304
  327.5 10.4 %all-to-all-start.3 = ((f32[16,4,256]{2,1,0:T(4,128)}), f32[16,4,256]{2,1,0:T(4,128)S(1)}, u32[]{:S(2)}, u32[]{:S(2)}) async-start(f32[16,4,256]{2,1,0:T(4,128)} %broadcast_in_dim.460), calls=%async_computation.3 | async-start | bytes 131072 | tf_op jit(solution)/shard_map/all_to_all | solution.py:194
  331.0 276.2 %reduce-scatter.4.cloned.1.call-start = ((), (), s32[]{:S(2)}) async-start(), calls=%async_computation.11 | async-start | bytes 4386816 | tf_op jit(solution)/shard_map/reduce_scatter | solution.py:479
  434.2 22.4 %collective-permute-start.21 = (bf16[512,768]{1,0:T(8,128)(2,1)S(1)}, bf16[512,768]{1,0:T(8,128)(2,1)S(1)}, u32[]{:S(2)}, u32[]{:S(2)}) collective-permute-start(bf16[512,768]{1,0:T(8,128)(2,1)S(1)} %copy-done.19), channel_id=1, source_target_pairs={{16,0},{17,1},{18,2},{19,3},{20,4},{21,5},{22,6},{23,7},{24,8},{25... | collective-permute-start | bytes 2359304 | tf_op jit(solution)/shard_map/ppermute | solution.py:448
  435.5 28.0 %collective-permute-start.24 = (bf16[32,4608]{1,0:T(8,128)(2,1)S(1)}, bf16[32,4608]{1,0:T(8,128)(2,1)S(1)}, u32[]{:S(2)}, u32[]{:S(2)}) collective-permute-start(bf16[32,4608]{1,0:T(8,128)(2,1)S(1)} %pad_maximum_fusion.9), channel_id=1, source_target_pairs={{16,0},{17,1},{18,2},{19,3},{20,4},{21,5},{22,6},{23,7},{24,8},{25... | collective-permute-start | bytes 884744 | tf_op jit(solution)/shard_map/ppermute | solution.py:409
  458.8 50.5 %all-to-all-start.6 = ((bf16[16,64,768]{2,1,0:T(8,128)(2,1)}), bf16[16,64,768]{2,1,0:T(8,128)(2,1)}, u32[]{:S(2)}, u32[]{:S(2)}) async-start(bf16[16,64,768]{2,1,0:T(8,128)(2,1)} %bitcast.94), calls=%async_computation.6 | async-start | bytes 3145728 | tf_op jit(solution)/shard_map/all_to_all | solution.py:451
  463.4 181.4 %all-gather.2.cloned.1.call-start = ((), (), s32[]{:S(2)}) async-start(), calls=%async_computation.10 | async-start | bytes 5013504 | tf_op jit(solution)/shard_map/all_gather | solution.py:412
  464.3 21.6 %collective-permute-start.20 = (bf16[512,768]{1,0:T(8,128)(2,1)S(1)}, bf16[512,768]{1,0:T(8,128)(2,1)S(1)}, u32[]{:S(2)}, u32[]{:S(2)}) collective-permute-start(bf16[512,768]{1,0:T(8,128)(2,1)S(1)} %copy-done.17), channel_id=1, source_target_pairs={{16,0},{17,1},{18,2},{19,3},{20,4},{21,5},{22,6},{23,7},{24,8},{25... | collective-permute-start | bytes 2359304 | tf_op jit(solution)/shard_map/ppermute | solution.py:448
  509.4 66.9 %all-to-all-start.5 = ((bf16[16,64,768]{2,1,0:T(8,128)(2,1)}), bf16[16,64,768]{2,1,0:T(8,128)(2,1)}, u32[]{:S(2)}, u32[]{:S(2)}) async-start(bf16[16,64,768]{2,1,0:T(8,128)(2,1)} %bitcast.256), calls=%async_computation.5 | async-start | bytes 3145728 | tf_op jit(solution)/shard_map/all_to_all | solution.py:451
  518.2 55.3 %collective-permute-start.17 = (bf16[256,3144]{0,1:T(8,128)(2,1)S(1)}, bf16[256,3144]{0,1:T(8,128)(2,1)}, u32[]{:S(2)}, u32[]{:S(2)}) collective-permute-start(bf16[256,3144]{0,1:T(8,128)(2,1)S(1)} %copy-done.3), channel_id=1, source_target_pairs={{0,16},{16,0},{1,17},{17,1},{2,18},{18,2},{3,19},{19,3},{4,20},{20... | collective-permute-start | bytes 4829192 | tf_op jit(solution)/shard_map/ppermute | solution.py:387
  521.2 43.7 %collective-permute-start.23 = (bf16[16,32,288]{2,1,0:T(8,128)(2,1)S(1)}, bf16[16,32,288]{2,1,0:T(8,128)(2,1)}, u32[]{:S(2)}, u32[]{:S(2)}) collective-permute-start(bf16[16,32,288]{2,1,0:T(8,128)(2,1)S(1)} %pad_maximum_fusion.8), channel_id=1, source_target_pairs={{16,0},{17,1},{18,2},{19,3},{20,4},{21,5},{22,6},{23,7},{24,8},{25... | collective-permute-start | bytes 884744 | tf_op jit(solution)/shard_map/ppermute | solution.py:408
  522.5 50.1 %collective-permute-start.18 = (bf16[256,768]{1,0:T(8,128)(2,1)S(1)}, bf16[256,768]{1,0:T(8,128)(2,1)S(1)}, u32[]{:S(2)}, u32[]{:S(2)}) collective-permute-start(bf16[256,768]{1,0:T(8,128)(2,1)S(1)} %bitcast.244), channel_id=1, source_target_pairs={{0,16},{16,0},{1,17},{17,1},{2,18},{18,2},{3,19},{19,3},{4,20},{20... | collective-permute-start | bytes 1179656 | tf_op jit(solution)/shard_map/ppermute | solution.py:388
  576.3 68.5 %all-to-all-start.7 = ((bf16[16,32,288]{2,1,0:T(8,128)(2,1)}), bf16[16,32,288]{2,1,0:T(8,128)(2,1)}, u32[]{:S(2)}, u32[]{:S(2)}) async-start(bf16[16,32,288]{2,1,0:T(8,128)(2,1)} %select_add_fusion.1), calls=%async_computation.7 | async-start | bytes 786432 | tf_op jit(solution)/shard_map/all_to_all | solution.py:410
  607.2 10.9 %collective-permute-start.22 = (bf16[48,2688]{1,0:T(8,128)(2,1)}, bf16[48,2688]{1,0:T(8,128)(2,1)}, u32[]{:S(2)}, u32[]{:S(2)}) collective-permute-start(bf16[48,2688]{1,0:T(8,128)(2,1)} %reduce-scatter.4.cloned.1.call-done), channel_id=1, source_target_pairs={{16,0},{17,1},{18,2},{19,3},{20,4},{21,5},{22,6},{23,7},{24,8},{25... | collective-permute-start | bytes 774152 | tf_op jit(solution)/shard_map/ppermute | solution.py:480
  660.0 11.0 %all-to-all-start.8 = ((f32[32,1,128]{2,1,0:T(1,128)}), f32[32,1,128]{2,1,0:T(1,128)S(1)}, u32[]{:S(2)}, u32[]{:S(2)}) async-start(f32[32,1,128]{2,1,0:T(1,128)} %broadcast_in_dim.478), calls=%async_computation.8 | async-start | bytes 32768 | tf_op jit(solution)/shard_map/all_to_all | solution.py:194
  (156 other events, 1482.7 us)
Sparse Core Ops, SparseCore 0:
  433.2 102.9 reduce-scatter.3
  539.1 63.5 all-gather.1

commit v2 on v1

v2 whole, which is shorter than its diff:
```python
import functools

import jax
import jax.numpy as jnp
from jax import lax
from jax.experimental import pallas as pl
from jax.experimental.pallas import tpu as pltpu
from jax.sharding import PartitionSpec as P

H = 12
MB = 2
STEP = 10
LONGEST = 256
LANES = 128
VMEM_BYTES = 56 * 1024 * 1024


learn_rate = 0.25
beta_one = 0.9
beta_two = 0.999
adam_eps = 1e-08
decay_rate = 0.1
clip_limit = 0.02
norm_eps = 1e-05
neg_big = -1000000000.0
gelu_scale = 0.7978845608028654
gelu_cube = 0.044715

low = jnp.bfloat16
wide = jnp.float32


def layer_norm(values, norm_gain, norm_shift):
    center = jnp.mean(values, axis=-1, keepdims=True)
    offsets = values - center
    spread = jnp.mean(offsets * offsets, axis=-1, keepdims=True)
    return offsets * lax.rsqrt(spread + norm_eps) * norm_gain + norm_shift


def gelu_tanh(values):
    return jax.nn.gelu(values, approximate=True)


def dot_plain(left_side, right_side):
    return jnp.dot(left_side, right_side, preferred_element_type=wide)


def dot_first(left_side, right_side):
    return lax.dot_general(
        left_side, right_side, (((0,), (0,)), ((), ())), preferred_element_type=wide
    )


def dot_last(left_side, right_side):
    return lax.dot_general(
        left_side, right_side, (((1,), (1,)), ((), ())), preferred_element_type=wide
    )


def chip_ring(chips):
    if chips % 8:
        return list(range(chips))
    if chips == 8:
        return [0, 2, 4, 6, 7, 5, 3, 1]
    lines = chips // 4
    order = list(range(lines))
    for k in range(0, lines - 3, 4):
        order[k + 2], order[k + 3] = order[k + 3], order[k + 2]
    ring = [order[0] * 4]
    for k, line in enumerate(order):
        columns = (1, 2, 3) if k % 2 == 0 else (3, 2, 1)
        ring = ring + [line * 4 + column for column in columns]
    return ring + [line * 4 for line in reversed(order[1:])]


def ring_gather(block, hold):
    devices = lax.axis_size("dp")
    if devices % 4:
        return lax.all_gather(block, "dp", axis=0), hold
    chips = devices // 2
    ring = chip_ring(chips)
    place_of = [ring.index(chip) for chip in range(chips)]
    me = lax.axis_index("dp")
    core = me % 2
    place = jnp.asarray(place_of, jnp.int32)[me // 2]
    onward = [(2 * ring[k] + c, 2 * ring[(k + 1) % chips] + c) for k in range(chips) for c in (0, 1)]
    backward = [(there, here) for here, there in onward]
    across = [(d, d ^ 1) for d in range(devices)]
    half_rows = block.shape[0] // 32 * 16
    whole = jnp.zeros((devices,) + block.shape, block.dtype)

    def keep(whole, piece, distance):
        chip = jnp.asarray(ring, jnp.int32)[(place + distance) % chips]
        partner = lax.ppermute(piece, "dp", across)
        whole = lax.dynamic_update_slice(whole, piece[None], (2 * chip + core, 0, 0))
        return lax.dynamic_update_slice(whole, partner[None], (2 * chip + 1 - core, 0, 0))

    ahead, behind = block, block
    for distance in range(1, chips // 2):
        ahead = lax.ppermute(ahead, "dp", onward)
        behind = lax.ppermute(behind, "dp", backward)
        if distance == 1:
            whole = keep(whole, block, 0)
            ahead, behind, hold = lax.optimization_barrier((ahead, behind, hold))
        whole = keep(whole, ahead, -distance)
        whole = keep(whole, behind, distance)
    first = lax.ppermute(ahead[:half_rows], "dp", onward)
    second = lax.ppermute(behind[half_rows:], "dp", backward)
    whole = keep(whole, jnp.concatenate([first, second], axis=0), chips // 2)
    return whole, hold


def adam_update(master, moment_one, moment_two, gradient, factor):
    clipped = gradient * factor
    new_one = beta_one * moment_one + (1.0 - beta_one) * clipped
    new_two = beta_two * moment_two + (1.0 - beta_two) * clipped * clipped
    fixed_one = new_one / (1.0 - beta_one**STEP)
    fixed_two = new_two / (1.0 - beta_two**STEP)
    updated = master - learn_rate * (
        fixed_one / (jnp.sqrt(fixed_two) + adam_eps) + decay_rate * master
    )
    return (updated, new_one, new_two)


def to_all(value, axis):
    copies = lax.axis_size(axis)
    spread = jnp.broadcast_to(value[None], (copies,) + value.shape)
    return lax.all_to_all(spread, axis, split_axis=0, concat_axis=0, tiled=True)


def norm_parts(values):
    center = jnp.mean(values, axis=-1, keepdims=True)
    offsets = values - center
    spread = jnp.mean(offsets * offsets, axis=-1, keepdims=True)
    scale = lax.rsqrt(spread + norm_eps)
    return offsets * scale, scale


def norm_back(grad, centered, scale, gain):
    inner = grad * gain
    mean_one = jnp.mean(inner, axis=-1, keepdims=True)
    mean_two = jnp.mean(inner * centered, axis=-1, keepdims=True)
    d_values = scale * (inner - mean_one - centered * mean_two)
    d_gain = jnp.sum(grad * centered, axis=0, keepdims=True)
    return d_values, d_gain, jnp.sum(grad, axis=0, keepdims=True)


def gelu_back(values):
    inner = gelu_scale * (values + gelu_cube * values * values * values)
    bend = jnp.tanh(inner)
    slope = gelu_scale * (1.0 + 3.0 * gelu_cube * values * values)
    return 0.5 * (1.0 + bend) + 0.5 * values * (1.0 - bend * bend) * slope


def spread_heads(rows, width):
    size = width // H
    head_of = lax.broadcasted_iota(jnp.int32, rows.shape, 1) // size
    nothing = jnp.zeros_like(rows)
    return jnp.concatenate([jnp.where(head_of == h, rows, nothing) for h in range(H)], axis=0)


def join_heads(spread, count, width):
    size = width // H
    head_of = lax.broadcasted_iota(jnp.int32, (count, width), 1) // size
    total = jnp.zeros((count, width), wide)
    for h in range(H):
        total = total + jnp.where(head_of == h, spread[h * count : (h + 1) * count], 0.0)
    return total


def one_hot(column, count):
    spots = lax.broadcasted_iota(jnp.int32, (column.shape[0], count), 1)
    return jnp.where(column == spots, 1.0, 0.0).astype(low)


def weight(w_ref, j):
    devices, _, width = w_ref.shape
    rows = width // devices
    return w_ref[:, j * rows : (j + 1) * rows, :].reshape(width, width)


def weight_copies(w_hbm, w_ref, sems):
    rows = w_ref.shape[2] // w_ref.shape[0]
    cuts = (0, 3, 4, 8, 12)
    copies = []
    for k in range(4):
        span = pl.ds(cuts[k] * rows, (cuts[k + 1] - cuts[k]) * rows)
        copies.append(
            pltpu.make_async_copy(w_hbm.at[:, span, :], w_ref.at[:, span, :], sems.at[k])
        )
    for copy in copies:
        copy.start()
    return copies


def weight_tail(w_ref):
    devices, _, width = w_ref.shape
    rows = width // devices
    folds = w_ref.shape[1] // rows - 8
    return w_ref[:, 8 * rows : (8 + folds) * rows, :].reshape(folds * width, width)


def forward_kernel(
    cols_ref,
    docs_ref,
    picks_ref,
    back_ref,
    pos_ref,
    vec_ref,
    w_hbm,
    final_ref,
    x_ref,
    kv_ref,
    q_ref,
    probs_ref,
    attn_ref,
    mid_ref,
    pre_ref,
    top_ref,
    w_ref,
    sems,
):
    copies = weight_copies(w_hbm, w_ref, sems)
    batches, length, width = x_ref.shape
    picks = picks_ref.shape[1]
    devices, held, _ = back_ref.shape
    capacity = held // batches
    slot_count = devices * capacity
    scaling = (width // H) ** (-0.5)
    vec = vec_ref[...]

    def row(k):
        return vec[k : k + 1]

    for m in range(batches):
        sources = back_ref[:, m * capacity : (m + 1) * capacity, :].reshape(slot_count, width)
        pos = pos_ref[...]
        pick = one_hot(cols_ref[m, :, 0:1], slot_count)
        pick_pos = one_hot(cols_ref[m, :, 1:2], LONGEST)
        chosen = picks_ref[m, :, 0:1]
        select = one_hot(chosen, length)
        x_embed = dot_plain(pick, sources) + dot_plain(pick_pos, pos)
        x_ref[m] = x_embed
        pick_c = dot_plain(select, pick).astype(low)
        pick_pos_c = dot_plain(select, pick_pos).astype(low)
        x_chosen = dot_plain(pick_c, sources) + dot_plain(pick_pos_c, pos)
        normed = (norm_parts(x_embed)[0] * row(0) + row(1)).astype(low)
        normed_c = dot_plain(select, normed).astype(low)
        if m == 0:
            copies[0].wait()
        kv_ref[m, :, :width] = dot_plain(normed, weight(w_ref, 1)).astype(low)
        kv_ref[m, :, width:] = (dot_plain(normed, weight(w_ref, 2)) + row(7)).astype(low)
        queries = (dot_plain(normed_c, weight(w_ref, 0)) + row(6)).astype(low)
        q_ref[m * picks : (m + 1) * picks] = queries
        scores = dot_last(spread_heads(queries, width), kv_ref[m, :, :width]) * scaling
        spots = lax.broadcasted_iota(jnp.int32, (picks, length), 1)
        allowed = (picks_ref[m, :, 1:2] == docs_ref[m]) & (spots <= chosen)
        penalty = jnp.where(allowed, 0.0, 1.0)
        blocked = jnp.concatenate([penalty] * H, axis=0) > 0.5
        scores = jnp.where(blocked, neg_big, scores)
        row_max = jnp.max(scores, axis=-1, keepdims=True)
        weights_exp = jnp.exp(scores - row_max)
        probs = weights_exp / jnp.sum(weights_exp, axis=-1, keepdims=True)
        probs_ref[m] = probs
        spread = dot_plain(probs.astype(low), kv_ref[m, :, width:])
        attn_ref[m * picks : (m + 1) * picks] = join_heads(spread, picks, width).astype(low)
        mid_ref[m * picks : (m + 1) * picks] = x_chosen
    copies[1].wait()
    x_mid = mid_ref[...] + dot_plain(attn_ref[...], weight(w_ref, 3)) + row(8)
    mid_ref[...] = x_mid
    normed_two = (norm_parts(x_mid)[0] * row(2) + row(3)).astype(low)
    copies[2].wait()
    for j in range(4):
        span = slice(j * width, (j + 1) * width)
        pre_ref[:, span] = dot_plain(normed_two, weight(w_ref, 4 + j)) + row(10 + j)
    activated = gelu_tanh(pre_ref[...]).astype(low)
    copies[3].wait()
    x_top = x_mid + dot_plain(activated, weight_tail(w_ref)) + row(9)
    top_ref[...] = x_top
    final_ref[...] = (norm_parts(x_top)[0] * row(4) + row(5)).astype(low)


def run_forward(cols, docs, picked, back, pos, vec, whole):
    batches, length = cols.shape[:2]
    picks = picked.shape[1]
    width = vec.shape[1]
    devices = whole.shape[0]
    weight_rows = 12 * (width // devices)
    vmem = pl.BlockSpec(memory_space=pltpu.VMEM)
    count = batches * picks

    def shape(dims, kind):
        return jax.ShapeDtypeStruct(dims, kind)

    return pl.pallas_call(
        forward_kernel,
        out_shape=(
            shape((count, width), low),
            shape((batches, length, width), wide),
            shape((batches, length, 2 * width), low),
            shape((count, width), low),
            shape((batches, H * picks, length), wide),
            shape((count, width), low),
            shape((count, width), wide),
            shape((count, 4 * width), wide),
            shape((count, width), wide),
        ),
        in_specs=[vmem] * 6 + [pl.BlockSpec(memory_space=pl.ANY)],
        out_specs=(vmem,) * 9,
        scratch_shapes=[
            pltpu.VMEM((devices, weight_rows, width), low),
            pltpu.SemaphoreType.DMA((4,)),
        ],
        compiler_params=pltpu.CompilerParams(vmem_limit_bytes=VMEM_BYTES),
        name="layer_forward",
    )(cols, docs, picked, back, pos, vec, whole)


def backward_kernel(
    d_final_ref,
    cols_ref,
    picks_ref,
    vec_ref,
    x_ref,
    kv_ref,
    q_ref,
    probs_ref,
    attn_ref,
    mid_ref,
    pre_ref,
    top_ref,
    w_hbm,
    d_embed_ref,
    g_attn_ref,
    g_vec_ref,
    g_pos_ref,
    lefts_ref,
    rights_ref,
    w_ref,
    sems,
):
    copies = weight_copies(w_hbm, w_ref, sems)
    batches, length, width = x_ref.shape
    picks = picks_ref.shape[1]
    hidden = 4 * width
    scaling = (width // H) ** (-0.5)
    vec = vec_ref[...]

    def row(k):
        return vec[k : k + 1]

    def column_sum(values):
        return jnp.sum(values.astype(wide), axis=0, keepdims=True)

    centered, scale = norm_parts(top_ref[...])
    d_top, d_gain, d_shift = norm_back(d_final_ref[...], centered, scale, row(4))
    g_vec_ref[4:5] = d_gain
    g_vec_ref[5:6] = d_shift
    d_branch = d_top.astype(low)
    rights_ref[:, :width] = d_branch
    g_vec_ref[9:10] = column_sum(d_branch)
    pre = pre_ref[...]
    lefts_ref[:, :hidden] = gelu_tanh(pre).astype(low)
    copies[3].wait()
    d_pre = (dot_last(d_branch, weight_tail(w_ref)) * gelu_back(pre)).astype(low)
    rights_ref[:, width : width + hidden] = d_pre
    copies[2].wait()
    d_normed = jnp.zeros(d_top.shape, wide)
    for j in range(4):
        piece = d_pre[:, j * width : (j + 1) * width]
        g_vec_ref[10 + j : 11 + j] = column_sum(piece)
        d_normed = d_normed + dot_last(piece, weight(w_ref, 4 + j))
    centered, scale = norm_parts(mid_ref[...])
    lefts_ref[:, hidden : hidden + width] = (centered * row(2) + row(3)).astype(low)
    d_mid, d_gain, d_shift = norm_back(d_normed, centered, scale, row(2))
    g_vec_ref[2:3] = d_gain
    g_vec_ref[3:4] = d_shift
    d_mid = d_top + d_mid
    d_attn_branch = d_mid.astype(low)
    rights_ref[:, width + hidden :] = d_attn_branch
    lefts_ref[:, hidden + width :] = attn_ref[...]
    g_vec_ref[8:9] = column_sum(d_attn_branch)
    copies[1].wait()
    d_attended = dot_last(d_attn_branch, weight(w_ref, 3)).astype(low)
    copies[0].wait()
    for m in range(batches):
        mine = slice(m * picks, (m + 1) * picks)
        keys_all = kv_ref[m, :, :width]
        values = kv_ref[m, :, width:]
        probs = probs_ref[m]
        d_spread = spread_heads(d_attended[mine], width)
        d_probs = dot_last(d_spread, values)
        row_inner = jnp.sum(probs * d_probs, axis=-1, keepdims=True)
        d_scores = (probs * (d_probs - row_inner)).astype(low)
        q_spread = spread_heads(q_ref[mine], width)
        d_query = (join_heads(dot_plain(d_scores, keys_all), picks, width) * scaling).astype(low)
        select = one_hot(picks_ref[m, :, 0:1], length)
        d_query = dot_first(select, d_query).astype(low)
        d_key = (dot_first(d_scores, q_spread) * scaling).astype(low)
        d_value = dot_first(probs.astype(low), d_spread).astype(low)
        centered, scale = norm_parts(x_ref[m])
        normed = (centered * row(0) + row(1)).astype(low)
        d_normed = jnp.zeros((length, width), wide)
        for j, piece in enumerate((d_query, d_key, d_value)):
            span = slice(j * width, (j + 1) * width)
            product = dot_first(normed, piece)
            if m == 0:
                g_attn_ref[:, span] = product
            else:
                g_attn_ref[:, span] += product
            d_normed = d_normed + dot_last(piece, weight(w_ref, j))
        d_embed, d_gain, d_shift = norm_back(d_normed, centered, scale, row(0))
        d_embed = d_embed + lax.dot_general(
            jnp.where(
                picks_ref[m, :, 0:1]
                == lax.broadcasted_iota(jnp.int32, (picks, length), 1),
                1.0,
                0.0,
            ),
            d_mid[mine],
            (((0,), (0,)), ((), ())),
            precision=lax.Precision.HIGHEST,
            preferred_element_type=wide,
        )
        d_embed = d_embed.astype(low)
        d_embed_ref[m] = d_embed
        sums = (d_gain, d_shift, column_sum(d_query), column_sum(d_value))
        g_pos = dot_first(one_hot(cols_ref[m, :, 1:2], LONGEST), d_embed)
        for k, value in zip((0, 1, 6, 7), sums):
            if m == 0:
                g_vec_ref[k : k + 1] = value
            else:
                g_vec_ref[k : k + 1] += value
        if m == 0:
            g_pos_ref[...] = g_pos
        else:
            g_pos_ref[...] += g_pos
    g_vec_ref[14:16] = jnp.zeros((2, width), wide)


def run_backward(d_final, cols, picked, vec, kept, whole):
    batches, length = cols.shape[:2]
    picks = picked.shape[1]
    width = vec.shape[1]
    devices = whole.shape[0]
    weight_rows = 12 * (width // devices)
    vmem = pl.BlockSpec(memory_space=pltpu.VMEM)
    count = batches * picks

    def shape(dims, kind):
        return jax.ShapeDtypeStruct(dims, kind)

    return pl.pallas_call(
        backward_kernel,
        out_shape=(
            shape((batches, length, width), low),
            shape((width, 3 * width), wide),
            shape((16, width), wide),
            shape((LONGEST, width), wide),
            shape((count, 6 * width), low),
            shape((count, 6 * width), low),
        ),
        in_specs=[vmem] * 12 + [pl.BlockSpec(memory_space=pl.ANY)],
        out_specs=(vmem,) * 6,
        scratch_shapes=[
            pltpu.VMEM((devices, weight_rows, width), low),
            pltpu.SemaphoreType.DMA((4,)),
        ],
        compiler_params=pltpu.CompilerParams(vmem_limit_bytes=VMEM_BYTES),
        name="layer_backward",
    )(d_final, cols, picked, vec, *kept, whole)


def pack_kernel(
    student_ref, attn_in, attn_out, mlp_in, mlp_out, pos, vecs, t_attn_in, t_attn_out, t_mlp_in, t_mlp_out, t_pos, t_vecs, out_ref
):
    is_student = student_ref[0] == 1
    rows, width = attn_out.shape

    def write(refs):
        ins, out, up, down, spots, small = refs
        for j in range(3):
            out_ref[j * rows : (j + 1) * rows] = ins[:, j * width : (j + 1) * width].astype(low)
        out_ref[3 * rows : 4 * rows] = out[...].astype(low)
        for j in range(4):
            out_ref[(4 + j) * rows : (5 + j) * rows] = up[
                :, j * width : (j + 1) * width
            ].astype(low)
        out_ref[8 * rows : 12 * rows] = down[...].astype(low)
        end = 12 * rows + spots.shape[0]
        out_ref[12 * rows : end] = spots[...].astype(low)
        out_ref[end : end + 16] = small[...].astype(low)

    @pl.when(is_student)
    def _():
        write((attn_in, attn_out, mlp_in, mlp_out, pos, vecs))

    @pl.when(jnp.logical_not(is_student))
    def _():
        write((t_attn_in, t_attn_out, t_mlp_in, t_mlp_out, t_pos, t_vecs))


def pack_plain(attn_in, attn_out, mlp_in, mlp_out, pos, vecs):
    width = attn_out.shape[1]
    ins = [attn_in[:, j * width : (j + 1) * width] for j in range(3)]
    up = [mlp_in[:, j * width : (j + 1) * width] for j in range(4)]
    parts = [*ins, attn_out, *up, mlp_out, pos, vecs]
    return jnp.concatenate([p.astype(low) for p in parts], axis=0)


def pack(is_student, student, teacher):
    rows, width = student[1].shape

    def padded(parts):
        vecs = parts[5]
        fill = ((0, 16 - vecs.shape[0]), (0, width - vecs.shape[1]))
        return [*parts[:5], jnp.pad(vecs, fill)]

    student, teacher = padded(student), padded(teacher)
    if rows % 16 or student[4].shape[0] % 16:
        return jnp.where(is_student, pack_plain(*student), pack_plain(*teacher))
    total = 12 * rows + student[4].shape[0] + 16
    vmem = pl.BlockSpec(memory_space=pltpu.VMEM)
    return pl.pallas_call(
        pack_kernel,
        out_shape=jax.ShapeDtypeStruct((total, width), low),
        in_specs=[pl.BlockSpec(memory_space=pltpu.SMEM)] + [vmem] * 12,
        out_specs=vmem,
        compiler_params=pltpu.CompilerParams(vmem_limit_bytes=VMEM_BYTES),
        name="pack_weights",
    )(is_student.astype(jnp.int32).reshape(1), *student, *teacher)


def unpack(whole, pos_rows, vec_width):
    devices, _, width = whole.shape
    rows = width // devices
    base = 12 * rows
    owners = LONGEST // pos_rows
    pos = whole[:owners, base : base + pos_rows].reshape(LONGEST, width)
    small = whole[:, base + pos_rows : base + pos_rows + 16, :vec_width]
    vec = small.transpose(1, 0, 2).reshape(16, width).astype(wide)
    if rows % 16:
        blocks = whole[:, : 8 * rows].reshape(devices, 8, rows, width).transpose(1, 0, 2, 3)
        tail = whole[:, 8 * rows : base].reshape(1, 4 * width, width)
        whole = jnp.concatenate([blocks.reshape(1, 8 * width, width), tail], axis=1)
    return whole, pos, vec


def place_kernel(student_ref, slots_ref, mine_ref, theirs_ref, out_ref):
    batches, _, length = slots_ref.shape
    devices, held, width = out_ref.shape
    capacity = held // batches
    for m in range(batches):
        spots = lax.broadcasted_iota(jnp.int32, (devices * capacity, length), 0)
        pick = jnp.where(spots == slots_ref[m], 1.0, 0.0).astype(low)
        rows = jnp.where(student_ref[0] == 1, mine_ref[m], theirs_ref[m])
        placed = dot_plain(pick, rows).astype(low)
        out_ref[:, m * capacity : (m + 1) * capacity, :] = placed.reshape(devices, capacity, width)


def run_place(is_student, slots, mine, theirs, devices, capacity):
    batches, _, width = mine.shape
    vmem = pl.BlockSpec(memory_space=pltpu.VMEM)
    return pl.pallas_call(
        place_kernel,
        out_shape=jax.ShapeDtypeStruct((devices, batches * capacity, width), low),
        in_specs=[pl.BlockSpec(memory_space=pltpu.SMEM)] + [vmem] * 3,
        out_specs=vmem,
        compiler_params=pltpu.CompilerParams(vmem_limit_bytes=VMEM_BYTES),
        name="place_rows",
    )(is_student.astype(jnp.int32).reshape(1), slots, mine, theirs)


def table_kernel(limit, d_low_ref, rows_ref, asked_ref, arrived_ref, out_ref, square_ref):
    step = pl.program_id(0)
    block, width = out_ref.shape
    ids = step * block + lax.broadcasted_iota(jnp.int32, (block, 1), 0)
    wanted = jnp.where(ids == asked_ref[...], 1.0, 0.0).astype(low)
    gradient = dot_plain(wanted, arrived_ref[...]) + dot_plain(d_low_ref[...], rows_ref[...])
    out_ref[...] = gradient
    inside = jnp.where(ids < limit, gradient, 0.0)
    squares = jnp.sum((inside * inside).reshape(block // 8, 8, width), axis=0)

    @pl.when(step == 0)
    def _():
        square_ref[...] = squares

    @pl.when(step > 0)
    def _():
        square_ref[...] += squares


def run_table(d_low, rows, asked, arrived, vocab_rows):
    width = rows.shape[1]
    block = -(-vocab_rows // 96) * 16
    steps = -(-vocab_rows // block)
    count = asked.shape[1]

    def fixed(dims):
        return pl.BlockSpec(dims, lambda k: (0, 0))

    return pl.pallas_call(
        functools.partial(table_kernel, vocab_rows),
        grid=(steps,),
        out_shape=(
            jax.ShapeDtypeStruct((vocab_rows, width), wide),
            jax.ShapeDtypeStruct((8, width), wide),
        ),
        in_specs=[
            pl.BlockSpec((block, rows.shape[0]), lambda k: (k, 0)),
            fixed(rows.shape),
            fixed((1, count)),
            fixed((count, width)),
        ],
        out_specs=(pl.BlockSpec((block, width), lambda k: (k, 0)), fixed((8, width))),
        compiler_params=pltpu.CompilerParams(vmem_limit_bytes=VMEM_BYTES),
        name="table_gradient",
    )(d_low, rows, asked, arrived)


def adam_kernel(count, factor_ref, *refs):
    ins, outs = refs[: 4 * count], refs[4 * count :]
    for k in range(count):
        master, one, two, gradient = [ref[...] for ref in ins[4 * k : 4 * k + 4]]
        results = adam_update(master, one, two, gradient, factor_ref[0])
        for ref, value in zip(outs[3 * k : 3 * k + 3], results):
            ref[...] = value


def run_adam(factor, groups):
    flat = [value for group in groups for value in group]
    vmem = pl.BlockSpec(memory_space=pltpu.VMEM)
    outs = [jax.ShapeDtypeStruct(g[0].shape, wide) for g in groups for _ in range(3)]
    return pl.pallas_call(
        functools.partial(adam_kernel, len(groups)),
        out_shape=tuple(outs),
        in_specs=[pl.BlockSpec(memory_space=pltpu.SMEM)] + [vmem] * len(flat),
        out_specs=(vmem,) * len(outs),
        compiler_params=pltpu.CompilerParams(vmem_limit_bytes=VMEM_BYTES),
        name="small_updates",
    )(factor.reshape(1), *flat)


def shards(
    token_shard,
    token_row,
    doc_ids,
    loss_rows,
    teacher_table,
    teacher_pos,
    teacher_attn_in,
    teacher_attn_out,
    teacher_mlp_in,
    teacher_mlp_out,
    teacher_vecs,
    table,
    pos_table,
    attn_in,
    attn_out,
    mlp_in,
    mlp_out,
    vectors,
    table_m,
    pos_m,
    attn_in_m,
    attn_out_m,
    mlp_in_m,
    mlp_out_m,
    vectors_m,
    table_v,
    pos_v,
    attn_in_v,
    attn_out_v,
    mlp_in_v,
    mlp_out_v,
    vectors_v,
):
    part = lax.axis_index("pair")
    is_student = part == 1
    me = lax.axis_index("dp")
    devices = lax.axis_size("dp")
    vocab_rows, width = table.shape
    hidden = mlp_in.shape[1]
    rows = attn_in.shape[0]
    fold_rows = mlp_out.shape[0]
    vec_count, vec_width = vectors.shape
    pos_count = pos_table.shape[0]
    swap = [(0, 1), (1, 0)]
    to_teacher = [(1, 0)]
    to_student = [(0, 1)]

    owners = token_shard[:, 0, :, 0]
    shard_rows = token_row[:, 0]
    docs = doc_ids[:, 0]
    chosen = loss_rows[:, 0]
    length = owners.shape[1]
    picks = chosen.shape[1]
    capacity = 2 * length // devices
    slot_count = devices * capacity
    total_rows = MB * devices * picks
    indices = jnp.arange(length, dtype=jnp.int32)
    before = indices[None, :] < indices[:, None]
    same_owner = owners[:, :, None] == owners[:, None, :]
    slot = owners * capacity + jnp.sum(same_owner & before, axis=-1, dtype=jnp.int32)
    slots = jnp.arange(slot_count, dtype=jnp.int32)
    filled = slots[None, :, None] == slot[:, None, :]
    request = vocab_rows + jnp.sum(
        jnp.where(filled, shard_rows[:, None, :] - vocab_rows, 0), axis=-1
    )
    request = request.reshape(MB, devices, capacity).transpose(1, 0, 2).reshape(devices, -1)
    is_next = indices[None, None, :] == (chosen + 1)[:, :, None]
    next_ids = jnp.sum(
        jnp.where(is_next, (owners * vocab_rows + shard_rows)[:, None, :], 0), axis=-1
    )
    notes = jnp.broadcast_to(next_ids.reshape(1, -1), (devices, MB * picks))
    notes = jnp.concatenate([request, notes], axis=1)
    arrived_notes = lax.all_to_all(notes, "dp", split_axis=0, concat_axis=0, tiled=True)
    asked = arrived_notes[:, : MB * capacity]
    targets = arrived_notes[:, MB * capacity :].reshape(devices, MB, picks).transpose(1, 0, 2)
    targets = targets.reshape(MB, devices * picks)[part]

    _, flag = lax.optimization_barrier((notes, is_student))
    own_block = pack(
        flag,
        (attn_in, attn_out, mlp_in, mlp_out, pos_table, vectors),
        (
            teacher_attn_in,
            teacher_attn_out,
            teacher_mlp_in,
            teacher_mlp_out,
            teacher_pos,
            teacher_vecs,
        ),
    )
    safe = jnp.minimum(asked, vocab_rows - 1)
    found = lax.cond(
        is_student,
        lambda at: jnp.take(table, at, axis=0).astype(low),
        lambda at: jnp.take(teacher_table, at, axis=0),
        safe,
    )
    whole, found = ring_gather(own_block, found)
    back = lax.all_to_all(found, "dp", split_axis=0, concat_axis=0, tiled=True)
    whole, w_pos, vec = unpack(whole, pos_count, vec_width)

    positions = indices - jnp.sum(docs[:, None, :] < docs[:, :, None], axis=-1, dtype=jnp.int32)
    is_chosen = chosen[:, :, None] == indices[None, None, :]
    doc_c = jnp.sum(jnp.where(is_chosen, docs[:, None, :], 0), axis=-1)
    cols = jnp.stack([slot, positions], axis=-1)
    picked = jnp.stack([chosen, doc_c], axis=-1)
    final, *kept = run_forward(cols, docs[:, None, :], picked, back, w_pos, vec, whole)
    final = final.reshape(MB, picks, width)

    other_final = lax.ppermute(final[1 - part], "pair", swap)
    own_final = final[part]
    both = jnp.stack(
        [
            jnp.where(is_student, other_final, own_final),
            jnp.where(is_student, own_final, other_final),
        ]
    )
    every = lax.all_gather(both.reshape(2 * picks, width), "dp", axis=0)
    every = every.reshape(devices, 2, picks, width).transpose(1, 0, 2, 3)
    every = every.reshape(2, devices * picks, width)
    teacher_rows, student_rows = every[0], every[1]
    table_low = table.astype(low)
    teacher_logits = dot_last(teacher_rows, teacher_table)
    logits = dot_last(student_rows, table_low)
    teacher_max = jnp.max(teacher_logits, axis=1)
    teacher_sum = jnp.sum(jnp.exp(teacher_logits - teacher_max[:, None]), axis=1)
    own_max = jnp.max(logits, axis=1)
    own_sum = jnp.sum(jnp.exp(logits - own_max[:, None]), axis=1)
    stats = to_all(jnp.stack([teacher_max, teacher_sum, own_max, own_sum]), "dp")

    def log_total(maxima, sums):
        big = jnp.max(maxima, axis=0)
        return big + jnp.log(jnp.sum(sums * jnp.exp(maxima - big[None]), axis=0))

    teacher_total = log_total(stats[:, 0], stats[:, 1])[:, None]
    own_total = log_total(stats[:, 2], stats[:, 3])[:, None]
    teacher_log = teacher_logits - teacher_total
    teacher_prob = jnp.exp(teacher_log)
    own_log = logits - own_total
    own_prob = jnp.exp(own_log)
    kl_local = jnp.sum(teacher_prob * (teacher_log - own_log))
    vocab_iota = jnp.arange(vocab_rows, dtype=jnp.int32)
    target_hit = (targets - me * vocab_rows)[:, None] == vocab_iota[None, :]
    d_logits = (2.0 * own_prob - target_hit.astype(wide) - teacher_prob) * (1.0 / total_rows)
    d_low = d_logits.astype(low)
    d_final_parts = dot_plain(d_low, table_low).astype(low).reshape(devices, picks, width)
    d_final_parts = lax.all_to_all(d_final_parts, "dp", split_axis=0, concat_axis=0, tiled=True)
    d_final = jnp.sum(d_final_parts.astype(wide), axis=0)
    d_final_first = lax.ppermute(d_final, "pair", to_student)
    d_final = jnp.concatenate([d_final_first, d_final], axis=0)

    d_embed, g_attn_in, g_vecs, g_pos, lefts, rights = run_backward(
        d_final, cols, picked, vec, kept, whole
    )
    d_embed_there = lax.ppermute(d_embed, "pair", to_teacher)
    out_rows = run_place(is_student, slot[:, None, :], d_embed, d_embed_there, devices, capacity)
    arrived = lax.all_to_all(out_rows, "dp", split_axis=0, concat_axis=0, tiled=True)
    arrived = arrived.reshape(devices * MB * capacity, width)

    g_vecs = jnp.pad(g_vecs.T, ((0, 0), (0, LANES - g_vecs.shape[0])))
    pos_share = LONGEST // devices
    shared = jnp.concatenate([g_attn_in, g_vecs, g_pos.reshape(width, -1)], axis=1).astype(low)
    shared = lax.psum_scatter(shared, "dp", scatter_dimension=0, tiled=True)
    _, d_low_sent, rows_sent, lefts, rights = lax.optimization_barrier(
        (d_embed_there, d_low, student_rows, lefts, rights)
    )
    d_low_other = lax.ppermute(d_low_sent, "pair", swap)
    student_rows_other = lax.ppermute(rows_sent, "pair", swap)

    def column_blocks(values):
        return values.reshape(values.shape[0], devices, -1).transpose(1, 0, 2)

    cuts = (0, hidden, hidden + width, hidden + 2 * width)
    lefts = jnp.concatenate(
        [column_blocks(lefts[:, a:b]) for a, b in zip(cuts, cuts[1:])], axis=2
    )
    lefts = lax.ppermute(lefts, "pair", to_teacher) + jnp.where(is_student, lefts, 0)
    rights = lax.ppermute(rights, "pair", to_teacher) + jnp.where(is_student, rights, 0)
    lefts = lax.all_to_all(lefts, "dp", split_axis=0, concat_axis=0, tiled=True)
    lefts = lefts.reshape(-1, lefts.shape[2])
    rights = lax.all_gather(rights, "dp", axis=0, tiled=True)
    g_mlp_out = dot_first(lefts[:, :fold_rows], rights[:, :width])
    g_mlp_in = dot_first(lefts[:, fold_rows : fold_rows + rows], rights[:, width : width + hidden])
    g_attn_out = dot_first(lefts[:, fold_rows + rows :], rights[:, width + hidden :])

    shared = lax.ppermute(shared, "pair", to_teacher) + jnp.where(is_student, shared, 0)
    shared = shared.astype(wide)
    g_attn_in = shared[:, : 3 * width]
    g_vecs = shared[:, 3 * width : 3 * width + vec_count].T
    pos_near = shared[:, 3 * width + LANES :].reshape(pos_share, width).astype(low)
    pos_near = lax.all_gather(pos_near, "dp", axis=0, tiled=True).astype(wide)
    pos_all = jnp.concatenate([pos_near, jnp.zeros((pos_count, width), wide)], axis=0)
    g_pos = lax.dynamic_slice(
        pos_all, (jnp.minimum(me * pos_count, LONGEST), 0), (pos_count, width)
    )
    smalls = (g_pos, g_attn_in, g_attn_out, g_mlp_in, g_mlp_out, g_vecs)
    squares = jnp.zeros((), wide)
    for gradient in smalls:
        squares = squares + jnp.sum(gradient * gradient)

    d_low_all = jnp.concatenate(
        [jnp.where(is_student, d_low_other, d_low), jnp.where(is_student, d_low, d_low_other)],
        axis=0,
    )
    rows_all = jnp.concatenate(
        [
            jnp.where(is_student, student_rows_other, student_rows),
            jnp.where(is_student, student_rows, student_rows_other),
        ],
        axis=0,
    )
    g_table, table_squares = run_table(
        d_low_all.T, rows_all, asked.reshape(1, -1), arrived, vocab_rows
    )
    squares = squares + jnp.sum(table_squares)
    lane = jnp.arange(LANES, dtype=jnp.int32)[None, :]
    totals = to_all(
        jnp.where(lane == 0, squares, jnp.where(lane == 1, kl_local, 0.0)), ("pair", "dp")
    )
    grad_norm = jnp.sqrt(jnp.sum(totals[devices:, 0, 0]))
    kl_mean = jnp.sum(totals[:, 0, 1]) / total_rows
    factor = jnp.minimum(1.0, clip_limit / (grad_norm + 1e-06))
    masters = (pos_table, attn_in, attn_out, mlp_in, mlp_out, vectors)
    firsts = (pos_m, attn_in_m, attn_out_m, mlp_in_m, mlp_out_m, vectors_m)
    seconds = (pos_v, attn_in_v, attn_out_v, mlp_in_v, mlp_out_v, vectors_v)
    small_out = run_adam(factor, list(zip(masters, firsts, seconds, smalls)))
    table_out = adam_update(table, table_m, table_v, g_table, factor)
    return (*table_out, *small_out, grad_norm, kl_mean)


def solution(mesh):
    return jax.shard_map(
        shards,
        mesh=mesh,
        in_specs=(
            P(None, "dp", None, None),
            P(None, "dp", None),
            P(None, "dp", None),
            P(None, "dp", None),
            P("dp", None),
            P("dp", None),
            P("dp", None),
            P("dp", None),
            P("dp", None),
            P("dp", None),
            P(None, "dp"),
            P("dp", None),
            P("dp", None),
            P("dp", None),
            P("dp", None),
            P("dp", None),
            P("dp", None),
            P(None, "dp"),
            P("dp", None),
            P("dp", None),
            P("dp", None),
            P("dp", None),
            P("dp", None),
            P("dp", None),
            P(None, "dp"),
            P("dp", None),
            P("dp", None),
            P("dp", None),
            P("dp", None),
            P("dp", None),
            P("dp", None),
            P(None, "dp"),
        ),
        out_specs=(
            P("dp", None),
            P("dp", None),
            P("dp", None),
            P("dp", None),
            P("dp", None),
            P("dp", None),
            P("dp", None),
            P("dp", None),
            P("dp", None),
            P("dp", None),
            P("dp", None),
            P("dp", None),
            P("dp", None),
            P("dp", None),
            P("dp", None),
            P("dp", None),
            P("dp", None),
            P("dp", None),
            P(None, "dp"),
            P(None, "dp"),
            P(None, "dp"),
            P(),
            P(),
        ),
        check_vma=False,
    )
```

time: 736 us -> 621 us (0.84)
  matrix products: 128 us -> 25.1 us
  Pallas kernels: 0 us -> 76 us
  local copies, waits for them, and re-layouts: 120 us -> 44 us
  other arithmetic: 91.6 us -> 63.3 us
  waiting for transfers between devices: 198 us -> 214 us
  starting transfers between devices: 83.7 us -> 93.1 us
    pallas_call x0 -> x6, Pallas kernels: none -> 76 us  [the longest x1 29 us: run_backward(): pl.pallas_call(backward_kernel, out_shape=(shape((batches, length, width)...]
    dot_general x15 -> x3, matrix products: 62.3 us -> 9.81 us  [dot_first(): lax.dot_general(left_side, right_side, (((0,), (0,)), ((), ())), preferre...]
    dot_general x18 -> x1, matrix products: 33.8 us -> 5.93 us  [dot_plain(): return jnp.dot(left_side, right_side, preferred_element_type=wide)]
    all_to_all x1, starting transfers between devices: 6 us -> 26.5 us  [shards(): lefts = lax.all_to_all(lefts, 'dp', split_axis=0, concat_axis=0, tiled=True)]
    unnamed x336 -> x41, local copies, waits for them, and re-layouts: 29.9 us -> 9.6 us
    dot_general x11 -> x2, matrix products: 28.4 us -> 9.35 us  [dot_last(): lax.dot_general(left_side, right_side, (((1,), (1,)), ((), ())), preferre...]
    reshape x12 -> x0, local copies, waits for them, and re-layouts: 16.3 us -> none  [the longest x1 9.96 us: unpack(): folded.reshape(devices, rows, folds, width).transpose(0, 2, 1, 3)]
    all_to_all x5 -> x3, starting transfers between devices: 30.7 us -> 14.9 us  [the longest x1 6.38 us: shards(): lax.all_to_all(notes, 'dp', split_axis=0, concat_axis=0, tiled=True)]
  transfers between devices with their start and end apart: 35 -> 32, of which waited for: 15 -> 17; matrix products, arithmetic and copies ran while one was open for 19% -> 9% of each run, Pallas kernels for 0% -> 4%
where the time goes in v2:
time: 621 us; the launch traced here: 613 us
  waiting for transfers between devices  214 us (34%)
  starting transfers between devices  93.1 us (15%)
  Pallas kernels  76 us (12%)
  other arithmetic  63.3 us (10%)
  blocking collectives  62.6 us (10%)
  local copies, waits for them, and re-layouts  44 us (7%)
  between operations  35.3 us (6%)
  matrix products  25.1 us (4%)
    ppermute x3, waiting for transfers between devices, ring_gather(): ahead = lax.ppermute(ahead, 'dp', onward)  69.5 us
    ppermute x1, waiting for transfers between devices, shards(): lax.ppermute(lefts, 'pair', to_teacher) + jnp.where(is_student, lefts, 0)  40.2 us
    ppermute x1, waiting for transfers between devices, shards(): d_embed_there = lax.ppermute(d_embed, 'pair', to_teacher)  36.1 us
    pallas_call x1, Pallas kernels, run_backward(): pl.pallas_call(backward_kernel, out_shape=(shape((batches, length, width)...  29 us
    all_to_all x1, starting transfers between devices, shards(): lefts = lax.all_to_all(lefts, 'dp', split_axis=0, concat_axis=0, tiled=True)  26.5 us
    all_gather x1, blocking collectives, shards(): pos_near = lax.all_gather(pos_near, 'dp', axis=0, tiled=True).astype(wide)  24.8 us
    sub x1, other arithmetic, adam_update(): master - learn_rate * (fixed_one / (jnp.sqrt(fixed_two) + adam_eps) + dec...  24.4 us
    ppermute x3, starting transfers between devices, ring_gather(): ahead = lax.ppermute(ahead, 'dp', onward)  23.3 us
  transfers between devices with their start and end apart: 32, of which 17 were waited for; matrix products, arithmetic and copies ran while one was open for 9% of the time, Pallas kernels for 4%

profile of v2, /device:TPU:0, one launch (start us, length us, event | category | flops | bytes accessed | tf_op | source)
XLA Modules:
  0.0 613.1 jit_solution(4237658741737906963)
XLA Ops:
  21.5 6.4 %all-to-all-start = ((s32[16,1,160]{2,1,0:T(1,128)}), s32[16,1,160]{2,1,0:T(1,128)S(1)}, u32[]{:S(2)}, u32[]{:S(2)}) async-start(s32[16,1,160]{2,1,0:T(1,128)} %copy.160), calls=%async_computation | async-start | bytes 32768 | tf_op jit(solution)/shard_map/all_to_all | solution.py:717
  27.9 13.9 %all-to-all-done = s32[16,1,160]{2,1,0:T(1,128)S(1)} async-done(((s32[16,1,160]{2,1,0:T(1,128)}), s32[16,1,160]{2,1,0:T(1,128)S(1)}, u32[]{:S(2)}, u32[]{:S(2)}) %all-to-all-start) | async-done | bytes 10272 | tf_op jit(solution)/shard_map/all_to_all | solution.py:717
  42.4 13.4 %conditional.1 = (bf16[16,128,768]{2,1,0:T(8,128)(2,1)}) conditional(s32[]{:T(128)} %convert_element_type.59, (s32[16,128]{1,0:T(8,128)S(1)}, bf16[3144,768]{1,0:T(8,128)(2,1)}) %tuple.18, (s32[16,128]{1,0:T(8,128)S(1)}, f32[3144,768]{1,0:T(8,128)}) %tuple.19), branch_computations={%region_5.6_spmd, %region_6.7_spmd} | conditional | flops 1593344 | bytes 12619784 | solution.py:736
  42.4 11.4 %gather_fusion = bf16[2048,768]{1,0:T(8,128)(2,1)S(1)} fusion(bf16[3144,768]{1,0:T(8,128)(2,1)} %get-tuple-element.12, s32[2048]{0:T(1024)S(1)} %bitcast_clamp_fusion), kind=kCustom, calls=%fused_computation | custom fusion | bytes 6299648 | tf_op jit(solution)/shard_map/cond/branch_0_fun/jit(_take)/gather | solution.py:739
  82.0 51.2 %collective-permute-done.5 = bf16[656,768]{1,0:T(8,128)(2,1)} collective-permute-done((bf16[656,768]{1,0:T(8,128)(2,1)}, bf16[656,768]{1,0:T(8,128)(2,1)}, u32[]{:S(2)}, u32[]{:S(2)}) %collective-permute-start.5) | collective-permute-done | bytes 1007648 | tf_op jit(solution)/shard_map/ppermute | solution.py:100
  133.2 18.5 %collective-permute-start.9 = (bf16[656,768]{1,0:T(8,128)(2,1)}, bf16[656,768]{1,0:T(8,128)(2,1)S(1)}, u32[]{:S(2)}, u32[]{:S(2)}) collective-permute-start(bf16[656,768]{1,0:T(8,128)(2,1)} %collective-permute-done.5), channel_id=1, source_target_pairs={{0,4},{1,5},{4,8},{5,9},{8,12},{9,13},{12,14},{13,15},{14,10},{15,... | collective-permute-start | bytes 3022856 | tf_op jit(solution)/shard_map/ppermute | solution.py:100
  155.9 18.3 %collective-permute-done.9 = bf16[656,768]{1,0:T(8,128)(2,1)S(1)} collective-permute-done((bf16[656,768]{1,0:T(8,128)(2,1)}, bf16[656,768]{1,0:T(8,128)(2,1)S(1)}, u32[]{:S(2)}, u32[]{:S(2)}) %collective-permute-start.9) | collective-permute-done | bytes 1007648 | tf_op jit(solution)/shard_map/ppermute | solution.py:100
  180.7 8.9 %collective-permute-done.13 = bf16[320,768]{1,0:T(8,128)(2,1)S(1)} collective-permute-done((bf16[320,768]{1,0:T(8,128)(2,1)S(1)}, bf16[320,768]{1,0:T(8,128)(2,1)S(1)}, u32[]{:S(2)}, u32[]{:S(2)}) %collective-permute-start.13) | collective-permute-done | bytes 491552 | tf_op jit(solution)/shard_map/ppermute | solution.py:107
  194.7 4.8 copy-done
  202.0 15.2 %layer_forward.1 = (bf16[32,768]{1,0:T(8,128)(2,1)}, f32[2,512,768]{2,1,0:T(8,128)}, bf16[2,512,1536]{2,1,0:T(8,128)(2,1)}, bf16[32,768]{1,0:T(8,128)(2,1)}, f32...) custom-call(s32[2,512,2]{2,1,0:T(8,128)} %copy.162.cols_ref, ...), custom_call_target="tpu_custom_call" | custom-call | tf_op jit(solution)/shard_map/layer_forward/pallas_call | solution.py:295
  223.0 23.0 %all_gather.9 = bf16[16,32,768]{2,1,0:T(8,128)(2,1)S(1)} all-gather(bf16[1,32,768]{2,1,0:T(8,128)(2,1)S(1)} %bitcast.187), channel_id=1, replica_groups=mesh['pair'=2,'dp'=16] {'dp'}, dimensions={0}, use_global_device_ids=true | all-gather | bytes 835584 | tf_op jit(solution)/shard_map/all_gather | solution.py:762
  250.1 5.3 fusion.40
  262.5 6.6 %all-to-all-done.2 = f32[16,4,256]{2,1,0:T(4,128)S(1)} async-done(((f32[16,4,256]{2,1,0:T(4,128)}), f32[16,4,256]{2,1,0:T(4,128)S(1)}, u32[]{:S(2)}, u32[]{:S(2)}) %all-to-all-start.2) | async-done | bytes 65568 | tf_op jit(solution)/shard_map/all_to_all | solution.py:128
  269.3 4.2 multiply_reduce_fusion
  273.5 5.9 fusion.11
  279.5 14.8 %all_to_all.42 = bf16[16,16,768]{2,1,0:T(8,128)(2,1)S(1)} all-to-all(bf16[16,16,768]{2,1,0:T(8,128)(2,1)S(1)} %bitcast.177), channel_id=1, replica_groups=mesh['pair'=2,'dp'=16] {'dp'}, dimensions={0} | all-to-all | bytes 786432 | tf_op jit(solution)/shard_map/all_to_all | solution.py:791
  294.3 4.1 collective-permute-start.17
  300.7 29.0 %layer_backward.1 = (bf16[2,512,768]{2,1,0:T(8,128)(2,1)}, f32[768,2304]{1,0:T(8,128)}, f32[16,768]{1,0:T(8,128)}, f32[256,768]{1,0:T(8,128)}, bf16[32,4608]{1,0:T(8,128)(2,1)}, /*index=5*/bf16[32,4608]{1,0:T(8,128)(2,1)}) custom-call(f32[32,768]{1,0:T(8,128)} %pad_maximum_fusion.2.d_final_ref, s32[2,512,2]{2,1,0:T(8,128)} %copy.162.cols_ref, ...), custom_call_target="tpu_custom_call" | custom-call | tf_op jit(solution)/shard_map/layer_backward/pallas_call | solution.py:453
  338.9 36.1 %collective-permute-done.18.theirs_ref = bf16[2,512,768]{2,1,0:T(8,128)(2,1)S(1)} collective-permute-done((bf16[2,512,768]{2,1,0:T(8,128)(2,1)S(1)}, bf16[2,512,768]{2,1,0:T(8,128)(2,1)S(1)}, u32[]{:S(2)}, u32[]{:S(2)}) %collective-permute-start.18) | collective-permute-done | bytes 1572896 | tf_op jit(solution)/shard_map/ppermute | solution.py:799
  376.3 8.2 %collective-permute-done.23 = bf16[32,4608]{1,0:T(8,128)(2,1)S(1)} collective-permute-done((bf16[32,4608]{1,0:T(8,128)(2,1)}, bf16[32,4608]{1,0:T(8,128)(2,1)S(1)}, u32[]{:S(2)}, u32[]{:S(2)}) %collective-permute-start.23) | collective-permute-done | bytes 294944 | tf_op jit(solution)/shard_map/ppermute | solution.py:822
  385.3 5.4 place_rows.1
  390.7 4.6 all-to-all-start.4
  401.8 40.2 %collective-permute-done.22 = bf16[16,32,288]{2,1,0:T(8,128)(2,1)} collective-permute-done((bf16[16,32,288]{2,1,0:T(8,128)(2,1)S(1)}, bf16[16,32,288]{2,1,0:T(8,128)(2,1)}, u32[]{:S(2)}, u32[]{:S(2)}) %collective-permute-start.22) | collective-permute-done | bytes 294944 | tf_op jit(solution)/shard_map/ppermute | solution.py:821
  444.0 5.6 collective-permute-done.20
  458.5 4.6 collective-permute-done.21
  463.8 7.3 %all-to-all-done.4 = bf16[16,128,768]{2,1,0:T(8,128)(2,1)} async-done(((bf16[16,128,768]{2,1,0:T(8,128)(2,1)}), bf16[16,128,768]{2,1,0:T(8,128)(2,1)}, u32[]{:S(2)}, u32[]{:S(2)}) %all-to-all-start.4) | async-done | bytes 3145760 | tf_op jit(solution)/shard_map/all_to_all | solution.py:801
  471.2 26.5 %all-to-all-start.5 = ((bf16[16,32,288]{2,1,0:T(8,128)(2,1)}), bf16[16,32,288]{2,1,0:T(8,128)(2,1)S(1)}, u32[]{:S(2)}, u32[]{:S(2)}) async-start(bf16[16,32,288]{2,1,0:T(8,128)(2,1)} %select_add_fusion.1), calls=%async_computation.5 | async-start | bytes 786432 | tf_op jit(solution)/shard_map/all_to_all | solution.py:823
  497.7 24.8 %all_gather.10 = bf16[256,768]{1,0:T(8,128)(2,1)S(1)} all-gather(bf16[16,768]{1,0:T(8,128)(2,1)S(1)} %convert_element_type.68), channel_id=1, replica_groups=mesh['pair'=2,'dp'=16] {'dp'}, dimensions={0}, use_global_device_ids=true | all-gather | bytes 417792 | tf_op jit(solution)/shard_map/all_gather | solution.py:835
  526.5 17.3 %table_gradient.1 = (f32[3144,768]{1,0:T(8,128)}, f32[8,768]{1,0:T(8,128)}) custom-call(bf16[3144,512]{1,0:T(8,128)(2,1)} %maximum_bitcast_fusion.d_low_ref, bf16[512,768]{1,0:T(8,128)(2,1)} %pad_maximum_fusion.rows_ref, s32[1,2048]{1,0:T(1,128)} %bitcast.197, bf16[2048,768]{1,0:T(8,128)(2,1)} %bitcast.65.arrived_ref), custom_call_target="tpu_custom_call" | custom-call | tf_op jit(solution)/shard_map/table_gradient/pallas_call | solution.py:602
  564.9 5.2 all-to-all-done.6
  572.8 24.4 %multiply_subtract_fusion = (f32[3144,768]{1,0:T(8,128)}, f32[3144,768]{1,0:T(8,128)}, f32[3144,768]{1,0:T(8,128)}) fusion(f32[3144,768]{1,0:T(8,128)} %param.54, f32[3144,768]{1,0:T(8,128)} %get-tuple-element.99, f32[]{:T(128)} %min_shard_map.3, f32[3144,768]{1,0:T(8,128)} %param.61, f32[3144,768]{1,0:T(8,128)} %param.68), kind=kLoop, calls=%fused_computation.14 | loop fusion | flops 38633472 | bytes 67608576 | tf_op jit(solution)/shard_map/sub | solution.py:119
  597.2 6.3 %small_updates.1 = (f32[64,768]{1,0:T(8,128)}, f32[64,768]{1,0:T(8,128)}, f32[64,768]{1,0:T(8,128)}, f32[48,2304]{1,0:T(8,128)}, f32[48,2304]{1,0:T(8,128)}, /*i...) custom-call(f32[1]{0:T(128)} %bitcast.72.factor_ref, ...), custom_call_target="tpu_custom_call" | custom-call | tf_op jit(solution)/shard_map/small_updates/pallas_call | solution.py:634
  (206 shorter events, 119.6 us)
Async XLA Ops:
  12.6 43.2 %collective-permute-start = (bf16[656,768]{1,0:T(8,128)(2,1)}, bf16[656,768]{1,0:T(8,128)(2,1)}, u32[]{:S(2)}, u32[]{:S(2)}) collective-permute-start(bf16[656,768]{1,0:T(8,128)(2,1)} %pack_weights.1), channel_id=1, source_target_pairs={{0,4},{1,5},{4,8},{5,9},{8,12},{9,13},{12,14},{13,15},{14,10},{15,... | collective-permute-start | bytes 3022856 | tf_op jit(solution)/shard_map/ppermute | solution.py:100
  15.7 40.1 %collective-permute-start.1 = (bf16[656,768]{1,0:T(8,128)(2,1)}, bf16[656,768]{1,0:T(8,128)(2,1)}, u32[]{:S(2)}, u32[]{:S(2)}) collective-permute-start(bf16[656,768]{1,0:T(8,128)(2,1)} %pack_weights.1), channel_id=1, source_target_pairs={{4,0},{5,1},{8,4},{9,5},{12,8},{13,9},{14,12},{15,13},{10,14},{11,... | collective-permute-start | bytes 3022856 | tf_op jit(solution)/shard_map/ppermute | solution.py:101
  21.5 20.3 %all-to-all-start = ((s32[16,1,160]{2,1,0:T(1,128)}), s32[16,1,160]{2,1,0:T(1,128)S(1)}, u32[]{:S(2)}, u32[]{:S(2)}) async-start(s32[16,1,160]{2,1,0:T(1,128)} %copy.160), calls=%async_computation | async-start | bytes 32768 | tf_op jit(solution)/shard_map/all_to_all | solution.py:717
  55.8 144.5 %all-to-all-start.1 = ((bf16[16,128,768]{2,1,0:T(8,128)(2,1)}), bf16[16,128,768]{2,1,0:T(8,128)(2,1)S(1)}, u32[]{:S(2)}, u32[]{:S(2)}) async-start(bf16[16,128,768]{2,1,0:T(8,128)(2,1)} %get-tuple-element.174), calls=%async_computation.1 | async-start | bytes 6291456 | tf_op jit(solution)/shard_map/all_to_all | solution.py:743
  59.7 19.7 %collective-permute-start.2 = (bf16[656,768]{1,0:T(8,128)(2,1)}, bf16[656,768]{1,0:T(8,128)(2,1)}, u32[]{:S(2)}, u32[]{:S(2)}) collective-permute-start(bf16[656,768]{1,0:T(8,128)(2,1)} %pack_weights.1), channel_id=1, source_target_pairs={{0,1},{1,0},{2,3},{3,2},{4,5},{5,4},{6,7},{7,6},{8,9},{9,8},{10,11... | collective-permute-start | bytes 3022856 | tf_op jit(solution)/shard_map/ppermute | solution.py:94
  74.6 77.3 %collective-permute-start.3 = (bf16[656,768]{1,0:T(8,128)(2,1)}, bf16[656,768]{1,0:T(8,128)(2,1)}, u32[]{:S(2)}, u32[]{:S(2)}) collective-permute-start(bf16[656,768]{1,0:T(8,128)(2,1)} %collective-permute-done), channel_id=1, source_target_pairs={{0,1},{1,0},{2,3},{3,2},{4,5},{5,4},{6,7},{7,6},{8,9},{9,8},{10,11... | collective-permute-start | bytes 3022856 | tf_op jit(solution)/shard_map/ppermute | solution.py:94
  74.9 58.3 %collective-permute-start.5 = (bf16[656,768]{1,0:T(8,128)(2,1)}, bf16[656,768]{1,0:T(8,128)(2,1)}, u32[]{:S(2)}, u32[]{:S(2)}) collective-permute-start(bf16[656,768]{1,0:T(8,128)(2,1)} %collective-permute-done), channel_id=1, source_target_pairs={{0,4},{1,5},{4,8},{5,9},{8,12},{9,13},{12,14},{13,15},{14,10},{15,... | collective-permute-start | bytes 3022856 | tf_op jit(solution)/shard_map/ppermute | solution.py:100
  76.7 75.0 %collective-permute-start.7 = (bf16[656,768]{1,0:T(8,128)(2,1)}, bf16[656,768]{1,0:T(8,128)(2,1)}, u32[]{:S(2)}, u32[]{:S(2)}) collective-permute-start(bf16[656,768]{1,0:T(8,128)(2,1)} %collective-permute-done.1), channel_id=1, source_target_pairs={{4,0},{5,1},{8,4},{9,5},{12,8},{13,9},{14,12},{15,13},{10,14},{11,... | collective-permute-start | bytes 3022856 | tf_op jit(solution)/shard_map/ppermute | solution.py:101
  79.3 75.2 %collective-permute-start.4 = (bf16[656,768]{1,0:T(8,128)(2,1)}, bf16[656,768]{1,0:T(8,128)(2,1)S(1)}, u32[]{:S(2)}, u32[]{:S(2)}) collective-permute-start(bf16[656,768]{1,0:T(8,128)(2,1)} %collective-permute-done.1), channel_id=1, source_target_pairs={{0,1},{1,0},{2,3},{3,2},{4,5},{5,4},{6,7},{7,6},{8,9},{9,8},{10,11... | collective-permute-start | bytes 3022856 | tf_op jit(solution)/shard_map/ppermute | solution.py:94
  133.2 45.5 %collective-permute-start.6 = (bf16[656,768]{1,0:T(8,128)(2,1)}, bf16[656,768]{1,0:T(8,128)(2,1)S(1)}, u32[]{:S(2)}, u32[]{:S(2)}) collective-permute-start(bf16[656,768]{1,0:T(8,128)(2,1)} %collective-permute-done.5), channel_id=1, source_target_pairs={{0,1},{1,0},{2,3},{3,2},{4,5},{5,4},{6,7},{7,6},{8,9},{9,8},{10,11... | collective-permute-start | bytes 3022856 | tf_op jit(solution)/shard_map/ppermute | solution.py:94
  133.2 41.0 %collective-permute-start.9 = (bf16[656,768]{1,0:T(8,128)(2,1)}, bf16[656,768]{1,0:T(8,128)(2,1)S(1)}, u32[]{:S(2)}, u32[]{:S(2)}) collective-permute-start(bf16[656,768]{1,0:T(8,128)(2,1)} %collective-permute-done.5), channel_id=1, source_target_pairs={{0,4},{1,5},{4,8},{5,9},{8,12},{9,13},{12,14},{13,15},{14,10},{15,... | collective-permute-start | bytes 3022856 | tf_op jit(solution)/shard_map/ppermute | solution.py:100
  151.7 28.9 %collective-permute-start.8 = (bf16[656,768]{1,0:T(8,128)(2,1)}, bf16[656,768]{1,0:T(8,128)(2,1)S(1)}, u32[]{:S(2)}, u32[]{:S(2)}) collective-permute-start(bf16[656,768]{1,0:T(8,128)(2,1)} %collective-permute-done.7), channel_id=1, source_target_pairs={{0,1},{1,0},{2,3},{3,2},{4,5},{5,4},{6,7},{7,6},{8,9},{9,8},{10,11... | collective-permute-start | bytes 3022856 | tf_op jit(solution)/shard_map/ppermute | solution.py:94
  151.9 25.4 %collective-permute-start.11 = (bf16[656,768]{1,0:T(8,128)(2,1)}, bf16[656,768]{1,0:T(8,128)(2,1)S(1)}, u32[]{:S(2)}, u32[]{:S(2)}) collective-permute-start(bf16[656,768]{1,0:T(8,128)(2,1)} %collective-permute-done.7), channel_id=1, source_target_pairs={{4,0},{5,1},{8,4},{9,5},{12,8},{13,9},{14,12},{15,13},{10,14},{11,... | collective-permute-start | bytes 3022856 | tf_op jit(solution)/shard_map/ppermute | solution.py:101
  174.2 15.4 %collective-permute-start.13 = (bf16[320,768]{1,0:T(8,128)(2,1)S(1)}, bf16[320,768]{1,0:T(8,128)(2,1)S(1)}, u32[]{:S(2)}, u32[]{:S(2)}) collective-permute-start(bf16[320,768]{1,0:T(8,128)(2,1)S(1)} %slice.112), channel_id=1, source_target_pairs={{0,4},{1,5},{4,8},{5,9},{8,12},{9,13},{12,14},{13,15},{14,10},{15,... | collective-permute-start | bytes 1474568 | tf_op jit(solution)/shard_map/ppermute | solution.py:107
  177.4 13.7 %collective-permute-start.14 = (bf16[336,768]{1,0:T(8,128)(2,1)S(1)}, bf16[336,768]{1,0:T(8,128)(2,1)S(1)}, u32[]{:S(2)}, u32[]{:S(2)}) collective-permute-start(bf16[336,768]{1,0:T(8,128)(2,1)S(1)} %slice.113), channel_id=1, source_target_pairs={{4,0},{5,1},{8,4},{9,5},{12,8},{13,9},{14,12},{15,13},{10,14},{11,... | collective-permute-start | bytes 1548296 | tf_op jit(solution)/shard_map/ppermute | solution.py:108
  178.6 12.6 %collective-permute-start.10 = (bf16[656,768]{1,0:T(8,128)(2,1)S(1)}, bf16[656,768]{1,0:T(8,128)(2,1)S(1)}, u32[]{:S(2)}, u32[]{:S(2)}) collective-permute-start(bf16[656,768]{1,0:T(8,128)(2,1)S(1)} %collective-permute-done.9), channel_id=1, source_target_pairs={{0,1},{1,0},{2,3},{3,2},{4,5},{5,4},{6,7},{7,6},{8,9},{9,8},{10,11... | collective-permute-start | bytes 3022856 | tf_op jit(solution)/shard_map/ppermute | solution.py:94
  178.6 12.8 %collective-permute-start.12 = (bf16[656,768]{1,0:T(8,128)(2,1)S(1)}, bf16[656,768]{1,0:T(8,128)(2,1)S(1)}, u32[]{:S(2)}, u32[]{:S(2)}) collective-permute-start(bf16[656,768]{1,0:T(8,128)(2,1)S(1)} %collective-permute-done.11), channel_id=1, source_target_pairs={{0,1},{1,0},{2,3},{3,2},{4,5},{5,4},{6,7},{7,6},{8,9},{9,8},{10,11... | collective-permute-start | bytes 3022856 | tf_op jit(solution)/shard_map/ppermute | solution.py:94
  191.1 2.7 collective-permute-start.15
  218.0 4.2 collective-permute-start.16
  258.8 10.4 %all-to-all-start.2 = ((f32[16,4,256]{2,1,0:T(4,128)}), f32[16,4,256]{2,1,0:T(4,128)S(1)}, u32[]{:S(2)}, u32[]{:S(2)}) async-start(f32[16,4,256]{2,1,0:T(4,128)} %broadcast_in_dim.199), calls=%async_computation.2 | async-start | bytes 131072 | tf_op jit(solution)/shard_map/all_to_all | solution.py:128
  262.3 191.1 %reduce-scatter.4.cloned.1.call-start = ((), (), s32[]{:S(2)}) async-start(), calls=%async_computation.9 | async-start | bytes 4386816 | tf_op jit(solution)/shard_map/reduce_scatter | solution.py:807
  294.3 5.7 collective-permute-start.17
  337.5 207.6 %all-gather.2.cloned.1.call-start = ((), (), s32[]{:S(2)}) async-start(), calls=%async_computation.8 | async-start | bytes 5013504 | tf_op jit(solution)/shard_map/all_gather | solution.py:825
  337.6 37.4 %collective-permute-start.18 = (bf16[2,512,768]{2,1,0:T(8,128)(2,1)S(1)}, bf16[2,512,768]{2,1,0:T(8,128)(2,1)S(1)}, u32[]{:S(2)}, u32[]{:S(2)}) collective-permute-start(bf16[2,512,768]{2,1,0:T(8,128)(2,1)S(1)} %copy-done.8), channel_id=1, source_target_pairs={{16,0},{17,1},{18,2},{19,3},{20,4},{21,5},{22,6},{23,7},{24,8},{25... | collective-permute-start | bytes 4718600 | tf_op jit(solution)/shard_map/ppermute | solution.py:799
  375.1 9.4 %collective-permute-start.23 = (bf16[32,4608]{1,0:T(8,128)(2,1)}, bf16[32,4608]{1,0:T(8,128)(2,1)S(1)}, u32[]{:S(2)}, u32[]{:S(2)}) collective-permute-start(bf16[32,4608]{1,0:T(8,128)(2,1)} %get-tuple-element.104), channel_id=1, source_target_pairs={{16,0},{17,1},{18,2},{19,3},{20,4},{21,5},{22,6},{23,7},{24,8},{25... | collective-permute-start | bytes 884744 | tf_op jit(solution)/shard_map/ppermute | solution.py:822
  390.7 80.5 %all-to-all-start.4 = ((bf16[16,128,768]{2,1,0:T(8,128)(2,1)}), bf16[16,128,768]{2,1,0:T(8,128)(2,1)}, u32[]{:S(2)}, u32[]{:S(2)}) async-start(bf16[16,128,768]{2,1,0:T(8,128)(2,1)} %place_rows.1), calls=%async_computation.4 | async-start | bytes 6291456 | tf_op jit(solution)/shard_map/all_to_all | solution.py:801
  395.3 55.2 %collective-permute-start.19 = (bf16[256,3144]{0,1:T(8,128)(2,1)S(1)}, bf16[256,3144]{0,1:T(8,128)(2,1)}, u32[]{:S(2)}, u32[]{:S(2)}) collective-permute-start(bf16[256,3144]{0,1:T(8,128)(2,1)S(1)} %copy-done.3), channel_id=1, source_target_pairs={{0,16},{16,0},{1,17},{17,1},{2,18},{18,2},{3,19},{19,3},{4,20},{20... | collective-permute-start | bytes 4829192 | tf_op jit(solution)/shard_map/ppermute | solution.py:811
  397.1 44.9 %collective-permute-start.22 = (bf16[16,32,288]{2,1,0:T(8,128)(2,1)S(1)}, bf16[16,32,288]{2,1,0:T(8,128)(2,1)}, u32[]{:S(2)}, u32[]{:S(2)}) collective-permute-start(bf16[16,32,288]{2,1,0:T(8,128)(2,1)S(1)} %pad_maximum_fusion.1), channel_id=1, source_target_pairs={{16,0},{17,1},{18,2},{19,3},{20,4},{21,5},{22,6},{23,7},{24,8},{25... | collective-permute-start | bytes 884744 | tf_op jit(solution)/shard_map/ppermute | solution.py:821
  398.4 51.2 %collective-permute-start.20 = (bf16[256,768]{1,0:T(8,128)(2,1)S(1)}, bf16[256,768]{1,0:T(8,128)(2,1)S(1)}, u32[]{:S(2)}, u32[]{:S(2)}) collective-permute-start(bf16[256,768]{1,0:T(8,128)(2,1)S(1)} %bitcast.173), channel_id=1, source_target_pairs={{0,16},{16,0},{1,17},{17,1},{2,18},{18,2},{3,19},{19,3},{4,20},{20... | collective-permute-start | bytes 1179656 | tf_op jit(solution)/shard_map/ppermute | solution.py:812
  453.4 9.8 %collective-permute-start.21 = (bf16[48,2688]{1,0:T(8,128)(2,1)}, bf16[48,2688]{1,0:T(8,128)(2,1)S(1)}, u32[]{:S(2)}, u32[]{:S(2)}) collective-permute-start(bf16[48,2688]{1,0:T(8,128)(2,1)} %reduce-scatter.4.cloned.1.call-done), channel_id=1, source_target_pairs={{16,0},{17,1},{18,2},{19,3},{20,4},{21,5},{22,6},{23,7},{24,8},{25... | collective-permute-start | bytes 774152 | tf_op jit(solution)/shard_map/ppermute | solution.py:830
  471.2 74.0 %all-to-all-start.5 = ((bf16[16,32,288]{2,1,0:T(8,128)(2,1)}), bf16[16,32,288]{2,1,0:T(8,128)(2,1)S(1)}, u32[]{:S(2)}, u32[]{:S(2)}) async-start(bf16[16,32,288]{2,1,0:T(8,128)(2,1)} %select_add_fusion.1), calls=%async_computation.5 | async-start | bytes 786432 | tf_op jit(solution)/shard_map/all_to_all | solution.py:823
  559.5 10.6 %all-to-all-start.6 = ((f32[32,1,128]{2,1,0:T(1,128)}), f32[32,1,128]{2,1,0:T(1,128)S(1)}, u32[]{:S(2)}, u32[]{:S(2)}) async-start(f32[32,1,128]{2,1,0:T(1,128)} %broadcast_in_dim.206), calls=%async_computation.6 | async-start | bytes 32768 | tf_op jit(solution)/shard_map/all_to_all | solution.py:128
  (17 other events, 132.4 us)
Sparse Core Ops, SparseCore 0:
  337.7 89.6 reduce-scatter.3
  430.2 73.6 all-gather.1

commit v3 on v2

v3 whole, which is shorter than its diff:
```python
import functools

import jax
import jax.numpy as jnp
from jax import lax
from jax.experimental import pallas as pl
from jax.experimental.pallas import tpu as pltpu
from jax.sharding import PartitionSpec as P

H = 12
MB = 2
STEP = 10
LONGEST = 256
LANES = 128
MEBI = 1024 * 1024


learn_rate = 0.25
beta_one = 0.9
beta_two = 0.999
adam_eps = 1e-08
decay_rate = 0.1
clip_limit = 0.02
norm_eps = 1e-05
neg_big = -1000000000.0
gelu_scale = 0.7978845608028654
gelu_cube = 0.044715

low = jnp.bfloat16
wide = jnp.float32


def layer_norm(values, norm_gain, norm_shift):
    center = jnp.mean(values, axis=-1, keepdims=True)
    offsets = values - center
    spread = jnp.mean(offsets * offsets, axis=-1, keepdims=True)
    return offsets * lax.rsqrt(spread + norm_eps) * norm_gain + norm_shift


def gelu_tanh(values):
    return jax.nn.gelu(values, approximate=True)


def dot_plain(left_side, right_side):
    return jnp.dot(left_side, right_side, preferred_element_type=wide)


def dot_first(left_side, right_side):
    return lax.dot_general(
        left_side, right_side, (((0,), (0,)), ((), ())), preferred_element_type=wide
    )


def dot_last(left_side, right_side):
    return lax.dot_general(
        left_side, right_side, (((1,), (1,)), ((), ())), preferred_element_type=wide
    )


def tied(*values):
    return lax.optimization_barrier(values)


def kernel_cost(micros):
    return pl.CostEstimate(
        flops=int(micros * 1e8), transcendentals=0, bytes_accessed=int(micros * 3.4e6)
    )


def kernel_limit(mebi):
    return pltpu.CompilerParams(vmem_limit_bytes=mebi * MEBI)


distances = (0, -1, 1, -2, 2, -3, 3, 4)


def ring_gather(block, after, over, share):
    devices = lax.axis_size("dp")
    chips = devices // 2
    ring = [*range(0, chips, 2), *range(chips - 1, 0, -2)]
    onward = [(2 * ring[k] + c, 2 * ring[(k + 1) % chips] + c) for k in range(chips) for c in (0, 1)]
    backward = [(there, here) for here, there in onward]
    across = [(d, d ^ 1) for d in range(devices)]
    half_rows = block.shape[0] // 32 * 16
    whole = jnp.zeros((devices,) + block.shape, block.dtype)

    def keep(whole, piece, distance):
        k = 2 * distances.index(distance)
        partner = lax.ppermute(piece, "dp", across)
        whole = lax.dynamic_update_slice(whole, piece[None], (piece_slot(k, devices), 0, 0))
        return lax.dynamic_update_slice(whole, partner[None], (piece_slot(k + 1, devices), 0, 0))

    ahead, behind = block, block
    sent = [over(block[:share])]
    for distance in range(1, chips // 2):
        ahead = lax.ppermute(ahead, "dp", onward)
        behind = lax.ppermute(behind, "dp", backward)
        if distance == 1:
            ahead, behind = after(ahead, behind)
            whole = keep(whole, block, 0)
        else:
            ahead, behind, *sent = tied(ahead, behind, *sent)
        if distance < 3:
            sent += [over(ahead[:share]), over(behind[:share])]
        whole = keep(whole, ahead, -distance)
        whole = keep(whole, behind, distance)
    first = lax.ppermute(ahead[:half_rows], "dp", onward)
    second = lax.ppermute(behind[half_rows:], "dp", backward)
    last = jnp.concatenate([first, second], axis=0)
    late = jnp.stack([ahead[:share], behind[:share], last[:share]])
    return keep(whole, last, chips // 2), jnp.stack(sent), late


def piece_slot(k, count):
    if count == 1:
        return 0
    me = lax.axis_index("dp")
    chip, core = me // 2, me % 2
    chips = count // 2
    line, side = chip // 2, chip % 2
    place = jnp.where(side == 0, line, chips - 1 - line)
    spot = lax.rem(place + distances[k // 2] + chips, chips)
    there = jnp.where(spot < chips // 2, 2 * spot, 2 * (chips - 1 - spot) + 1)
    return 2 * there + (core if k % 2 == 0 else 1 - core)


def adam_update(master, moment_one, moment_two, gradient, factor):
    clipped = gradient * factor
    new_one = beta_one * moment_one + (1.0 - beta_one) * clipped
    new_two = beta_two * moment_two + (1.0 - beta_two) * clipped * clipped
    fixed_one = new_one / (1.0 - beta_one**STEP)
    fixed_two = new_two / (1.0 - beta_two**STEP)
    updated = master - learn_rate * (
        fixed_one / (jnp.sqrt(fixed_two) + adam_eps) + decay_rate * master
    )
    return (updated, new_one, new_two)


def to_all(value, axis):
    copies = lax.axis_size(axis)
    spread = jnp.broadcast_to(value[None], (copies,) + value.shape)
    return lax.all_to_all(spread, axis, split_axis=0, concat_axis=0, tiled=True)


def norm_parts(values):
    center = jnp.mean(values, axis=-1, keepdims=True)
    offsets = values - center
    spread = jnp.mean(offsets * offsets, axis=-1, keepdims=True)
    scale = lax.rsqrt(spread + norm_eps)
    return offsets * scale, scale


def norm_back(grad, centered, scale, gain):
    inner = grad * gain
    mean_one = jnp.mean(inner, axis=-1, keepdims=True)
    mean_two = jnp.mean(inner * centered, axis=-1, keepdims=True)
    d_values = scale * (inner - mean_one - centered * mean_two)
    d_gain = jnp.sum(grad * centered, axis=0, keepdims=True)
    return d_values, d_gain, jnp.sum(grad, axis=0, keepdims=True)


def gelu_back(values):
    inner = gelu_scale * (values + gelu_cube * values * values * values)
    bend = jnp.tanh(inner)
    slope = gelu_scale * (1.0 + 3.0 * gelu_cube * values * values)
    return 0.5 * (1.0 + bend) + 0.5 * values * (1.0 - bend * bend) * slope


def spread_heads(rows, width):
    size = width // H
    head_of = lax.broadcasted_iota(jnp.int32, rows.shape, 1) // size
    nothing = jnp.zeros_like(rows)
    return jnp.concatenate([jnp.where(head_of == h, rows, nothing) for h in range(H)], axis=0)


def join_heads(spread, count, width):
    size = width // H
    head_of = lax.broadcasted_iota(jnp.int32, (count, width), 1) // size
    total = jnp.zeros((count, width), wide)
    for h in range(H):
        total = total + jnp.where(head_of == h, spread[h * count : (h + 1) * count], 0.0)
    return total


def one_hot(column, count):
    spots = lax.broadcasted_iota(jnp.int32, (column.shape[0], count), 1)
    return jnp.where(column == spots, 1.0, 0.0).astype(low)


def weight(w_ref, j):
    devices, _, width = w_ref.shape
    rows = width // devices
    return w_ref[:, j * rows : (j + 1) * rows, :].reshape(width, width)


def weight_tail(w_ref, first):
    devices, _, width = w_ref.shape
    rows = width // devices
    return w_ref[:, first * rows : (first + 4) * rows, :].reshape(4 * width, width)


def position_rows(w_ref, first, owners):
    devices, _, width = w_ref.shape
    base = first * (width // devices)
    return w_ref[:owners, base : base + LONGEST // owners, :].reshape(LONGEST, width)


def weight_copies(w_hbm, w_ref, sems):
    rows = w_ref.shape[2] // w_ref.shape[0]
    cuts = (0, 3 * rows, 4 * rows, 8 * rows, w_ref.shape[1])
    copies = []
    for k in range(4):
        span = pl.ds(cuts[k], cuts[k + 1] - cuts[k])
        copies.append(
            pltpu.make_async_copy(w_hbm.at[:, span, :], w_ref.at[:, span, :], sems.at[k])
        )
    return copies


def attention_weights(queries, keys_all, picked, docs):
    width = queries.shape[1]
    picks, length = queries.shape[0], keys_all.shape[0]
    scaling = (width // H) ** (-0.5)
    scores = dot_last(spread_heads(queries, width), keys_all) * scaling
    spots = lax.broadcasted_iota(jnp.int32, (picks, length), 1)
    allowed = (picked[:, 1:2] == docs) & (spots <= picked[:, 0:1])
    penalty = jnp.where(allowed, 0.0, 1.0)
    blocked = jnp.concatenate([penalty] * H, axis=0) > 0.5
    scores = jnp.where(blocked, neg_big, scores)
    row_max = jnp.max(scores, axis=-1, keepdims=True)
    weights_exp = jnp.exp(scores - row_max)
    return weights_exp / jnp.sum(weights_exp, axis=-1, keepdims=True)


def forward_kernel(
    owners,
    cols_ref,
    docs_ref,
    picks_ref,
    back_ref,
    vec_ref,
    w_hbm,
    final_ref,
    x_ref,
    q_ref,
    mid_ref,
    pre_ref,
    top_ref,
    lefts_ref,
    w_ref,
    sems,
):
    copies = weight_copies(w_hbm, w_ref, sems)
    for k in (3, 0, 1, 2):
        copies[k].start()
    devices, held, width = back_ref.shape
    batches, length = cols_ref.shape[:2]
    picks = picks_ref.shape[1]
    capacity = held // batches
    slot_count = devices * capacity
    vec = vec_ref[...]

    def row(k):
        return vec[k : k + 1]

    mixed = []
    for m in range(batches):
        sources = back_ref[:, m * capacity : (m + 1) * capacity, :].reshape(slot_count, width)
        pick = one_hot(cols_ref[m, :, 0:1], slot_count)
        pick_pos = one_hot(cols_ref[m, :, 1:2], LONGEST)
        picked = picks_ref[m]
        select = one_hot(picked[:, 0:1], length)
        embedded = dot_plain(pick, sources)
        if m == 0:
            copies[3].wait()
        pos = position_rows(w_ref, 12, owners)
        x_embed = embedded + dot_plain(pick_pos, pos)
        x_ref[m] = x_embed
        pick_c = dot_plain(select, pick).astype(low)
        pick_pos_c = dot_plain(select, pick_pos).astype(low)
        x_chosen = dot_plain(pick_c, sources) + dot_plain(pick_pos_c, pos)
        normed = (norm_parts(x_embed)[0] * row(0) + row(1)).astype(low)
        normed_c = dot_plain(select, normed).astype(low)
        if m == 0:
            copies[0].wait()
        keys_all = dot_plain(normed, weight(w_ref, 1)).astype(low)
        values = (dot_plain(normed, weight(w_ref, 2)) + row(7)).astype(low)
        queries = (dot_plain(normed_c, weight(w_ref, 0)) + row(6)).astype(low)
        q_ref[m * picks : (m + 1) * picks] = queries
        probs = attention_weights(queries, keys_all, picked, docs_ref[m])
        spread = dot_plain(probs.astype(low), values)
        mixed.append(join_heads(spread, picks, width).astype(low))
        mid_ref[m * picks : (m + 1) * picks] = x_chosen
    mixed = jnp.concatenate(mixed, axis=0)
    copies[1].wait()
    x_mid = mid_ref[...] + dot_plain(mixed, weight(w_ref, 3)) + row(8)
    mid_ref[...] = x_mid
    normed_two = (norm_parts(x_mid)[0] * row(2) + row(3)).astype(low)
    copies[2].wait()
    for j in range(4):
        span = slice(j * width, (j + 1) * width)
        pre_ref[:, span] = dot_plain(normed_two, weight(w_ref, 4 + j)) + row(10 + j)
    activated = gelu_tanh(pre_ref[...]).astype(low)
    x_top = x_mid + dot_plain(activated, weight_tail(w_ref, 8)) + row(9)
    top_ref[...] = x_top
    final_ref[...] = (norm_parts(x_top)[0] * row(4) + row(5)).astype(low)
    share = width // devices
    for d in range(devices):
        lefts_ref[d, :, : 4 * share] = activated[:, 4 * share * d : 4 * share * (d + 1)]
        lefts_ref[d, :, 4 * share : 5 * share] = normed_two[:, share * d : share * (d + 1)]
        lefts_ref[d, :, 5 * share :] = mixed[:, share * d : share * (d + 1)]


def run_forward(cols, docs, picked, back, vec, whole, owners):
    batches, length = cols.shape[:2]
    picks = picked.shape[1]
    devices = back.shape[0]
    width = vec.shape[1]
    vmem = pl.BlockSpec(memory_space=pltpu.VMEM)
    count = batches * picks

    def shape(dims, kind):
        return jax.ShapeDtypeStruct(dims, kind)

    return pl.pallas_call(
        functools.partial(forward_kernel, owners),
        out_shape=(
            shape((count, width), low),
            shape((batches, length, width), wide),
            shape((count, width), low),
            shape((count, width), wide),
            shape((count, 4 * width), wide),
            shape((count, width), wide),
            shape((devices, count, 6 * width // devices), low),
        ),
        in_specs=[vmem] * 5 + [pl.BlockSpec(memory_space=pl.ANY)],
        out_specs=(vmem,) * 7,
        scratch_shapes=[
            pltpu.VMEM(whole.shape, low),
            pltpu.SemaphoreType.DMA((4,)),
        ],
        compiler_params=kernel_limit(44),
        cost_estimate=kernel_cost(15),
        name="layer_forward",
    )(cols, docs, picked, back, vec, whole)


def column_sum(values):
    return jnp.sum(values.astype(wide), axis=0, keepdims=True)


def upper_kernel(
    d_final_ref,
    vec_ref,
    mid_ref,
    pre_ref,
    top_ref,
    w_hbm,
    d_mid_ref,
    d_attended_ref,
    g_vec_ref,
    rights_ref,
    w_ref,
    sems,
):
    rows = w_ref.shape[2] // w_ref.shape[0]
    copies = []
    for k, (first, last) in enumerate(((8, 12), (4, 8), (3, 4))):
        count = (last - first) * rows
        copies.append(
            pltpu.make_async_copy(
                w_hbm.at[:, pl.ds(first * rows, count), :],
                w_ref.at[:, pl.ds((first - 3) * rows, count), :],
                sems.at[k],
            )
        )
        copies[k].start()
    width = mid_ref.shape[1]
    hidden = 4 * width
    vec = vec_ref[...]

    def row(k):
        return vec[k : k + 1]

    centered, scale = norm_parts(top_ref[...])
    d_top, d_gain, d_shift = norm_back(d_final_ref[...], centered, scale, row(4))
    g_vec_ref[0:4] = jnp.zeros((4, width), wide)
    g_vec_ref[4:5] = d_gain
    g_vec_ref[5:6] = d_shift
    g_vec_ref[6:8] = jnp.zeros((2, width), wide)
    g_vec_ref[14:16] = jnp.zeros((2, width), wide)
    d_branch = d_top.astype(low)
    rights_ref[:, :width] = d_branch
    g_vec_ref[9:10] = column_sum(d_branch)
    pre = pre_ref[...]
    bend = gelu_back(pre)
    centered, scale = norm_parts(mid_ref[...])
    copies[0].wait()
    d_pre = (dot_last(d_branch, weight_tail(w_ref, 5)) * bend).astype(low)
    rights_ref[:, width : width + hidden] = d_pre
    copies[1].wait()
    d_normed = jnp.zeros(d_top.shape, wide)
    for j in range(4):
        piece = d_pre[:, j * width : (j + 1) * width]
        g_vec_ref[10 + j : 11 + j] = column_sum(piece)
        d_normed = d_normed + dot_last(piece, weight(w_ref, 1 + j))
    d_mid, d_gain, d_shift = norm_back(d_normed, centered, scale, row(2))
    g_vec_ref[2:3] = d_gain
    g_vec_ref[3:4] = d_shift
    d_mid = d_top + d_mid
    d_mid_ref[...] = d_mid
    d_attn_branch = d_mid.astype(low)
    rights_ref[:, width + hidden :] = d_attn_branch
    g_vec_ref[8:9] = column_sum(d_attn_branch)
    copies[2].wait()
    d_attended_ref[...] = dot_last(d_attn_branch, weight(w_ref, 0)).astype(low)


def lower_kernel(
    count,
    flag_ref,
    d_mid_ref,
    d_attended_ref,
    g_vec_in_ref,
    cols_ref,
    docs_ref,
    picks_ref,
    vec_ref,
    x_ref,
    q_ref,
    w_hbm,
    *refs,
):
    there, near, rest = refs[:count], refs[count : 2 * count], refs[2 * count :]
    sent_ref, g_attn_ref, g_vec_ref, g_pos_ref, w_ref, sems = rest
    length, width = x_ref.shape
    devices, capacity, _ = sent_ref.shape
    slabs, share, _ = w_ref.shape

    def slab_copy(source, slab, sem):
        return pltpu.make_async_copy(source, w_ref.at[slab], sems.at[sem])

    @pl.when(flag_ref[0] == 1)
    def _():
        for k in range(slabs):
            slab_copy(w_hbm.at[k, pl.ds(0, share)], k, k).start()

    @pl.when(flag_ref[0] == 0)
    def _():
        at = 0
        for own, other in zip(there, near):
            for k in range(own.shape[0]):
                slab_copy(own.at[k], piece_slot(at, slabs), at).start()
                if slabs > 1:
                    slab_copy(other.at[k], piece_slot(at + 1, slabs), at + 1).start()
                at = at + 2

    picks = picks_ref.shape[0]
    scaling = (width // H) ** (-0.5)
    vec = vec_ref[...]

    def row(k):
        return vec[k : k + 1]

    pick_pos = one_hot(cols_ref[:, 1:2], LONGEST)
    picked = picks_ref[...]
    select = one_hot(picked[:, 0:1], length)
    queries = q_ref[...]
    d_spread = spread_heads(d_attended_ref[...], width)
    q_spread = spread_heads(queries, width)
    g_vec_ref[...] = g_vec_in_ref[...]
    centered, scale = norm_parts(x_ref[...])
    normed = (centered * row(0) + row(1)).astype(low)
    normed_c = dot_plain(select, normed).astype(low)
    for k in range(slabs):
        slab_copy(w_hbm.at[k, pl.ds(0, share)], k, k).wait()
    keys_all = dot_plain(normed, weight(w_ref, 1)).astype(low)
    values = (dot_plain(normed, weight(w_ref, 2)) + row(7)).astype(low)
    probs = attention_weights(queries, keys_all, picked, docs_ref[...])
    d_probs = dot_last(d_spread, values)
    row_inner = jnp.sum(probs * d_probs, axis=-1, keepdims=True)
    d_scores = (probs * (d_probs - row_inner)).astype(low)
    d_query = (join_heads(dot_plain(d_scores, keys_all), picks, width) * scaling).astype(low)
    g_attn_ref[:, :width] = dot_first(normed_c, d_query).astype(low)
    g_vec_ref[6:7] += column_sum(d_query)
    d_key = (dot_first(d_scores, q_spread) * scaling).astype(low)
    d_value = dot_first(probs.astype(low), d_spread).astype(low)
    g_vec_ref[7:8] += column_sum(d_value)
    d_chosen = dot_first(select, dot_last(d_query, weight(w_ref, 0)).astype(low))
    d_normed = dot_last(d_key, weight(w_ref, 1)) + dot_last(d_value, weight(w_ref, 2))
    d_normed = d_normed + d_chosen
    d_embed, d_gain, d_shift = norm_back(d_normed, centered, scale, row(0))
    g_vec_ref[0:1] += d_gain
    g_vec_ref[1:2] += d_shift
    d_embed = d_embed + lax.dot_general(
        select.astype(wide),
        d_mid_ref[...],
        (((0,), (0,)), ((), ())),
        precision=lax.Precision.HIGHEST,
        preferred_element_type=wide,
    )
    d_embed = d_embed.astype(low)
    pick = one_hot(cols_ref[:, 0:1], devices * capacity)
    sent_ref[...] = dot_first(pick, d_embed).astype(low).reshape(devices, capacity, width)
    g_attn_ref[:, width : 2 * width] = dot_first(normed, d_key).astype(low)
    g_attn_ref[:, 2 * width : 3 * width] = dot_first(normed, d_value).astype(low)
    g_pos = dot_first(pick_pos, d_embed)
    pos_share = LONGEST // devices
    if pos_share % 16:
        g_pos_ref[...] = g_pos
        return
    lane = lax.broadcasted_iota(jnp.int32, (16, LANES), 1)
    unit = jnp.where(lane == lax.broadcasted_iota(jnp.int32, (16, LANES), 0), 1.0, 0.0)
    turned_vec = lax.dot_general(
        g_vec_ref[...],
        unit,
        (((0,), (0,)), ((), ())),
        precision=lax.Precision.HIGHEST,
        preferred_element_type=wide,
    )
    g_attn_ref[:, 3 * width : 3 * width + LANES] = turned_vec.astype(low)
    g_pos = g_pos.astype(low)
    folds = width // devices // pos_share
    part = width // folds
    for d in range(devices):
        for k in range(folds):
            first = (d * folds + k) * pos_share
            g_attn_ref[first : first + pos_share, 3 * width + LANES :] = g_pos[
                d * pos_share : (d + 1) * pos_share, k * part : (k + 1) * part
            ]
    g_pos_ref[...] = jnp.zeros(g_pos_ref.shape, wide)


def run_upper(d_final, vec, kept, whole):
    count, width = d_final.shape
    slabs = whole.shape[0]
    vmem = pl.BlockSpec(memory_space=pltpu.VMEM)
    hbm = pl.BlockSpec(memory_space=pl.ANY)
    return pl.pallas_call(
        upper_kernel,
        out_shape=(
            jax.ShapeDtypeStruct((count, width), wide),
            jax.ShapeDtypeStruct((count, width), low),
            jax.ShapeDtypeStruct((16, width), wide),
            jax.ShapeDtypeStruct((count, 6 * width), low),
        ),
        in_specs=[vmem] * 5 + [hbm],
        out_specs=(vmem,) * 4,
        scratch_shapes=[
            pltpu.VMEM((slabs, 9 * width // slabs, width), low),
            pltpu.SemaphoreType.DMA((3,)),
        ],
        compiler_params=kernel_limit(44),
        cost_estimate=kernel_cost(9),
        name="upper_backward",
    )(d_final, vec, *kept, whole)


def run_lower(flag, upper, cols, docs, picked, vec, x_embed, queries, whole, there, near, devices):
    length = cols.shape[0]
    width = vec.shape[1]
    capacity = 2 * length // devices
    loose = LONGEST // devices % 16
    vmem = pl.BlockSpec(memory_space=pltpu.VMEM)
    hbm = pl.BlockSpec(memory_space=pl.ANY)

    def shape(dims, kind):
        return jax.ShapeDtypeStruct(dims, kind)

    return pl.pallas_call(
        functools.partial(lower_kernel, len(there)),
        out_shape=(
            shape((devices, capacity, width), low),
            shape((width, 3 * width + (0 if loose else LANES + LONGEST)), low),
            shape((16, width), wide),
            shape((LONGEST if loose else 8, width), wide),
        ),
        in_specs=[pl.BlockSpec(memory_space=pltpu.SMEM)] + [vmem] * 9 + [hbm] * (1 + 2 * len(there)),
        out_specs=(vmem,) * 4,
        scratch_shapes=[
            pltpu.VMEM((whole.shape[0], 3 * width // whole.shape[0], width), low),
            pltpu.SemaphoreType.DMA((whole.shape[0],)),
        ],
        compiler_params=kernel_limit(44),
        cost_estimate=kernel_cost(15),
        name="lower_backward",
    )(flag, *upper, cols, docs, picked, vec, x_embed, queries, whole, *there, *near)


def turned(column):
    count = column.shape[0]
    here = lax.broadcasted_iota(jnp.int32, (count, count), 0)
    there = lax.broadcasted_iota(jnp.int32, (count, count), 1)
    return jnp.sum(jnp.where(here == there, column, 0), axis=0, keepdims=True)


def stood(row):
    count = row.shape[1]
    here = lax.broadcasted_iota(jnp.int32, (count, count), 0)
    there = lax.broadcasted_iota(jnp.int32, (count, count), 1)
    return jnp.sum(jnp.where(here == there, row, 0), axis=1, keepdims=True)


def route_kernel(vocab_rows, shard_ref, row_ref, docs_ref, chosen_ref, notes_ref, cols_ref, picks_ref):
    batches, length, _ = cols_ref.shape
    picks = picks_ref.shape[1]
    devices = notes_ref.shape[0]
    capacity = 2 * length // devices
    slot_count = devices * capacity
    here = lax.broadcasted_iota(jnp.int32, (length, length), 0)
    there = lax.broadcasted_iota(jnp.int32, (length, length), 1)
    for m in range(batches):
        owner = shard_ref[m]
        row = stood(row_ref[m])
        docs = docs_ref[m]
        chosen = chosen_ref[m]
        earlier = jnp.where((owner == turned(owner)) & (there < here), 1, 0)
        slot = owner * capacity + jnp.sum(earlier, axis=1, keepdims=True)
        smaller = jnp.where(docs < stood(docs), 1, 0)
        spot = lax.broadcasted_iota(jnp.int32, (length, 1), 0)
        position = spot - jnp.sum(smaller, axis=1, keepdims=True)
        cols_ref[m, :, 0:1] = slot
        cols_ref[m, :, 1:2] = position
        slots = lax.broadcasted_iota(jnp.int32, (length, slot_count), 1)
        request = vocab_rows + jnp.sum(
            jnp.where(slots == slot, row - vocab_rows, 0), axis=0, keepdims=True
        )
        for d in range(devices):
            notes_ref[d : d + 1, m * capacity : (m + 1) * capacity] = request[
                :, d * capacity : (d + 1) * capacity
            ]
        is_next = lax.broadcasted_iota(jnp.int32, (length, picks), 0) == chosen + 1
        ids = jnp.sum(
            jnp.where(is_next, owner * vocab_rows + row, 0), axis=0, keepdims=True
        )
        base = batches * capacity + m * picks
        notes_ref[:, base : base + picks] = jnp.broadcast_to(ids, (devices, picks))
        chosen = stood(chosen)
        among = lax.broadcasted_iota(jnp.int32, (picks, length), 1) == chosen
        picks_ref[m, :, 0:1] = chosen
        picks_ref[m, :, 1:2] = jnp.sum(jnp.where(among, docs, 0), axis=1, keepdims=True)


def run_route(shard, row, docs, chosen, devices, vocab_rows):
    batches, length, _ = shard.shape
    picks = chosen.shape[2]
    vmem = pl.BlockSpec(memory_space=pltpu.VMEM)
    held = batches * (2 * length // devices + picks)
    return pl.pallas_call(
        functools.partial(route_kernel, vocab_rows),
        out_shape=(
            jax.ShapeDtypeStruct((devices, held), jnp.int32),
            jax.ShapeDtypeStruct((batches, length, 2), jnp.int32),
            jax.ShapeDtypeStruct((batches, picks, 2), jnp.int32),
        ),
        in_specs=[vmem] * 4,
        out_specs=(vmem,) * 3,
        compiler_params=kernel_limit(56),
        cost_estimate=kernel_cost(3),
        name="route_tokens",
    )(shard, row, docs, chosen)


def pack_kernel(
    student_ref, attn_in, attn_out, mlp_in, mlp_out, pos, vecs, t_attn_in, t_attn_out, t_mlp_in, t_mlp_out, t_pos, t_vecs, out_ref
):
    is_student = student_ref[0] == 1
    rows, width = attn_out.shape

    def write(refs):
        ins, out, up, down, spots, small = refs
        for j in range(3):
            out_ref[j * rows : (j + 1) * rows] = ins[:, j * width : (j + 1) * width].astype(low)
        out_ref[3 * rows : 4 * rows] = out[...].astype(low)
        for j in range(4):
            out_ref[(4 + j) * rows : (5 + j) * rows] = up[
                :, j * width : (j + 1) * width
            ].astype(low)
        out_ref[8 * rows : 12 * rows] = down[...].astype(low)
        end = 12 * rows + spots.shape[0]
        out_ref[12 * rows : end] = spots[...].astype(low)
        out_ref[end : end + 16] = small[...].astype(low)

    @pl.when(is_student)
    def _():
        write((attn_in, attn_out, mlp_in, mlp_out, pos, vecs))

    @pl.when(jnp.logical_not(is_student))
    def _():
        write((t_attn_in, t_attn_out, t_mlp_in, t_mlp_out, t_pos, t_vecs))


def pack_plain(attn_in, attn_out, mlp_in, mlp_out, pos, vecs):
    width = attn_out.shape[1]
    ins = [attn_in[:, j * width : (j + 1) * width] for j in range(3)]
    up = [mlp_in[:, j * width : (j + 1) * width] for j in range(4)]
    parts = [*ins, attn_out, *up, mlp_out, pos, vecs]
    return jnp.concatenate([p.astype(low) for p in parts], axis=0)


def pack(is_student, student, teacher):
    rows, width = student[1].shape

    def padded(parts):
        vecs = parts[5]
        fill = ((0, 16 - vecs.shape[0]), (0, width - vecs.shape[1]))
        return [*parts[:5], jnp.pad(vecs, fill)]

    student, teacher = padded(student), padded(teacher)
    if rows % 16 or student[4].shape[0] % 16:
        return jnp.where(is_student, pack_plain(*student), pack_plain(*teacher))
    total = 12 * rows + student[4].shape[0] + 16
    vmem = pl.BlockSpec(memory_space=pltpu.VMEM)
    return pl.pallas_call(
        pack_kernel,
        out_shape=jax.ShapeDtypeStruct((total, width), low),
        in_specs=[pl.BlockSpec(memory_space=pltpu.SMEM)] + [vmem] * 12,
        out_specs=vmem,
        compiler_params=kernel_limit(56),
        cost_estimate=kernel_cost(3),
        name="pack_weights",
    )(is_student.astype(jnp.int32).reshape(1), *student, *teacher)


def unpack(whole, pos_rows, vec_width):
    devices, _, width = whole.shape
    rows = width // devices
    base = 12 * rows
    owners = LONGEST // pos_rows
    small = whole[:, base + pos_rows : base + pos_rows + 16, :vec_width]
    vec = small.transpose(1, 0, 2).reshape(16, width).astype(wide)
    if devices != 16 or rows % 16 or pos_rows % 16:
        pos = whole[:owners, base : base + pos_rows].reshape(1, LONGEST, width)
        blocks = whole[:, : 8 * rows].reshape(devices, 8, rows, width).transpose(1, 0, 2, 3)
        tail = whole[:, 8 * rows : base].reshape(1, 4 * width, width)
        whole = jnp.concatenate([blocks.reshape(1, 8 * width, width), tail, pos], axis=1)
        owners = 1
    return whole, vec, owners


def table_part(limit, step, block, refs):
    flag_ref, own_ref, rows_ref, other_ref, rows_other_ref, asked_ref, asked_last_ref = refs[:7]
    arrived_ref, arrived_other_ref, both_ref = refs[7:]
    count = arrived_ref.shape[0]

    @pl.when((step == 0) & (flag_ref[0] == 1))
    def _():
        both_ref[:count] = arrived_other_ref[...]
        both_ref[count:] = arrived_ref[...]

    @pl.when((step == 0) & (flag_ref[0] == 0))
    def _():
        both_ref[:count] = arrived_ref[...]
        both_ref[count:] = arrived_other_ref[...]

    ids = step * block + lax.broadcasted_iota(jnp.int32, (block, 1), 0)
    wanted = jnp.where(ids == asked_ref[...], 1.0, 0.0).astype(low)
    wanted_last = jnp.where(ids == asked_last_ref[...], 1.0, 0.0).astype(low)
    is_last = flag_ref[0] == 1

    def ordered(own_ref, other_ref):
        own, other = own_ref[...], other_ref[...]
        return jnp.where(is_last, other, own), jnp.where(is_last, own, other)

    d_low_first, d_low_last = ordered(own_ref, other_ref)
    rows_first, rows_last = ordered(rows_ref, rows_other_ref)
    return ids, (
        dot_plain(d_low_first, rows_first)
        + dot_plain(d_low_last, rows_last)
        + dot_plain(wanted, both_ref[:count])
        + dot_plain(wanted_last, both_ref[count:])
    )


def table_kernel(limit, *refs):
    out_ref, square_ref, both_ref = refs[9:]
    step = pl.program_id(0)
    block = refs[1].shape[0]
    ids, gradient = table_part(limit, step, block, (*refs[:9], both_ref))
    out_ref[...] = gradient
    inside = jnp.where(ids < limit, gradient, 0.0)
    squares = jnp.sum((inside * inside).reshape(block // 8, 8, -1), axis=0)

    @pl.when(step == 0)
    def _():
        square_ref[...] = squares

    @pl.when(step > 0)
    def _():
        square_ref[...] += squares


def table_specs(parts, vocab_rows, cuts):
    block = -(-vocab_rows // (16 * cuts)) * 16
    steps = -(-vocab_rows // block)

    def fixed(dims):
        return pl.BlockSpec(dims, lambda k: (0, 0))

    tall = pl.BlockSpec((block, parts[1].shape[1]), lambda k: (k, 0))
    specs = [pl.BlockSpec(memory_space=pltpu.SMEM), tall, fixed(parts[2].shape), tall]
    specs += [fixed(part.shape) for part in parts[4:]]
    both = pltpu.VMEM((2 * parts[7].shape[0], parts[7].shape[1]), low)
    return block, steps, specs, fixed, both


def run_table(parts, vocab_rows):
    width = parts[2].shape[1]
    block, steps, specs, fixed, both = table_specs(parts, vocab_rows, 6)
    return pl.pallas_call(
        functools.partial(table_kernel, vocab_rows),
        grid=(steps,),
        out_shape=(
            jax.ShapeDtypeStruct((vocab_rows, width), wide),
            jax.ShapeDtypeStruct((8, width), wide),
        ),
        in_specs=specs,
        out_specs=(pl.BlockSpec((block, width), lambda k: (k, 0)), fixed((8, width))),
        scratch_shapes=[both],
        compiler_params=kernel_limit(58),
        cost_estimate=kernel_cost(17),
        name="table_gradient",
    )(*parts)


def adam_kernel(count, factor_ref, *refs):
    ins, outs = refs[: 4 * count], refs[4 * count :]
    for k in range(count):
        master, one, two, gradient = [ref[...] for ref in ins[4 * k : 4 * k + 4]]
        results = adam_update(master, one, two, gradient, factor_ref[0])
        for ref, value in zip(outs[3 * k : 3 * k + 3], results):
            ref[...] = value


def run_adam(factor, groups):
    flat = [value for group in groups for value in group]
    vmem = pl.BlockSpec(memory_space=pltpu.VMEM)
    outs = [jax.ShapeDtypeStruct(g[0].shape, wide) for g in groups for _ in range(3)]
    return pl.pallas_call(
        functools.partial(adam_kernel, len(groups)),
        out_shape=tuple(outs),
        in_specs=[pl.BlockSpec(memory_space=pltpu.SMEM)] + [vmem] * len(flat),
        out_specs=(vmem,) * len(outs),
        compiler_params=kernel_limit(58),
        cost_estimate=kernel_cost(6),
        name="small_updates",
    )(factor.reshape(1), *flat)


def shards(
    token_shard,
    token_row,
    doc_ids,
    loss_rows,
    teacher_table,
    teacher_pos,
    teacher_attn_in,
    teacher_attn_out,
    teacher_mlp_in,
    teacher_mlp_out,
    teacher_vecs,
    table,
    pos_table,
    attn_in,
    attn_out,
    mlp_in,
    mlp_out,
    vectors,
    table_m,
    pos_m,
    attn_in_m,
    attn_out_m,
    mlp_in_m,
    mlp_out_m,
    vectors_m,
    table_v,
    pos_v,
    attn_in_v,
    attn_out_v,
    mlp_in_v,
    mlp_out_v,
    vectors_v,
):
    part = lax.axis_index("pair")
    is_student = part == 1
    me = lax.axis_index("dp")
    devices = lax.axis_size("dp")
    vocab_rows, width = table.shape
    hidden = mlp_in.shape[1]
    rows = attn_in.shape[0]
    fold_rows = mlp_out.shape[0]
    vec_count, vec_width = vectors.shape
    pos_count = pos_table.shape[0]
    swap = [(0, 1), (1, 0)]
    to_teacher = [(1, 0)]
    to_student = [(0, 1)]

    length = token_row.shape[2]
    picks = loss_rows.shape[2]
    capacity = 2 * length // devices
    slot_count = devices * capacity
    total_rows = MB * devices * picks
    student_flag = is_student.astype(jnp.int32).reshape(1)
    docs = doc_ids
    notes, cols, picked = run_route(
        token_shard[:, 0], token_row, docs, loss_rows, devices, vocab_rows
    )
    arrived_notes = lax.all_to_all(notes, "dp", split_axis=0, concat_axis=0, tiled=True)
    arrived_notes, flag = tied(arrived_notes, is_student)
    asked = arrived_notes[:, : MB * capacity]
    targets = arrived_notes[:, MB * capacity :].reshape(devices, MB, picks).transpose(1, 0, 2)
    targets = targets.reshape(MB, devices * picks)[part]

    own_block = pack(
        flag,
        (attn_in, attn_out, mlp_in, mlp_out, pos_table, vectors),
        (
            teacher_attn_in,
            teacher_attn_out,
            teacher_mlp_in,
            teacher_mlp_out,
            teacher_pos,
            teacher_vecs,
        ),
    )
    safe = jnp.minimum(asked, vocab_rows - 1)
    found = lax.cond(
        is_student,
        lambda at: jnp.take(table, at, axis=0).astype(low),
        lambda at: jnp.take(teacher_table, at, axis=0),
        safe,
    )
    def over(value):
        return lax.ppermute(value, "pair", to_teacher)

    def after(ahead, behind):
        nonlocal found
        ahead, behind, found = tied(ahead, behind, found)
        return ahead, behind

    if devices == 16 and rows % 16 == 0 and pos_count % 16 == 0:
        whole, early, late = ring_gather(own_block, after, over, 3 * rows)
    else:
        whole, early, late = lax.all_gather(own_block, "dp", axis=0), None, None
    back = lax.all_to_all(found, "dp", split_axis=0, concat_axis=0, tiled=True)
    whole, vec, owners_pos = unpack(whole, pos_count, vec_width)
    final, x_embed, queries, mid, pre, top, lefts = run_forward(
        cols, docs, picked, back, vec, whole, owners_pos
    )
    final = final.reshape(MB, picks, width)

    def on_both(value):
        return jnp.where(is_student, value, over(value))

    def across(value):
        return lax.ppermute(value, "dp", [(d, d ^ 1) for d in range(devices)])

    core = me % 2
    other_final = lax.ppermute(final[1 - part], "pair", swap)
    own_final = final[part]
    if late is None:
        there = [over(whole[:, : 3 * width])]
    else:
        other_final, late = tied(other_final, late)
        there = [early, over(late)]
    x_over = jnp.concatenate([x_embed[0], queries[:picks].astype(wide), vec], axis=0)
    both = jnp.stack(
        [
            jnp.where(is_student, other_final, own_final),
            jnp.where(is_student, own_final, other_final),
        ]
    )
    every = lax.all_gather(both.reshape(2 * picks, width), "dp", axis=0)
    cuts = (0, 5 * length // 16, 11 * length // 16, x_over.shape[0])
    x_over = [x_over[a:b] for a, b in zip(cuts, cuts[1:])]
    other_final, x_over[0] = tied(other_final, x_over[0])
    x_over[0] = over(x_over[0])
    lefts = lax.all_to_all(lefts, "dp", split_axis=0, concat_axis=0, tiled=True)
    every, lefts, x_over[0], x_over[1] = tied(every, lefts, x_over[0], x_over[1])
    lefts = lefts.reshape(-1, lefts.shape[2])
    x_over[1] = over(x_over[1])
    every = every.reshape(devices, 2, picks, width).transpose(1, 0, 2, 3)
    every = every.reshape(2, devices * picks, width)
    teacher_rows, student_rows = every[0], every[1]
    table_low = table.astype(low)
    teacher_logits = dot_last(teacher_rows, teacher_table)
    logits = dot_last(student_rows, table_low)
    teacher_max = jnp.max(teacher_logits, axis=1)
    teacher_sum = jnp.sum(jnp.exp(teacher_logits - teacher_max[:, None]), axis=1)
    own_max = jnp.max(logits, axis=1)
    own_sum = jnp.sum(jnp.exp(logits - own_max[:, None]), axis=1)
    stats = to_all(jnp.stack([teacher_max, teacher_sum, own_max, own_sum]), "dp")

    stats, x_over[1], x_over[2], *there = tied(stats, x_over[1], x_over[2], *there)
    x_over[2] = over(x_over[2])
    near = [across(value) for value in there]

    def log_total(maxima, sums):
        big = jnp.max(maxima, axis=0)
        return big + jnp.log(jnp.sum(sums * jnp.exp(maxima - big[None]), axis=0))

    teacher_total = log_total(stats[:, 0], stats[:, 1])[:, None]
    own_total = log_total(stats[:, 2], stats[:, 3])[:, None]
    teacher_log = teacher_logits - teacher_total
    teacher_prob = jnp.exp(teacher_log)
    own_log = logits - own_total
    own_prob = jnp.exp(own_log)
    kl_local = jnp.sum(teacher_prob * (teacher_log - own_log))
    vocab_iota = jnp.arange(vocab_rows, dtype=jnp.int32)
    target_hit = (targets - me * vocab_rows)[:, None] == vocab_iota[None, :]
    d_logits = (2.0 * own_prob - target_hit.astype(wide) - teacher_prob) * (1.0 / total_rows)
    d_low = d_logits.astype(low)
    d_final_parts = dot_plain(d_low, table_low).astype(low).reshape(devices, picks, width)
    d_final_parts, x_over[2] = tied(d_final_parts, x_over[2])
    d_final_parts = lax.all_to_all(d_final_parts, "dp", split_axis=0, concat_axis=0, tiled=True)
    d_final = jnp.sum(d_final_parts.astype(wide), axis=0)
    d_final_first = lax.ppermute(d_final, "pair", to_student)
    d_final = jnp.concatenate([d_final_first, d_final], axis=0)

    d_final, rows_sent = tied(d_final, student_rows)
    rows_other = lax.ppermute(rows_sent, "pair", swap)
    d_mid, d_attended, g_vecs, rights = run_upper(d_final, vec, (mid, pre, top), whole)
    d_mid, rows_other = tied(d_mid, rows_other)
    passed = jnp.concatenate([d_mid, d_attended.astype(wide)], axis=1)
    passed = jnp.where(is_student, passed[picks:], over(passed[:picks]))
    x_last = jnp.concatenate([x_embed[1], queries[picks:].astype(wide), vec], axis=0)
    x_last = jnp.where(is_student, x_last, jnp.concatenate(x_over, axis=0))
    sent, g_attn, g_vecs, g_pos = run_lower(
        student_flag,
        (passed[:, :width], passed[:, width:].astype(low), jnp.where(is_student, g_vecs, 0.0)),
        cols[part],
        docs[part],
        picked[part],
        x_last[length + picks :],
        x_last[:length],
        x_last[length : length + picks].astype(low),
        whole,
        there,
        near,
        devices,
    )
    arrived = lax.all_to_all(sent, "dp", split_axis=0, concat_axis=0, tiled=True)
    arrived = arrived.reshape(slot_count, width)

    pos_share = LONGEST // devices
    if pos_share % 16:
        g_vecs = jnp.pad(g_vecs.T, ((0, 0), (0, LANES - g_vecs.shape[0]))).astype(low)
        parts = g_pos.reshape(devices, pos_share, -1, LONGEST).transpose(0, 2, 1, 3)
        parts = parts.reshape(width, LONGEST).astype(low)
        shared = jnp.concatenate([g_attn, g_vecs, parts], axis=1)
    else:
        shared = g_attn
    d_low_sent = d_low
    if devices % 2:
        shared = lax.psum_scatter(shared, "dp", scatter_dimension=0, tiled=True)
    else:
        chips = shared.reshape(devices // 2, 2, rows, -1)
        near_sum = across(lax.dynamic_index_in_dim(chips, 1 - core, 1, keepdims=False))
        near_sum, d_low_sent = tied(near_sum, d_low)
        mine = lax.dynamic_index_in_dim(chips, core, 1, keepdims=False)
        chips = (mine.astype(wide) + near_sum.astype(wide)).astype(low)
    d_low_other = lax.ppermute(d_low_sent, "pair", swap)

    rights = lax.all_gather(rights, "dp", axis=0, tiled=True)
    at = (0, fold_rows, fold_rows + rows, fold_rows + 2 * rows)
    ends = (0, width, width + hidden, 2 * width + hidden)
    products = [
        dot_first(lefts[:, at[k] : at[k + 1]], rights[:, ends[k] : ends[k + 1]]).astype(low)
        for k in range(3)
    ]
    squares = jnp.zeros((), wide)
    for product in products:
        squares = squares + jnp.sum(jnp.square(product.astype(wide)))
    products[1] = products[1].reshape(rows, 4, width).transpose(1, 0, 2).reshape(4 * rows, width)
    products = jnp.concatenate(products, axis=0)
    d_low_turned, d_low_other = d_low.T, d_low_other.T
    arrived, products, squares, d_low_turned, d_low_other = tied(
        arrived, products, squares, d_low_turned, d_low_other
    )
    arrived_other = lax.ppermute(arrived, "pair", swap)
    if devices % 2 == 0:
        chips, arrived = tied(chips, arrived)
        columns = [[2 * k + c for k in range(devices // 2)] for c in (0, 1)]
        chips = lax.all_to_all(
            chips, "dp", split_axis=0, concat_axis=0, axis_index_groups=columns, tiled=True
        )
    asked = asked.reshape(devices, MB, capacity).transpose(1, 0, 2).reshape(MB, 1, slot_count)
    asked_first, asked_last = asked[0], asked[1]
    own_last = is_student.astype(jnp.int32).reshape(1)
    parts = (
        own_last,
        d_low_turned,
        student_rows,
        d_low_other,
        rows_other,
        asked_first,
        asked_last,
        arrived,
        arrived_other,
    )
    if devices % 2 == 0:
        shared = jnp.sum(chips.astype(wide), axis=0).astype(low)
    pos_near = shared[:, 3 * width + LANES :]
    pos_near = pos_near.reshape(-1, pos_share, LONGEST).transpose(1, 0, 2).reshape(pos_share, width)
    pos_near = jnp.pad(pos_near, ((0, max(0, LANES // 2 - pos_share)), (0, 0)))
    pos_near = lax.all_gather(pos_near, "dp", axis=0)[:, :pos_share].reshape(LONGEST, width)
    pos_near = jnp.concatenate([pos_near, jnp.zeros((pos_count, width), low)], axis=0)
    pos_near = lax.dynamic_slice(
        pos_near, (jnp.minimum(me * pos_count, LONGEST), 0), (pos_count, width)
    )
    arrived_other, shared = tied(arrived_other, shared)
    shared_other = lax.ppermute(shared, "pair", swap)
    arrived_other, products = tied(arrived_other, products)
    products_there = over(products)
    parts = (*parts[:-1], arrived_other)
    g_table, table_squares = run_table(parts, vocab_rows)
    table_squares, products_there, shared_other = tied(
        table_squares, products_there, shared_other
    )
    shared = shared.astype(wide) + shared_other.astype(wide)
    squares = squares + jnp.sum(shared * shared) + jnp.sum(table_squares)
    lane = jnp.arange(LANES, dtype=jnp.int32)[None, :]
    totals = to_all(
        jnp.where(lane == 0, squares, jnp.where(lane == 1, kl_local, 0.0)), ("pair", "dp")
    )
    grad_norm = jnp.sqrt(jnp.sum(totals[devices:, 0, 0]))
    kl_mean = jnp.sum(totals[:, 0, 1]) / total_rows
    factor = jnp.minimum(1.0, clip_limit / (grad_norm + 1e-06))
    table_out = adam_update(table, table_m, table_v, g_table, factor)
    products = jnp.where(is_student, products, products_there).astype(wide)
    g_mlp_out, g_attn_out = products[:fold_rows], products[fold_rows + 4 * rows :]
    g_mlp_in = products[fold_rows : fold_rows + 4 * rows].reshape(4, rows, width)
    g_mlp_in = g_mlp_in.transpose(1, 0, 2).reshape(rows, hidden)
    g_pos = pos_near.astype(wide) + lax.ppermute(pos_near, "pair", swap).astype(wide)
    g_attn_in = shared[:, : 3 * width]
    g_vecs = shared[:, 3 * width : 3 * width + vec_count].T
    smalls = (g_pos, g_attn_in, g_attn_out, g_mlp_in, g_mlp_out, g_vecs)
    masters = (pos_table, attn_in, attn_out, mlp_in, mlp_out, vectors)
    firsts = (pos_m, attn_in_m, attn_out_m, mlp_in_m, mlp_out_m, vectors_m)
    seconds = (pos_v, attn_in_v, attn_out_v, mlp_in_v, mlp_out_v, vectors_v)
    small_out = run_adam(factor, list(zip(masters, firsts, seconds, smalls)))
    return (*table_out, *small_out, grad_norm, kl_mean)


def solution(mesh):
    return jax.shard_map(
        shards,
        mesh=mesh,
        in_specs=(
            P(None, "dp", None, None),
            P(None, "dp", None),
            P(None, "dp", None),
            P(None, "dp", None),
            P("dp", None),
            P("dp", None),
            P("dp", None),
            P("dp", None),
            P("dp", None),
            P("dp", None),
            P(None, "dp"),
            P("dp", None),
            P("dp", None),
            P("dp", None),
            P("dp", None),
            P("dp", None),
            P("dp", None),
            P(None, "dp"),
            P("dp", None),
            P("dp", None),
            P("dp", None),
            P("dp", None),
            P("dp", None),
            P("dp", None),
            P(None, "dp"),
            P("dp", None),
            P("dp", None),
            P("dp", None),
            P("dp", None),
            P("dp", None),
            P("dp", None),
            P(None, "dp"),
        ),
        out_specs=(
            P("dp", None),
            P("dp", None),
            P("dp", None),
            P("dp", None),
            P("dp", None),
            P("dp", None),
            P("dp", None),
            P("dp", None),
            P("dp", None),
            P("dp", None),
            P("dp", None),
            P("dp", None),
            P("dp", None),
            P("dp", None),
            P("dp", None),
            P("dp", None),
            P("dp", None),
            P("dp", None),
            P(None, "dp"),
            P(None, "dp"),
            P(None, "dp"),
            P(),
            P(),
        ),
        check_vma=False,
    )
```

time: 621 us -> 552 us (0.89)
  waiting for transfers between devices: 214 us -> 173 us
  local copies, waits for them, and re-layouts: 44 us -> 76.9 us
  blocking collectives: 62.6 us -> 38.9 us
  between operations: 35.3 us -> 22.3 us
  starting transfers between devices: 93.1 us -> 83.3 us
  other arithmetic: 63.3 us -> 55.6 us
  Pallas kernels: 76 us -> 68.7 us
    ppermute x5 -> x18, waiting for transfers between devices: 94.7 us -> 38.9 us  [the longest x11 30.5 us: over(): return lax.ppermute(value, 'pair', to_teacher)]
    all_to_all x1 -> x2, waiting for transfers between devices: 7.32 us -> 50.7 us  [the longest x1 46.6 us: shards(): lax.all_to_all(chips, 'dp', split_axis=0, concat_axis=0, axis_index_group...]
    ppermute x3, waiting for transfers between devices: 69.5 us -> 41 us  [ring_gather(): ahead = lax.ppermute(ahead, 'dp', onward)]
    all_gather x1 -> x0, blocking collectives: 24.8 us -> none  [shards(): pos_near = lax.all_gather(pos_near, 'dp', axis=0, tiled=True).astype(wide)]
    all_to_all x1, starting transfers between devices: 26.5 us -> 4.21 us  [shards(): lefts = lax.all_to_all(lefts, 'dp', split_axis=0, concat_axis=0, tiled=True)]
    ppermute x3, starting transfers between devices: 23.3 us -> 4.7 us  [ring_gather(): ahead = lax.ppermute(ahead, 'dp', onward)]
    dynamic_update_slice x16, local copies, waits for them, and re-layouts: 8.64 us -> 24.1 us  [the longest x8 13.2 us: keep(): lax.dynamic_update_slice(whole, piece[None], (piece_slot(k, devices), 0, 0))]
    all_gather x1, waiting for transfers between devices: 0.01 us -> 15.1 us  [shards(): rights = lax.all_gather(rights, 'dp', axis=0, tiled=True)]
  transfers between devices with their start and end apart: 32 -> 46, of which waited for: 17 -> 22; matrix products, arithmetic and copies ran while one was open for 9% -> 27% of each run, Pallas kernels for 4% -> 6%
where the time goes in v3:
time: 552 us; the launch traced here: 543 us
  waiting for transfers between devices  173 us (31%)
  starting transfers between devices  83.3 us (15%)
  local copies, waits for them, and re-layouts  76.9 us (14%)
  Pallas kernels  68.7 us (12%)
  other arithmetic  55.6 us (10%)
  blocking collectives  38.9 us (7%)
  matrix products  24.1 us (4%)
  between operations  22.3 us (4%)
    all_to_all x1, waiting for transfers between devices, shards(): lax.all_to_all(chips, 'dp', split_axis=0, concat_axis=0, axis_index_group...  46.6 us
    ppermute x3, waiting for transfers between devices, ring_gather(): ahead = lax.ppermute(ahead, 'dp', onward)  41 us
    ppermute x11, waiting for transfers between devices, over(): return lax.ppermute(value, 'pair', to_teacher)  30.5 us
    sub x1, other arithmetic, adam_update(): master - learn_rate * (fixed_one / (jnp.sqrt(fixed_two) + adam_eps) + dec...  24.4 us
    all_gather x1, blocking collectives, shards(): every = lax.all_gather(both.reshape(2 * picks, width), 'dp', axis=0)  24.1 us
    pallas_call x1, Pallas kernels, run_table(): pl.pallas_call(functools.partial(table_kernel, vocab_rows), grid=(steps,)...  17.8 us
    ppermute x1, starting transfers between devices, ring_gather(): first = lax.ppermute(ahead[:half_rows], 'dp', onward)  17.6 us
    pallas_call x1, Pallas kernels, run_lower(): pl.pallas_call(functools.partial(lower_kernel, len(there)), out_shape=(sh...  16.6 us
  transfers between devices with their start and end apart: 46, of which 22 were waited for; matrix products, arithmetic and copies ran while one was open for 27% of the time, Pallas kernels for 6%

profile of v3, /device:TPU:0, one launch (start us, length us, event | category | flops | bytes accessed | tf_op | source)
XLA Modules:
  0.0 543.3 jit_solution(14781656247607596549)
XLA Ops:
  14.6 7.4 %all-to-all-start = ((s32[16,1,160]{2,1,0:T(1,128)}), s32[16,1,160]{2,1,0:T(1,128)S(1)}, u32[]{:S(2)}, u32[]{:S(2)}) async-start(s32[16,1,160]{2,1,0:T(1,128)} %copy.125), calls=%async_computation | async-start | bytes 32768 | tf_op jit(solution)/shard_map/all_to_all | solution.py:908
  33.9 15.2 %conditional.1 = (bf16[16,128,768]{2,1,0:T(8,128)(2,1)S(1)}) conditional(s32[]{:T(128)} %convert_element_type.101, (s32[16,128]{1,0:T(8,128)S(1)}, bf16[3144,768]{1,0:T(8,128)(2,1)}) %tuple.32, (s32[16,128]{1,0:T(8,128)S(1)}, f32[3144,768]{1,0:T(8,128)}) %tuple.33), branch_computations={%region_0.1_spmd, %region_1.2_spmd} | conditional | flops 1593344 | bytes 12619784 | solution.py:927
  33.9 13.0 %gather_fusion = bf16[2048,768]{1,0:T(8,128)(2,1)} fusion(bf16[3144,768]{1,0:T(8,128)(2,1)} %get-tuple-element.12, s32[2048]{0:T(1024)S(1)} %bitcast_clamp_fusion), kind=kCustom, calls=%fused_computation | custom fusion | bytes 6299648 | tf_op jit(solution)/shard_map/cond/branch_0_fun/jit(_take)/gather | solution.py:930
  49.1 6.4 %collective-permute-done = bf16[656,768]{1,0:T(8,128)(2,1)} collective-permute-done((bf16[656,768]{1,0:T(8,128)(2,1)}, bf16[656,768]{1,0:T(8,128)(2,1)}, u32[]{:S(2)}, u32[]{:S(2)}) %collective-permute-start) | collective-permute-done | bytes 1007648 | tf_op jit(solution)/shard_map/ppermute | solution.py:96
  61.2 5.7 %broadcast_in_dim.113 = bf16[16,656,768]{2,1,0:T(8,128)(2,1)} broadcast(bf16[]{:T(256)} %constant.268.clone.1), dimensions={} | broadcast | bytes 16121858 | tf_op jit(solution)/shard_map/broadcast_in_dim | solution.py:85
  79.0 6.3 %collective-permute-done.8 = bf16[144,768]{1,0:T(8,128)(2,1)S(1)} collective-permute-done((bf16[144,768]{1,0:T(8,128)(2,1)}, bf16[144,768]{1,0:T(8,128)(2,1)S(1)}, u32[]{:S(2)}, u32[]{:S(2)}) %collective-permute-start.8) | collective-permute-done | bytes 221216 | tf_op jit(solution)/shard_map/ppermute | solution.py:934
  88.8 5.6 %collective-permute-done.9 = bf16[144,768]{1,0:T(8,128)(2,1)S(1)} collective-permute-done((bf16[144,768]{1,0:T(8,128)(2,1)}, bf16[144,768]{1,0:T(8,128)(2,1)S(1)}, u32[]{:S(2)}, u32[]{:S(2)}) %collective-permute-start.9) | collective-permute-done | bytes 221216 | tf_op jit(solution)/shard_map/ppermute | solution.py:934
  110.9 4.5 collective-permute-done.15
  115.4 34.6 %collective-permute-done.12 = bf16[656,768]{1,0:T(8,128)(2,1)S(1)} collective-permute-done((bf16[656,768]{1,0:T(8,128)(2,1)}, bf16[656,768]{1,0:T(8,128)(2,1)S(1)}, u32[]{:S(2)}, u32[]{:S(2)}) %collective-permute-start.12) | collective-permute-done | bytes 1007648 | tf_op jit(solution)/shard_map/ppermute | solution.py:96
  152.7 17.6 %collective-permute-start.18 = (bf16[320,768]{1,0:T(8,128)(2,1)S(1)}, bf16[320,768]{1,0:T(8,128)(2,1)S(1)}, u32[]{:S(2)}, u32[]{:S(2)}) collective-permute-start(bf16[320,768]{1,0:T(8,128)(2,1)S(1)} %slice.170), channel_id=1, source_target_pairs={{0,4},{1,5},{4,8},{5,9},{8,12},{9,13},{12,14},{13,15},{14,10},{15,... | collective-permute-start | bytes 1474568 | tf_op jit(solution)/shard_map/ppermute | solution.py:107
  176.5 4.5 collective-permute-done.18
  191.8 14.1 %layer_forward.1 = (bf16[32,768]{1,0:T(8,128)(2,1)S(1)}, f32[2,512,768]{2,1,0:T(8,128)S(1)}, bf16[32,768]{1,0:T(8,128)(2,1)S(1)}, f32[32,768]{1,0:T(8,128)S(1)},...) custom-call(s32[2,512,2]{2,1,0:T(8,128)S(1)} %copy-done.2, ...), custom_call_target="tpu_custom_call" | custom-call | flops 1500000000 | bytes 51000000 | tf_op jit(solution)/shard_map/layer_forward/pallas_call | solution.py:325
  218.4 24.1 %all_gather.12 = bf16[16,32,768]{2,1,0:T(8,128)(2,1)S(1)} all-gather(bf16[1,32,768]{2,1,0:T(8,128)(2,1)S(1)} %bitcast.191), channel_id=1, replica_groups=mesh['pair'=2,'dp'=16] {'dp'}, dimensions={0}, use_global_device_ids=true | all-gather | bytes 835584 | tf_op jit(solution)/shard_map/all_gather | solution.py:973
  247.2 6.5 %fusion.34 = (f32[256]{0:T(256)S(1)}, f32[256,3144]{0,1:T(8,128)S(1)}) fusion(bf16[256,768]{1,0:T(8,128)(2,1)} %bitcast.37.refs_2_, f32[3144,768]{1,0:T(8,128)} %param.45), kind=kOutput, calls=%fused_computation.140 | convolution fusion | flops 1239490304 | bytes 13272064 | tf_op jit(solution)/shard_map/dot_general | solution.py:55
  261.2 6.0 %all-to-all-done.3 = f32[16,4,256]{2,1,0:T(4,128)S(1)} async-done(((f32[16,4,256]{2,1,0:T(4,128)}), f32[16,4,256]{2,1,0:T(4,128)S(1)}, u32[]{:S(2)}, u32[]{:S(2)}) %all-to-all-start.3) | async-done | bytes 65568 | tf_op jit(solution)/shard_map/all_to_all | solution.py:142
  267.1 5.3 collective-permute-done.23
  273.9 6.4 %multiply_reduce_fusion = (f32[]{:T(128)}, bf16[256,3144]{0,1:T(8,128)(2,1)}) fusion(f32[256,3144]{0,1:T(8,128)} %copy-done.11, f32[256,3144]{0,1:T(8,128)} %copy-done.13, f32[256]{0:T(256)S(1)} %log_add_fusion, f32[256]{0:T(256)S(1)} %log_add_fusion.1, s32[256]{0:T(256)S(1)} %bitcast.200), kind=kLoop, calls=%fused_computation.21 | loop fusion | flops 9658367 | bytes 8051716 | tf_op jit(solution)/shard_map/reduce_sum | solution.py:1008
  280.3 5.8 %fusion.10 = bf16[256,768]{1,0:T(8,128)(2,1)S(1)} fusion(bf16[256,3144]{0,1:T(8,128)(2,1)} %get-tuple-element.175, f32[3144,768]{1,0:T(8,128)} %param.45), kind=kOutput, calls=%fused_computation.41 | convolution fusion | flops 1238882304 | bytes 11661312 | tf_op jit(solution)/shard_map/dot_general | solution.py:45
  290.5 14.8 %all_to_all.47 = bf16[16,16,768]{2,1,0:T(8,128)(2,1)S(1)} all-to-all(bf16[16,16,768]{2,1,0:T(8,128)(2,1)S(1)} %bitcast.187), channel_id=1, replica_groups=mesh['pair'=2,'dp'=16] {'dp'}, dimensions={0} | all-to-all | bytes 786432 | tf_op jit(solution)/shard_map/all_to_all | solution.py:1015
  308.7 6.7 %upper_backward.1 = (f32[32,768]{1,0:T(8,128)S(1)}, bf16[32,768]{1,0:T(8,128)(2,1)S(1)}, f32[16,768]{1,0:T(8,128)S(1)}, bf16[32,4608]{1,0:T(8,128)(2,1)}) custom-call(f32[32,768]{1,0:T(8,128)S(1)} %pad_maximum_fusion.6.d_final_ref, f32[16,768]{1,0:T(8,128)S(1)} %reshape.197.vec_ref, f32[32,768]{1,0:T(8,128)S(1)} %get-tuple-element.158.mid_ref, ...), custom_call_target="tpu_custom_call" | custom-call | flops 900000000 | bytes 30600000 | tf_op jit(solution)/shard_map/upper_backward/pallas_call | solution.py:539
  320.8 5.7 %collective-permute-done.27.refs_4_ = bf16[256,768]{1,0:T(8,128)(2,1)} collective-permute-done((bf16[256,768]{1,0:T(8,128)(2,1)}, bf16[256,768]{1,0:T(8,128)(2,1)}, u32[]{:S(2)}, u32[]{:S(2)}) %collective-permute-start.27) | collective-permute-done | bytes 393248 | tf_op jit(solution)/shard_map/ppermute | solution.py:1021
  327.8 5.2 collective-permute-done.28
  333.0 16.6 %lower_backward.1 = (bf16[16,64,768]{2,1,0:T(8,128)(2,1)}, bf16[768,2688]{1,0:T(8,128)(2,1)}, f32[16,768]{1,0:T(8,128)}, f32[8,768]{1,0:T(8,128)}) custom-call(s32[1]{0:T(128)} %bitcast.4.flag_ref.refs_0_, f32[16,768]{1,0:T(8,128)S(1)} %slice.229.d_mid_ref, bf16[16,768]{1,0:T(8,128)(2,1)S(1)} %slice.292.d_attended_ref, ...), custom_call_target="tpu_custom_call" | custom-call | flops 1500000000 | bytes 51000000 | tf_op jit(solution)/shard_map/lower_backward/pallas_call | solution.py:570
  352.9 4.4 all-to-all-start.5
  357.4 4.8 fusion.3.refs_1_
  365.6 15.1 %all-gather.4.cloned.1.call-done = bf16[512,4608]{1,0:T(8,128)(2,1)} async-done(((bf16[32,4608]{1,0:T(8,128)(2,1)}), bf16[512,4608]{1,0:T(8,128)(2,1)}) %all-gather.4.cloned.1.call-update) | async-done | bytes 4718608 | tf_op jit(solution)/shard_map/all_gather | solution.py:1064
  394.5 5.2 collective-permute-done.32
  400.9 5.5 %all-to-all-start.6 = ((bf16[8,48,2688]{2,1,0:T(8,128)(2,1)}), bf16[8,48,2688]{2,1,0:T(8,128)(2,1)S(1)}, u32[]{:S(2)}, u32[]{:S(2)}) async-start(bf16[8,48,2688]{2,1,0:T(8,128)(2,1)} %fusion.1), calls=%async_computation.6 | async-start | bytes 4128768 | tf_op jit(solution)/shard_map/all_to_all | solution.py:1084
  406.8 46.6 %all-to-all-done.6 = bf16[8,48,2688]{2,1,0:T(8,128)(2,1)S(1)} async-done(((bf16[8,48,2688]{2,1,0:T(8,128)(2,1)}), bf16[8,48,2688]{2,1,0:T(8,128)(2,1)S(1)}, u32[]{:S(2)}, u32[]{:S(2)}) %all-to-all-start.6) | async-done | bytes 2064416 | tf_op jit(solution)/shard_map/all_to_all | solution.py:1084
  460.3 17.8 %table_gradient.1 = (f32[3144,768]{1,0:T(8,128)}, f32[8,768]{1,0:T(8,128)}) custom-call(s32[1]{0:T(128)} %bitcast.4.flag_ref.refs_0_, bf16[3144,256]{1,0:T(8,128)(2,1)} %fusion.3.refs_1_, bf16[256,768]{1,0:T(8,128)(2,1)} %bitcast.37.refs_2_, bf16[3144,256]{1,0:T(8,128)(2,1)} %bitcast.186, bf16[256,768]{1,0:T(8,128)(2,1)} %collective-permute-done.27.refs_4_, ...), custom_call_target="tpu_custom_call" | custom-call | flops 1700000000 | bytes 57800000 | tf_op jit(solution)/shard_map/table_gradient/pallas_call | solution.py:810
  496.4 24.4 %multiply_subtract_fusion = (f32[3144,768]{1,0:T(8,128)}, f32[3144,768]{1,0:T(8,128)}, f32[3144,768]{1,0:T(8,128)}) fusion(f32[3144,768]{1,0:T(8,128)} %param.45, f32[3144,768]{1,0:T(8,128)} %get-tuple-element.186, f32[]{:T(128)} %min_shard_map.3, f32[3144,768]{1,0:T(8,128)} %param.52, f32[3144,768]{1,0:T(8,128)} %param.59), kind=kLoop, calls=%fused_computation.12 | loop fusion | flops 38633472 | bytes 67608576 | tf_op jit(solution)/shard_map/sub | solution.py:133
  527.4 6.3 %small_updates.1 = (f32[64,768]{1,0:T(8,128)}, f32[64,768]{1,0:T(8,128)}, f32[64,768]{1,0:T(8,128)}, f32[48,2304]{1,0:T(8,128)}, f32[48,2304]{1,0:T(8,128)}, /*i...) custom-call(f32[1]{0:T(128)} %bitcast.70.factor_ref, ...), custom_call_target="tpu_custom_call" | custom-call | flops 600000000 | bytes 20400000 | tf_op jit(solution)/shard_map/small_updates/pallas_call | solution.py:839
  (255 shorter events, 167.8 us)
Async XLA Ops:
  31.3 24.3 %collective-permute-start = (bf16[656,768]{1,0:T(8,128)(2,1)}, bf16[656,768]{1,0:T(8,128)(2,1)}, u32[]{:S(2)}, u32[]{:S(2)}) collective-permute-start(bf16[656,768]{1,0:T(8,128)(2,1)} %pack_weights.1), channel_id=1, source_target_pairs={{0,4},{1,5},{4,8},{5,9},{8,12},{9,13},{12,14},{13,15},{14,10},{15,... | collective-permute-start | bytes 3022856 | tf_op jit(solution)/shard_map/ppermute | solution.py:96
  31.7 24.3 %collective-permute-start.1 = (bf16[656,768]{1,0:T(8,128)(2,1)}, bf16[656,768]{1,0:T(8,128)(2,1)}, u32[]{:S(2)}, u32[]{:S(2)}) collective-permute-start(bf16[656,768]{1,0:T(8,128)(2,1)} %pack_weights.1), channel_id=1, source_target_pairs={{4,0},{5,1},{8,4},{9,5},{12,8},{13,9},{14,12},{15,13},{10,14},{11,... | collective-permute-start | bytes 3022856 | tf_op jit(solution)/shard_map/ppermute | solution.py:97
  33.3 42.2 %collective-permute-start.2 = (bf16[656,768]{1,0:T(8,128)(2,1)}, bf16[656,768]{1,0:T(8,128)(2,1)}, u32[]{:S(2)}, u32[]{:S(2)}) collective-permute-start(bf16[656,768]{1,0:T(8,128)(2,1)} %pack_weights.1), channel_id=1, source_target_pairs={{0,1},{1,0},{2,3},{3,2},{4,5},{5,4},{6,7},{7,6},{8,9},{9,8},{10,11... | collective-permute-start | bytes 3022856 | tf_op jit(solution)/shard_map/ppermute | solution.py:89
  56.1 38.4 %collective-permute-start.5 = (bf16[656,768]{1,0:T(8,128)(2,1)}, bf16[656,768]{1,0:T(8,128)(2,1)}, u32[]{:S(2)}, u32[]{:S(2)}) collective-permute-start(bf16[656,768]{1,0:T(8,128)(2,1)} %collective-permute-done), channel_id=1, source_target_pairs={{0,4},{1,5},{4,8},{5,9},{8,12},{9,13},{12,14},{13,15},{14,10},{15,... | collective-permute-start | bytes 3022856 | tf_op jit(solution)/shard_map/ppermute | solution.py:96
  56.7 37.8 %collective-permute-start.6 = (bf16[656,768]{1,0:T(8,128)(2,1)}, bf16[656,768]{1,0:T(8,128)(2,1)}, u32[]{:S(2)}, u32[]{:S(2)}) collective-permute-start(bf16[656,768]{1,0:T(8,128)(2,1)} %collective-permute-done.1), channel_id=1, source_target_pairs={{4,0},{5,1},{8,4},{9,5},{12,8},{13,9},{14,12},{15,13},{10,14},{11,... | collective-permute-start | bytes 3022856 | tf_op jit(solution)/shard_map/ppermute | solution.py:97
  58.1 42.1 %collective-permute-start.3 = (bf16[656,768]{1,0:T(8,128)(2,1)}, bf16[656,768]{1,0:T(8,128)(2,1)}, u32[]{:S(2)}, u32[]{:S(2)}) collective-permute-start(bf16[656,768]{1,0:T(8,128)(2,1)} %collective-permute-done), channel_id=1, source_target_pairs={{0,1},{1,0},{2,3},{3,2},{4,5},{5,4},{6,7},{7,6},{8,9},{9,8},{10,11... | collective-permute-start | bytes 3022856 | tf_op jit(solution)/shard_map/ppermute | solution.py:89
  59.8 15.2 %collective-permute-start.7 = (bf16[144,768]{1,0:T(8,128)(2,1)}, bf16[144,768]{1,0:T(8,128)(2,1)S(1)}, u32[]{:S(2)}, u32[]{:S(2)}) collective-permute-start(bf16[144,768]{1,0:T(8,128)(2,1)} %slice.220), channel_id=1, source_target_pairs={{16,0},{17,1},{18,2},{19,3},{20,4},{21,5},{22,6},{23,7},{24,8},{25... | collective-permute-start | bytes 663560 | tf_op jit(solution)/shard_map/ppermute | solution.py:934
  71.2 119.5 %all-to-all-start.1 = ((bf16[16,128,768]{2,1,0:T(8,128)(2,1)}), bf16[16,128,768]{2,1,0:T(8,128)(2,1)S(1)}, u32[]{:S(2)}, u32[]{:S(2)}) async-start(bf16[16,128,768]{2,1,0:T(8,128)(2,1)} %copy-done.14), calls=%async_computation.1 | async-start | bytes 6291456 | tf_op jit(solution)/shard_map/all_to_all | solution.py:945
  75.0 31.0 %collective-permute-start.4 = (bf16[656,768]{1,0:T(8,128)(2,1)}, bf16[656,768]{1,0:T(8,128)(2,1)S(1)}, u32[]{:S(2)}, u32[]{:S(2)}) collective-permute-start(bf16[656,768]{1,0:T(8,128)(2,1)} %collective-permute-done.1), channel_id=1, source_target_pairs={{0,1},{1,0},{2,3},{3,2},{4,5},{5,4},{6,7},{7,6},{8,9},{9,8},{10,11... | collective-permute-start | bytes 3022856 | tf_op jit(solution)/shard_map/ppermute | solution.py:89
  94.5 75.9 %collective-permute-start.10 = (bf16[656,768]{1,0:T(8,128)(2,1)}, bf16[656,768]{1,0:T(8,128)(2,1)S(1)}, u32[]{:S(2)}, u32[]{:S(2)}) collective-permute-start(bf16[656,768]{1,0:T(8,128)(2,1)} %collective-permute-done.5), channel_id=1, source_target_pairs={{0,1},{1,0},{2,3},{3,2},{4,5},{5,4},{6,7},{7,6},{8,9},{9,8},{10,11... | collective-permute-start | bytes 3022856 | tf_op jit(solution)/shard_map/ppermute | solution.py:89
  94.5 55.6 %collective-permute-start.12 = (bf16[656,768]{1,0:T(8,128)(2,1)}, bf16[656,768]{1,0:T(8,128)(2,1)S(1)}, u32[]{:S(2)}, u32[]{:S(2)}) collective-permute-start(bf16[656,768]{1,0:T(8,128)(2,1)} %collective-permute-done.5), channel_id=1, source_target_pairs={{0,4},{1,5},{4,8},{5,9},{8,12},{9,13},{12,14},{13,15},{14,10},{15,... | collective-permute-start | bytes 3022856 | tf_op jit(solution)/shard_map/ppermute | solution.py:96
  99.1 52.9 %collective-permute-start.13 = (bf16[656,768]{1,0:T(8,128)(2,1)}, bf16[656,768]{1,0:T(8,128)(2,1)S(1)}, u32[]{:S(2)}, u32[]{:S(2)}) collective-permute-start(bf16[656,768]{1,0:T(8,128)(2,1)} %collective-permute-done.6), channel_id=1, source_target_pairs={{4,0},{5,1},{8,4},{9,5},{12,8},{13,9},{14,12},{15,13},{10,14},{11,... | collective-permute-start | bytes 3022856 | tf_op jit(solution)/shard_map/ppermute | solution.py:97
  110.6 63.8 %collective-permute-start.11 = (bf16[656,768]{1,0:T(8,128)(2,1)}, bf16[656,768]{1,0:T(8,128)(2,1)S(1)}, u32[]{:S(2)}, u32[]{:S(2)}) collective-permute-start(bf16[656,768]{1,0:T(8,128)(2,1)} %collective-permute-done.6), channel_id=1, source_target_pairs={{0,1},{1,0},{2,3},{3,2},{4,5},{5,4},{6,7},{7,6},{8,9},{9,8},{10,11... | collective-permute-start | bytes 3022856 | tf_op jit(solution)/shard_map/ppermute | solution.py:89
  152.0 32.4 %collective-permute-start.16 = (bf16[656,768]{1,0:T(8,128)(2,1)S(1)}, bf16[656,768]{1,0:T(8,128)(2,1)S(1)}, u32[]{:S(2)}, u32[]{:S(2)}) collective-permute-start(bf16[656,768]{1,0:T(8,128)(2,1)S(1)} %collective-permute-done.12), channel_id=1, source_target_pairs={{0,1},{1,0},{2,3},{3,2},{4,5},{5,4},{6,7},{7,6},{8,9},{9,8},{10,11... | collective-permute-start | bytes 3022856 | tf_op jit(solution)/shard_map/ppermute | solution.py:89
  152.0 34.5 %collective-permute-start.17 = (bf16[656,768]{1,0:T(8,128)(2,1)S(1)}, bf16[656,768]{1,0:T(8,128)(2,1)S(1)}, u32[]{:S(2)}, u32[]{:S(2)}) collective-permute-start(bf16[656,768]{1,0:T(8,128)(2,1)S(1)} %collective-permute-done.13), channel_id=1, source_target_pairs={{0,1},{1,0},{2,3},{3,2},{4,5},{5,4},{6,7},{7,6},{8,9},{9,8},{10,11... | collective-permute-start | bytes 3022856 | tf_op jit(solution)/shard_map/ppermute | solution.py:89
  152.7 28.3 %collective-permute-start.18 = (bf16[320,768]{1,0:T(8,128)(2,1)S(1)}, bf16[320,768]{1,0:T(8,128)(2,1)S(1)}, u32[]{:S(2)}, u32[]{:S(2)}) collective-permute-start(bf16[320,768]{1,0:T(8,128)(2,1)S(1)} %slice.170), channel_id=1, source_target_pairs={{0,4},{1,5},{4,8},{5,9},{8,12},{9,13},{12,14},{13,15},{14,10},{15,... | collective-permute-start | bytes 1474568 | tf_op jit(solution)/shard_map/ppermute | solution.py:107
  170.4 13.9 %collective-permute-start.19 = (bf16[336,768]{1,0:T(8,128)(2,1)S(1)}, bf16[336,768]{1,0:T(8,128)(2,1)S(1)}, u32[]{:S(2)}, u32[]{:S(2)}) collective-permute-start(bf16[336,768]{1,0:T(8,128)(2,1)S(1)} %slice.171), channel_id=1, source_target_pairs={{4,0},{5,1},{8,4},{9,5},{12,8},{13,9},{14,12},{15,13},{10,14},{11,... | collective-permute-start | bytes 1548296 | tf_op jit(solution)/shard_map/ppermute | solution.py:108
  210.9 31.5 %all-to-all-start.2 = ((bf16[16,32,288]{2,1,0:T(8,128)(2,1)}), bf16[16,32,288]{2,1,0:T(8,128)(2,1)}, u32[]{:S(2)}, u32[]{:S(2)}) async-start(bf16[16,32,288]{2,1,0:T(8,128)(2,1)} %copy-done.4), calls=%async_computation.2 | async-start | bytes 786432 | tf_op jit(solution)/shard_map/all_to_all | solution.py:978
  215.7 26.7 %collective-permute-start.22 = (f32[160,768]{1,0:T(8,128)}, f32[160,768]{1,0:T(8,128)}, u32[]{:S(2)}, u32[]{:S(2)}) collective-permute-start(f32[160,768]{1,0:T(8,128)} %slice_bitcast_fusion.3), channel_id=1, source_target_pairs={{16,0},{17,1},{18,2},{19,3},{20,4},{21,5},{22,6},{23,7},{24,8},{25... | collective-permute-start | bytes 1474568 | tf_op jit(solution)/shard_map/ppermute | solution.py:934
  217.0 50.1 %collective-permute-start.24 = (bf16[3,144,768]{2,1,0:T(8,128)(2,1)}, bf16[3,144,768]{2,1,0:T(8,128)(2,1)S(1)}, u32[]{:S(2)}, u32[]{:S(2)}) collective-permute-start(bf16[3,144,768]{2,1,0:T(8,128)(2,1)} %pad_maximum_fusion.1), channel_id=1, source_target_pairs={{16,0},{17,1},{18,2},{19,3},{20,4},{21,5},{22,6},{23,7},{24,8},{25... | collective-permute-start | bytes 1990664 | tf_op jit(solution)/shard_map/ppermute | solution.py:934
  253.8 18.7 %collective-permute-start.23 = (f32[192,768]{1,0:T(8,128)S(1)}, f32[192,768]{1,0:T(8,128)}, u32[]{:S(2)}, u32[]{:S(2)}) collective-permute-start(f32[192,768]{1,0:T(8,128)S(1)} %copy-done.20), channel_id=1, source_target_pairs={{16,0},{17,1},{18,2},{19,3},{20,4},{21,5},{22,6},{23,7},{24,8},{25... | collective-permute-start | bytes 1769480 | tf_op jit(solution)/shard_map/ppermute | solution.py:934
  260.3 120.4 %all-gather.4.cloned.1.call-start = ((), (), s32[]{:S(2)}) async-start(), calls=%async_computation.8 | async-start | bytes 5013504 | tf_op jit(solution)/shard_map/all_gather | solution.py:1064
  272.6 17.1 %collective-permute-start.25 = (f32[192,768]{1,0:T(8,128)}, f32[192,768]{1,0:T(8,128)S(1)}, u32[]{:S(2)}, u32[]{:S(2)}) collective-permute-start(f32[192,768]{1,0:T(8,128)} %pad_maximum_fusion.3), channel_id=1, source_target_pairs={{16,0},{17,1},{18,2},{19,3},{20,4},{21,5},{22,6},{23,7},{24,8},{25... | collective-permute-start | bytes 1769480 | tf_op jit(solution)/shard_map/ppermute | solution.py:934
  317.9 15.1 %collective-permute-start.29 = (bf16[5,144,768]{2,1,0:T(8,128)(2,1)S(1)}, bf16[5,144,768]{2,1,0:T(8,128)(2,1)S(1)}, u32[]{:S(2)}, u32[]{:S(2)}) collective-permute-start(bf16[5,144,768]{2,1,0:T(8,128)(2,1)S(1)} %copy-done.1), channel_id=1, source_target_pairs={{0,1},{1,0},{2,3},{3,2},{4,5},{5,4},{6,7},{7,6},{8,9},{9,8},{10,11... | collective-permute-start | bytes 3317768 | tf_op jit(solution)/shard_map/ppermute | solution.py:956
  318.0 15.0 %collective-permute-start.30 = (bf16[3,144,768]{2,1,0:T(8,128)(2,1)S(1)}, bf16[3,144,768]{2,1,0:T(8,128)(2,1)S(1)}, u32[]{:S(2)}, u32[]{:S(2)}) collective-permute-start(bf16[3,144,768]{2,1,0:T(8,128)(2,1)S(1)} %collective-permute-done.24.refs_1_), channel_id=1, source_target_pairs={{0,1},{1,0},{2,3},{3,2},{4,5},{5,4},{6,7},{7,6},{8,9},{9,8},{10,11... | collective-permute-start | bytes 1990664 | tf_op jit(solution)/shard_map/ppermute | solution.py:956
  352.9 41.6 %all-to-all-start.5 = ((bf16[16,64,768]{2,1,0:T(8,128)(2,1)}), bf16[16,64,768]{2,1,0:T(8,128)(2,1)}, u32[]{:S(2)}, u32[]{:S(2)}) async-start(bf16[16,64,768]{2,1,0:T(8,128)(2,1)} %get-tuple-element.171), calls=%async_computation.5 | async-start | bytes 3145728 | tf_op jit(solution)/shard_map/all_to_all | solution.py:1042
  362.2 37.6 %collective-permute-start.32 = (bf16[256,3144]{0,1:T(8,128)(2,1)}, bf16[256,3144]{0,1:T(8,128)(2,1)S(1)}, u32[]{:S(2)}, u32[]{:S(2)}) collective-permute-start(bf16[256,3144]{0,1:T(8,128)(2,1)} %get-tuple-element.175), channel_id=1, source_target_pairs={{0,16},{16,0},{1,17},{17,1},{2,18},{18,2},{3,19},{19,3},{4,20},{20... | collective-permute-start | bytes 4829192 | tf_op jit(solution)/shard_map/ppermute | solution.py:1062
  400.9 52.5 %all-to-all-start.6 = ((bf16[8,48,2688]{2,1,0:T(8,128)(2,1)}), bf16[8,48,2688]{2,1,0:T(8,128)(2,1)S(1)}, u32[]{:S(2)}, u32[]{:S(2)}) async-start(bf16[8,48,2688]{2,1,0:T(8,128)(2,1)} %fusion.1), calls=%async_computation.6 | async-start | bytes 4128768 | tf_op jit(solution)/shard_map/all_to_all | solution.py:1084
  406.4 114.4 %all-gather.6.cloned.1.call-start = ((), (), s32[]{:S(2)}) async-start(), calls=%async_computation.9 | async-start | bytes 1671168 | tf_op jit(solution)/shard_map/all_gather | solution.py:1106
  406.5 47.3 %collective-permute-start.33 = (bf16[1024,768]{1,0:T(8,128)(2,1)}, bf16[1024,768]{1,0:T(8,128)(2,1)}, u32[]{:S(2)}, u32[]{:S(2)}) collective-permute-start(bf16[1024,768]{1,0:T(8,128)(2,1)} %bitcast.59.refs_7_), channel_id=1, source_target_pairs={{0,16},{16,0},{1,17},{17,1},{2,18},{18,2},{3,19},{19,3},{4,20},{20... | collective-permute-start | bytes 4718600 | tf_op jit(solution)/shard_map/ppermute | solution.py:1080
  453.8 24.3 %collective-permute-start.34 = (bf16[432,768]{1,0:T(8,128)(2,1)S(1)}, bf16[432,768]{1,0:T(8,128)(2,1)S(1)}, u32[]{:S(2)}, u32[]{:S(2)}) collective-permute-start(bf16[432,768]{1,0:T(8,128)(2,1)S(1)} %pad_maximum_fusion.2), channel_id=1, source_target_pairs={{16,0},{17,1},{18,2},{19,3},{20,4},{21,5},{22,6},{23,7},{24,8},{25... | collective-permute-start | bytes 1990664 | tf_op jit(solution)/shard_map/ppermute | solution.py:934
  455.2 22.9 %collective-permute-start.35 = (bf16[48,2688]{1,0:T(8,128)(2,1)S(1)}, bf16[48,2688]{1,0:T(8,128)(2,1)S(1)}, u32[]{:S(2)}, u32[]{:S(2)}) collective-permute-start(bf16[48,2688]{1,0:T(8,128)(2,1)S(1)} %reduce_sum.137), channel_id=1, source_target_pairs={{0,16},{16,0},{1,17},{17,1},{2,18},{18,2},{3,19},{19,3},{4,20},{20... | collective-permute-start | bytes 774152 | tf_op jit(solution)/shard_map/ppermute | solution.py:1112
  (42 other events, 403.3 us)
Sparse Core Ops, SparseCore 0:
  315.6 65.0 all-gather.3
  460.4 37.8 all-gather.5

commit v4 on v3

--- a/solution.py
+++ b/solution.py
@@ -82,7 +82,6 @@
     backward = [(there, here) for here, there in onward]
     across = [(d, d ^ 1) for d in range(devices)]
     half_rows = block.shape[0] // 32 * 16
-    whole = jnp.zeros((devices,) + block.shape, block.dtype)
 
     def keep(whole, piece, distance):
         k = 2 * distances.index(distance)
@@ -90,25 +89,31 @@
         whole = lax.dynamic_update_slice(whole, piece[None], (piece_slot(k, devices), 0, 0))
         return lax.dynamic_update_slice(whole, partner[None], (piece_slot(k + 1, devices), 0, 0))
 
-    ahead, behind = block, block
-    sent = [over(block[:share])]
-    for distance in range(1, chips // 2):
-        ahead = lax.ppermute(ahead, "dp", onward)
-        behind = lax.ppermute(behind, "dp", backward)
-        if distance == 1:
-            ahead, behind = after(ahead, behind)
-            whole = keep(whole, block, 0)
-        else:
-            ahead, behind, *sent = tied(ahead, behind, *sent)
-        if distance < 3:
-            sent += [over(ahead[:share]), over(behind[:share])]
-        whole = keep(whole, ahead, -distance)
-        whole = keep(whole, behind, distance)
+    def step(ahead, behind):
+        return lax.ppermute(ahead, "dp", onward), lax.ppermute(behind, "dp", backward)
+
+    near = after(1, *step(block, block))
+    far = after(2, *step(*near))
+    *far, block, near_ahead, near_behind, blank = tied(
+        *far, block, *near, jnp.zeros((), block.dtype)
+    )
+    whole = jnp.broadcast_to(blank, (devices,) + block.shape)
+    sent = [over(piece[:share]) for piece in (block, near_ahead, near_behind)]
+    whole = keep(whole, block, 0)
+    whole = keep(whole, near_ahead, -1)
+    whole = keep(whole, near_behind, 1)
+    ahead, behind = after(3, *step(*far))
+    ahead, behind, *sent = tied(ahead, behind, *sent)
+    sent += [over(piece[:share]) for piece in far]
+    whole = keep(whole, far[0], -2)
+    whole = keep(whole, far[1], 2)
     first = lax.ppermute(ahead[:half_rows], "dp", onward)
     second = lax.ppermute(behind[half_rows:], "dp", backward)
+    whole = keep(whole, ahead, -3)
+    whole = keep(whole, behind, 3)
     last = jnp.concatenate([first, second], axis=0)
     late = jnp.stack([ahead[:share], behind[:share], last[:share]])
-    return keep(whole, last, chips // 2), jnp.stack(sent), late
+    return keep(whole, last, 4), jnp.stack(sent), late
 
 
 def piece_slot(k, count):
@@ -234,13 +239,16 @@
 
 def forward_kernel(
     owners,
+    flag_ref,
     cols_ref,
     docs_ref,
     picks_ref,
     back_ref,
     vec_ref,
     w_hbm,
-    final_ref,
+    send_ref,
+    own_ref,
+    aims_ref,
     x_ref,
     q_ref,
     mid_ref,
@@ -278,6 +286,10 @@
         x_ref[m] = x_embed
         pick_c = dot_plain(select, pick).astype(low)
         pick_pos_c = dot_plain(select, pick_pos).astype(low)
+        following = one_hot(picked[:, 0:1] + 1, length)
+        aims_ref[m * picks : (m + 1) * picks] = dot_plain(
+            dot_plain(following, pick).astype(low), sources
+        )
         x_chosen = dot_plain(pick_c, sources) + dot_plain(pick_pos_c, pos)
         normed = (norm_parts(x_embed)[0] * row(0) + row(1)).astype(low)
         normed_c = dot_plain(select, normed).astype(low)
@@ -303,7 +315,10 @@
     activated = gelu_tanh(pre_ref[...]).astype(low)
     x_top = x_mid + dot_plain(activated, weight_tail(w_ref, 8)) + row(9)
     top_ref[...] = x_top
-    final_ref[...] = (norm_parts(x_top)[0] * row(4) + row(5)).astype(low)
+    final = (norm_parts(x_top)[0] * row(4) + row(5)).astype(low)
+    is_last = flag_ref[0] == 1
+    send_ref[...] = jnp.where(is_last, final[:picks], final[picks:])
+    own_ref[...] = jnp.where(is_last, final[picks:], final[:picks])
     share = width // devices
     for d in range(devices):
         lefts_ref[d, :, : 4 * share] = activated[:, 4 * share * d : 4 * share * (d + 1)]
@@ -311,7 +326,7 @@
         lefts_ref[d, :, 5 * share :] = mixed[:, share * d : share * (d + 1)]
 
 
-def run_forward(cols, docs, picked, back, vec, whole, owners):
+def run_forward(flag, cols, docs, picked, back, vec, whole, owners):
     batches, length = cols.shape[:2]
     picks = picked.shape[1]
     devices = back.shape[0]
@@ -325,7 +340,9 @@
     return pl.pallas_call(
         functools.partial(forward_kernel, owners),
         out_shape=(
-            shape((count, width), low),
+            shape((picks, width), low),
+            shape((picks, width), low),
+            shape((count, width), wide),
             shape((batches, length, width), wide),
             shape((count, width), low),
             shape((count, width), wide),
@@ -333,16 +350,16 @@
             shape((count, width), wide),
             shape((devices, count, 6 * width // devices), low),
         ),
-        in_specs=[vmem] * 5 + [pl.BlockSpec(memory_space=pl.ANY)],
-        out_specs=(vmem,) * 7,
+        in_specs=[pl.BlockSpec(memory_space=pltpu.SMEM)] + [vmem] * 5 + [pl.BlockSpec(memory_space=pl.ANY)],
+        out_specs=(vmem,) * 9,
         scratch_shapes=[
             pltpu.VMEM(whole.shape, low),
             pltpu.SemaphoreType.DMA((4,)),
         ],
-        compiler_params=kernel_limit(44),
+        compiler_params=kernel_limit(36),
         cost_estimate=kernel_cost(15),
         name="layer_forward",
-    )(cols, docs, picked, back, vec, whole)
+    )(flag, cols, docs, picked, back, vec, whole)
 
 
 def column_sum(values):
@@ -356,8 +373,8 @@
     pre_ref,
     top_ref,
     w_hbm,
-    d_mid_ref,
-    d_attended_ref,
+    first_ref,
+    last_ref,
     g_vec_ref,
     rights_ref,
     w_ref,
@@ -408,12 +425,16 @@
     g_vec_ref[2:3] = d_gain
     g_vec_ref[3:4] = d_shift
     d_mid = d_top + d_mid
-    d_mid_ref[...] = d_mid
+    picks = first_ref.shape[0]
+    first_ref[:, :width] = d_mid[:picks]
+    last_ref[:, :width] = d_mid[picks:]
     d_attn_branch = d_mid.astype(low)
     rights_ref[:, width + hidden :] = d_attn_branch
     g_vec_ref[8:9] = column_sum(d_attn_branch)
     copies[2].wait()
-    d_attended_ref[...] = dot_last(d_attn_branch, weight(w_ref, 0)).astype(low)
+    d_attended = dot_last(d_attn_branch, weight(w_ref, 0)).astype(low).astype(wide)
+    first_ref[:, width:] = d_attended[:picks]
+    last_ref[:, width:] = d_attended[picks:]
 
 
 def lower_kernel(
@@ -502,8 +523,8 @@
     d_embed = d_embed.astype(low)
     pick = one_hot(cols_ref[:, 0:1], devices * capacity)
     sent_ref[...] = dot_first(pick, d_embed).astype(low).reshape(devices, capacity, width)
-    g_attn_ref[:, width : 2 * width] = dot_first(normed, d_key).astype(low)
-    g_attn_ref[:, 2 * width : 3 * width] = dot_first(normed, d_value).astype(low)
+    d_both = jnp.concatenate([d_key, d_value], axis=1)
+    g_attn_ref[:, width : 3 * width] = dot_first(normed, d_both).astype(low)
     g_pos = dot_first(pick_pos, d_embed)
     pos_share = LONGEST // devices
     if pos_share % 16:
@@ -539,8 +560,8 @@
     return pl.pallas_call(
         upper_kernel,
         out_shape=(
-            jax.ShapeDtypeStruct((count, width), wide),
-            jax.ShapeDtypeStruct((count, width), low),
+            jax.ShapeDtypeStruct((count // MB, 2 * width), wide),
+            jax.ShapeDtypeStruct((count // MB, 2 * width), wide),
             jax.ShapeDtypeStruct((16, width), wide),
             jax.ShapeDtypeStruct((count, 6 * width), low),
         ),
@@ -585,6 +606,55 @@
         cost_estimate=kernel_cost(15),
         name="lower_backward",
     )(flag, *upper, cols, docs, picked, vec, x_embed, queries, whole, *there, *near)
+
+
+def combine_kernel(parts_ref, d_final_ref, totals_ref):
+    devices, held, width = parts_ref.shape
+    picks = d_final_ref.shape[0]
+    count = width // 3
+    stats = parts_ref[:, 2 * picks :, :].astype(wide)
+    stats = (
+        stats[:, :, :count] + stats[:, :, count : 2 * count] + stats[:, :, 2 * count :]
+    )
+    here = lax.axis_index("dp") * picks + lax.broadcasted_iota(jnp.int32, (picks, count), 0)
+    mine = jnp.where(here == lax.broadcasted_iota(jnp.int32, (picks, count), 1), 1.0, 0.0)
+    shares = []
+    for k in range(2):
+        maxima, sums = stats[:, 2 * k], stats[:, 2 * k + 1]
+        big = jnp.max(maxima, axis=0, keepdims=True)
+        total = big + jnp.log(jnp.sum(sums * jnp.exp(maxima - big), axis=0, keepdims=True))
+        totals_ref[k : k + 1] = total
+        shares.append(
+            lax.dot_general(
+                mine,
+                jnp.exp(maxima - total),
+                (((1,), (1,)), ((), ())),
+                precision=lax.Precision.HIGHEST,
+                preferred_element_type=wide,
+            )
+        )
+    total = jnp.zeros((picks, width), wide)
+    for d in range(devices):
+        total = total + 2.0 * shares[1][:, d : d + 1] * parts_ref[d, picks : 2 * picks].astype(wide)
+        total = total - shares[0][:, d : d + 1] * parts_ref[d, :picks].astype(wide)
+    d_final_ref[...] = total
+
+
+def run_combine(parts, picks):
+    width = parts.shape[2]
+    vmem = pl.BlockSpec(memory_space=pltpu.VMEM)
+    return pl.pallas_call(
+        combine_kernel,
+        out_shape=(
+            jax.ShapeDtypeStruct((picks, width), wide),
+            jax.ShapeDtypeStruct((2, width // 3), wide),
+        ),
+        in_specs=[vmem],
+        out_specs=(vmem, vmem),
+        compiler_params=kernel_limit(16),
+        cost_estimate=kernel_cost(3),
+        name="combine_parts",
+    )(parts)
 
 
 def turned(column):
@@ -679,7 +749,13 @@
         out_ref[8 * rows : 12 * rows] = down[...].astype(low)
         end = 12 * rows + spots.shape[0]
         out_ref[12 * rows : end] = spots[...].astype(low)
-        out_ref[end : end + 16] = small[...].astype(low)
+        count, share = small.shape
+        tall = lax.broadcasted_iota(jnp.int32, (16, count), 0)
+        tall = jnp.where(tall == lax.broadcasted_iota(jnp.int32, (16, count), 1), 1.0, 0.0)
+        broad = lax.broadcasted_iota(jnp.int32, (share, width), 1)
+        broad = jnp.where(broad == lax.broadcasted_iota(jnp.int32, (share, width), 0), 1.0, 0.0)
+        moved = dot_plain(tall.astype(low), small[...].astype(low)).astype(low)
+        out_ref[end : end + 16] = dot_plain(moved, broad.astype(low)).astype(low)
 
     @pl.when(is_student)
     def _():
@@ -706,8 +782,8 @@
         fill = ((0, 16 - vecs.shape[0]), (0, width - vecs.shape[1]))
         return [*parts[:5], jnp.pad(vecs, fill)]
 
-    student, teacher = padded(student), padded(teacher)
     if rows % 16 or student[4].shape[0] % 16:
+        student, teacher = padded(student), padded(teacher)
         return jnp.where(is_student, pack_plain(*student), pack_plain(*teacher))
     total = 12 * rows + student[4].shape[0] + 16
     vmem = pl.BlockSpec(memory_space=pltpu.VMEM)
@@ -821,6 +897,31 @@
         cost_estimate=kernel_cost(17),
         name="table_gradient",
     )(*parts)
+
+
+def norm_kernel(products_ref, squares_ref, mine_ref, theirs_ref, kl_ref, shared_ref, note_ref):
+    shared = mine_ref[...].astype(wide) + theirs_ref[...].astype(wide)
+    shared_ref[...] = shared
+    total = jnp.sum(shared * shared) + jnp.sum(squares_ref[...]) + products_ref[0]
+    lane = lax.broadcasted_iota(jnp.int32, note_ref.shape, 2)
+    note_ref[...] = jnp.where(lane == 0, total, jnp.where(lane == 1, kl_ref[0], 0.0))
+
+
+def run_norm(products, squares, mine, theirs, kl_local, copies):
+    vmem = pl.BlockSpec(memory_space=pltpu.VMEM)
+    smem = pl.BlockSpec(memory_space=pltpu.SMEM)
+    return pl.pallas_call(
+        norm_kernel,
+        out_shape=(
+            jax.ShapeDtypeStruct(mine.shape, wide),
+            jax.ShapeDtypeStruct((copies, 1, LANES), wide),
+        ),
+        in_specs=[smem, vmem, vmem, vmem, smem],
+        out_specs=(vmem, vmem),
+        compiler_params=kernel_limit(16),
+        cost_estimate=kernel_cost(2),
+        name="norm_note",
+    )(products.reshape(1), squares, mine, theirs, kl_local.reshape(1))
 
 
 def adam_kernel(count, factor_ref, *refs):
@@ -933,9 +1034,15 @@
     def over(value):
         return lax.ppermute(value, "pair", to_teacher)
 
-    def after(ahead, behind):
-        nonlocal found
-        ahead, behind, found = tied(ahead, behind, found)
+    table_low = table.astype(low)
+
+    def after(distance, ahead, behind):
+        nonlocal table_low
+        if distance == 1:
+            ahead, behind, _ = tied(ahead, behind, found)
+        if distance == 2:
+            ahead, behind, table_low = tied(ahead, behind, table)
+            table_low = table_low.astype(low)
         return ahead, behind
 
     if devices == 16 and rows % 16 == 0 and pos_count % 16 == 0:
@@ -944,10 +1051,9 @@
         whole, early, late = lax.all_gather(own_block, "dp", axis=0), None, None
     back = lax.all_to_all(found, "dp", split_axis=0, concat_axis=0, tiled=True)
     whole, vec, owners_pos = unpack(whole, pos_count, vec_width)
-    final, x_embed, queries, mid, pre, top, lefts = run_forward(
-        cols, docs, picked, back, vec, whole, owners_pos
-    )
-    final = final.reshape(MB, picks, width)
+    final, own_final, aims, x_embed, queries, mid, pre, top, lefts = run_forward(
+        student_flag, cols, docs, picked, back, vec, whole, owners_pos
+    )
 
     def on_both(value):
         return jnp.where(is_student, value, over(value))
@@ -956,8 +1062,7 @@
         return lax.ppermute(value, "dp", [(d, d ^ 1) for d in range(devices)])
 
     core = me % 2
-    other_final = lax.ppermute(final[1 - part], "pair", swap)
-    own_final = final[part]
+    other_final = lax.ppermute(final, "pair", swap)
     if late is None:
         there = [over(whole[:, : 3 * width])]
     else:
@@ -971,7 +1076,7 @@
         ]
     )
     every = lax.all_gather(both.reshape(2 * picks, width), "dp", axis=0)
-    cuts = (0, 5 * length // 16, 11 * length // 16, x_over.shape[0])
+    cuts = (0, 3 * length // 8, x_over.shape[0])
     x_over = [x_over[a:b] for a, b in zip(cuts, cuts[1:])]
     other_final, x_over[0] = tied(other_final, x_over[0])
     x_over[0] = over(x_over[0])
@@ -982,25 +1087,59 @@
     every = every.reshape(devices, 2, picks, width).transpose(1, 0, 2, 3)
     every = every.reshape(2, devices * picks, width)
     teacher_rows, student_rows = every[0], every[1]
-    table_low = table.astype(low)
     teacher_logits = dot_last(teacher_rows, teacher_table)
     logits = dot_last(student_rows, table_low)
     teacher_max = jnp.max(teacher_logits, axis=1)
-    teacher_sum = jnp.sum(jnp.exp(teacher_logits - teacher_max[:, None]), axis=1)
+    teacher_exp = jnp.exp(teacher_logits - teacher_max[:, None])
+    teacher_sum = jnp.sum(teacher_exp, axis=1)
     own_max = jnp.max(logits, axis=1)
-    own_sum = jnp.sum(jnp.exp(logits - own_max[:, None]), axis=1)
-    stats = to_all(jnp.stack([teacher_max, teacher_sum, own_max, own_sum]), "dp")
-
-    stats, x_over[1], x_over[2], *there = tied(stats, x_over[1], x_over[2], *there)
-    x_over[2] = over(x_over[2])
+    own_exp = jnp.exp(logits - own_max[:, None])
+    own_sum = jnp.sum(own_exp, axis=1)
+    own_sum, *there = tied(own_sum, *there)
     near = [across(value) for value in there]
-
-    def log_total(maxima, sums):
-        big = jnp.max(maxima, axis=0)
-        return big + jnp.log(jnp.sum(sums * jnp.exp(maxima - big[None]), axis=0))
-
-    teacher_total = log_total(stats[:, 0], stats[:, 1])[:, None]
-    own_total = log_total(stats[:, 2], stats[:, 3])[:, None]
+    stats = jnp.stack([teacher_max, teacher_sum, own_max, own_sum])
+    high = lax.reduce_precision(stats, 8, 7)
+    middle = lax.reduce_precision(stats - high, 8, 7)
+    wide_rows = devices * picks * 3 == width
+    pieces = jnp.stack([high, middle, stats - high - middle], axis=1).astype(low)
+    pieces = pieces.reshape(-1, width)
+    d_parts = jnp.concatenate(
+        [
+            dot_plain(teacher_exp.astype(low), table_low).astype(low).reshape(devices, picks, width),
+            dot_plain(own_exp.astype(low), table_low).astype(low).reshape(devices, picks, width),
+            jnp.broadcast_to(pieces[None], (devices,) + pieces.shape),
+        ],
+        axis=1,
+    )
+    d_parts = lax.all_to_all(d_parts, "dp", split_axis=0, concat_axis=0, tiled=True)
+    d_parts, x_over[1] = tied(d_parts, x_over[1])
+    if wide_rows:
+        d_final, totals = run_combine(d_parts, picks)
+        teacher_total, own_total = totals[0], totals[1]
+    else:
+        d_parts = d_parts.astype(wide)
+        stats = jnp.sum(d_parts[:, 2 * picks :].reshape(devices, 4, 3, -1), axis=2)
+
+        def log_total(maxima, sums):
+            big = jnp.max(maxima, axis=0)
+            return big + jnp.log(jnp.sum(sums * jnp.exp(maxima - big[None]), axis=0))
+
+        teacher_total = log_total(stats[:, 0], stats[:, 1])
+        own_total = log_total(stats[:, 2], stats[:, 3])
+
+        def shares(maxima, totals):
+            scale = jnp.exp(maxima - totals[None])
+            return lax.dynamic_slice_in_dim(scale, me * picks, picks, 1)[..., None]
+
+        d_final = jnp.sum(
+            2.0 * shares(stats[:, 2], own_total) * d_parts[:, picks : 2 * picks]
+            - shares(stats[:, 0], teacher_total) * d_parts[:, :picks],
+            axis=0,
+        )
+    d_final_first = lax.ppermute(d_final, "pair", to_student)
+    d_final = (jnp.concatenate([d_final_first, d_final], axis=0) - aims) * (1.0 / total_rows)
+    teacher_total, own_total, d_final_first = tied(teacher_total, own_total, d_final_first)
+    teacher_total, own_total = teacher_total[:, None], own_total[:, None]
     teacher_log = teacher_logits - teacher_total
     teacher_prob = jnp.exp(teacher_log)
     own_log = logits - own_total
@@ -1010,19 +1149,9 @@
     target_hit = (targets - me * vocab_rows)[:, None] == vocab_iota[None, :]
     d_logits = (2.0 * own_prob - target_hit.astype(wide) - teacher_prob) * (1.0 / total_rows)
     d_low = d_logits.astype(low)
-    d_final_parts = dot_plain(d_low, table_low).astype(low).reshape(devices, picks, width)
-    d_final_parts, x_over[2] = tied(d_final_parts, x_over[2])
-    d_final_parts = lax.all_to_all(d_final_parts, "dp", split_axis=0, concat_axis=0, tiled=True)
-    d_final = jnp.sum(d_final_parts.astype(wide), axis=0)
-    d_final_first = lax.ppermute(d_final, "pair", to_student)
-    d_final = jnp.concatenate([d_final_first, d_final], axis=0)
-
-    d_final, rows_sent = tied(d_final, student_rows)
-    rows_other = lax.ppermute(rows_sent, "pair", swap)
-    d_mid, d_attended, g_vecs, rights = run_upper(d_final, vec, (mid, pre, top), whole)
-    d_mid, rows_other = tied(d_mid, rows_other)
-    passed = jnp.concatenate([d_mid, d_attended.astype(wide)], axis=1)
-    passed = jnp.where(is_student, passed[picks:], over(passed[:picks]))
+    passed_first, passed_last, g_vecs, rights = run_upper(d_final, vec, (mid, pre, top), whole)
+    passed_there, d_low = tied(over(passed_first), d_low)
+    passed = jnp.where(is_student, passed_last, passed_there)
     x_last = jnp.concatenate([x_embed[1], queries[picks:].astype(wide), vec], axis=0)
     x_last = jnp.where(is_student, x_last, jnp.concatenate(x_over, axis=0))
     sent, g_attn, g_vecs, g_pos = run_lower(
@@ -1039,6 +1168,8 @@
         near,
         devices,
     )
+    sent, rows_sent, d_low_sent = tied(sent, student_rows, d_low)
+    rows_other = lax.ppermute(rows_sent, "pair", swap)
     arrived = lax.all_to_all(sent, "dp", split_axis=0, concat_axis=0, tiled=True)
     arrived = arrived.reshape(slot_count, width)
 
@@ -1050,13 +1181,12 @@
         shared = jnp.concatenate([g_attn, g_vecs, parts], axis=1)
     else:
         shared = g_attn
-    d_low_sent = d_low
     if devices % 2:
         shared = lax.psum_scatter(shared, "dp", scatter_dimension=0, tiled=True)
     else:
         chips = shared.reshape(devices // 2, 2, rows, -1)
         near_sum = across(lax.dynamic_index_in_dim(chips, 1 - core, 1, keepdims=False))
-        near_sum, d_low_sent = tied(near_sum, d_low)
+        near_sum, rows_other = tied(near_sum, rows_other)
         mine = lax.dynamic_index_in_dim(chips, core, 1, keepdims=False)
         chips = (mine.astype(wide) + near_sum.astype(wide)).astype(low)
     d_low_other = lax.ppermute(d_low_sent, "pair", swap)
@@ -1117,15 +1247,12 @@
     table_squares, products_there, shared_other = tied(
         table_squares, products_there, shared_other
     )
-    shared = shared.astype(wide) + shared_other.astype(wide)
-    squares = squares + jnp.sum(shared * shared) + jnp.sum(table_squares)
-    lane = jnp.arange(LANES, dtype=jnp.int32)[None, :]
-    totals = to_all(
-        jnp.where(lane == 0, squares, jnp.where(lane == 1, kl_local, 0.0)), ("pair", "dp")
-    )
+    shared, note = run_norm(squares, table_squares, shared, shared_other, kl_local, 2 * devices)
+    totals = lax.all_to_all(note, ("pair", "dp"), split_axis=0, concat_axis=0, tiled=True)
     grad_norm = jnp.sqrt(jnp.sum(totals[devices:, 0, 0]))
     kl_mean = jnp.sum(totals[:, 0, 1]) / total_rows
     factor = jnp.minimum(1.0, clip_limit / (grad_norm + 1e-06))
+    factor, pos_near = tied(factor, pos_near)
     table_out = adam_update(table, table_m, table_v, g_table, factor)
     products = jnp.where(is_student, products, products_there).astype(wide)
     g_mlp_out, g_attn_out = products[:fold_rows], products[fold_rows + 4 * rows :]

time: 552 us -> 542 us (0.982)
  waiting for transfers between devices: 173 us -> 201 us
  local copies, waits for them, and re-layouts: 76.9 us -> 59.8 us
  blocking collectives: 38.9 us -> 25.7 us
  other arithmetic: 55.6 us -> 47.5 us
    ppermute x1, waiting for transfers between devices: 4.45 us -> 34.1 us  [ring_gather(): first = lax.ppermute(ahead[:half_rows], 'dp', onward)]
    ppermute x1, starting transfers between devices: 17.6 us -> 0.06 us  [ring_gather(): first = lax.ppermute(ahead[:half_rows], 'dp', onward)]
    all_to_all x1, starting transfers between devices: 4.21 us -> 20.8 us  [shards(): lefts = lax.all_to_all(lefts, 'dp', split_axis=0, concat_axis=0, tiled=True)]
    all_to_all x1 -> x0, blocking collectives: 14.8 us -> none  [shards(): lax.all_to_all(d_final_parts, 'dp', split_axis=0, concat_axis=0, tiled=True)]
    dynamic_update_slice x8, local copies, waits for them, and re-layouts: 10.9 us -> 1.9 us  [keep(): lax.dynamic_update_slice(whole, partner[None], (piece_slot(k + 1, devices...]
    all_gather x1, waiting for transfers between devices: 15.1 us -> 23.6 us  [shards(): rights = lax.all_gather(rights, 'dp', axis=0, tiled=True)]
    unnamed x62 -> x79, local copies, waits for them, and re-layouts: 3.91 us -> 12.4 us
    ppermute x11 -> x10, waiting for transfers between devices: 30.5 us -> 39 us  [over(): return lax.ppermute(value, 'pair', to_teacher)]
  transfers between devices with their start and end apart: 46 -> 45, of which waited for: 22 -> 21; matrix products, arithmetic and copies ran while one was open for 27% -> 20% of each run, Pallas kernels for 6% -> 7%
where the time goes in v4:
time: 542 us; the launch traced here: 533 us
  waiting for transfers between devices  201 us (37%)
  starting transfers between devices  86.8 us (16%)
  Pallas kernels  72.1 us (13%)
  local copies, waits for them, and re-layouts  59.8 us (11%)
  other arithmetic  47.5 us (9%)
  blocking collectives  25.7 us (5%)
  between operations  21.2 us (4%)
  matrix products  18.9 us (3%)
    all_to_all x1, waiting for transfers between devices, shards(): lax.all_to_all(chips, 'dp', split_axis=0, concat_axis=0, axis_index_group...  44.5 us
    ppermute x10, waiting for transfers between devices, over(): return lax.ppermute(value, 'pair', to_teacher)  39 us
    ppermute x1, waiting for transfers between devices, ring_gather(): first = lax.ppermute(ahead[:half_rows], 'dp', onward)  34.1 us
    ppermute x3, waiting for transfers between devices, step(): lax.ppermute(ahead, 'dp', onward)  29.7 us
    all_gather x1, blocking collectives, shards(): every = lax.all_gather(both.reshape(2 * picks, width), 'dp', axis=0)  25.7 us
    sub x1, other arithmetic, adam_update(): master - learn_rate * (fixed_one / (jnp.sqrt(fixed_two) + adam_eps) + dec...  24.4 us
    all_gather x1, waiting for transfers between devices, shards(): rights = lax.all_gather(rights, 'dp', axis=0, tiled=True)  23.6 us
    all_to_all x1, starting transfers between devices, shards(): lefts = lax.all_to_all(lefts, 'dp', split_axis=0, concat_axis=0, tiled=True)  20.8 us
  transfers between devices with their start and end apart: 45, of which 21 were waited for; matrix products, arithmetic and copies ran while one was open for 20% of the time, Pallas kernels for 7%

profile of v4, /device:TPU:0, one launch (start us, length us, event | category | flops | bytes accessed | tf_op | source)
XLA Modules:
  0.0 533.5 jit_solution(3061068225070600178)
XLA Ops:
  8.9 4.3 route_tokens.1
  14.6 7.4 %all-to-all-start = ((s32[16,1,160]{2,1,0:T(1,128)}), s32[16,1,160]{2,1,0:T(1,128)S(1)}, u32[]{:S(2)}, u32[]{:S(2)}) async-start(s32[16,1,160]{2,1,0:T(1,128)} %copy.72), calls=%async_computation | async-start | bytes 32768 | tf_op jit(solution)/shard_map/all_to_all | solution.py:1009
  22.0 6.5 %all-to-all-done = s32[16,1,160]{2,1,0:T(1,128)S(1)} async-done(((s32[16,1,160]{2,1,0:T(1,128)}), s32[16,1,160]{2,1,0:T(1,128)S(1)}, u32[]{:S(2)}, u32[]{:S(2)}) %all-to-all-start) | async-done | bytes 10272 | tf_op jit(solution)/shard_map/all_to_all | solution.py:1009
  34.2 13.4 %conditional.1 = (bf16[16,128,768]{2,1,0:T(8,128)(2,1)}) conditional(s32[]{:T(128)} %convert_element_type.96, (s32[16,128]{1,0:T(8,128)S(1)}, bf16[3144,768]{1,0:T(8,128)(2,1)}) %tuple.35, (s32[16,128]{1,0:T(8,128)S(1)}, f32[3144,768]{1,0:T(8,128)}) %tuple.36), branch_computations={%region_0.1_spmd, %region_1.0_spmd} | conditional | flops 1593344 | bytes 12619784 | solution.py:1028
  34.2 11.5 %gather_fusion = bf16[2048,768]{1,0:T(8,128)(2,1)S(1)} fusion(bf16[3144,768]{1,0:T(8,128)(2,1)} %get-tuple-element.12, s32[2048]{0:T(1024)S(1)} %bitcast_clamp_fusion), kind=kCustom, calls=%fused_computation | custom fusion | bytes 6299648 | tf_op jit(solution)/shard_map/cond/branch_0_fun/jit(_take)/gather | solution.py:1031
  47.6 8.2 %collective-permute-done = bf16[656,768]{1,0:T(8,128)(2,1)} collective-permute-done((bf16[656,768]{1,0:T(8,128)(2,1)}, bf16[656,768]{1,0:T(8,128)(2,1)}, u32[]{:S(2)}, u32[]{:S(2)}) %collective-permute-start) | collective-permute-done | bytes 1007648 | tf_op jit(solution)/shard_map/ppermute | solution.py:93
  58.4 21.4 %collective-permute-done.2 = bf16[656,768]{1,0:T(8,128)(2,1)} collective-permute-done((bf16[656,768]{1,0:T(8,128)(2,1)}, bf16[656,768]{1,0:T(8,128)(2,1)}, u32[]{:S(2)}, u32[]{:S(2)}) %collective-permute-start.2) | collective-permute-done | bytes 1007648 | tf_op jit(solution)/shard_map/ppermute | solution.py:93
  82.1 3.7 all-to-all-start.1
  96.3 4.0 collective-permute-done.11
  105.1 3.9 collective-permute-done.13
  109.5 6.0 %collective-permute-done.10 = bf16[656,768]{1,0:T(8,128)(2,1)} collective-permute-done((bf16[656,768]{1,0:T(8,128)(2,1)}, bf16[656,768]{1,0:T(8,128)(2,1)}, u32[]{:S(2)}, u32[]{:S(2)}) %collective-permute-start.10) | collective-permute-done | bytes 1007648 | tf_op jit(solution)/shard_map/ppermute | solution.py:93
  130.3 34.1 %collective-permute-done.16 = bf16[320,768]{1,0:T(8,128)(2,1)S(1)} collective-permute-done((bf16[320,768]{1,0:T(8,128)(2,1)S(1)}, bf16[320,768]{1,0:T(8,128)(2,1)S(1)}, u32[]{:S(2)}, u32[]{:S(2)}) %collective-permute-start.16) | collective-permute-done | bytes 491552 | tf_op jit(solution)/shard_map/ppermute | solution.py:110
  169.8 5.5 %copy-done.13 = bf16[16,656,768]{2,1,0:T(8,128)(2,1)} copy-done((bf16[16,656,768]{2,1,0:T(8,128)(2,1)}, bf16[16,656,768]{2,1,0:T(8,128)(2,1)S(1)}, u32[]{:S(2)}) %copy-start.13) | copy-done | bytes 16121880
  177.3 15.3 %layer_forward.1 = (bf16[16,768]{1,0:T(8,128)(2,1)}, bf16[16,768]{1,0:T(8,128)(2,1)S(1)}, f32[32,768]{1,0:T(8,128)S(1)}, f32[2,512,768]{2,1,0:T(8,128)S(1)}, bf1...) custom-call(s32[1]{0:T(128)} %bitcast.4.flag_ref.refs_0_, ...), custom_call_target="tpu_custom_call" | custom-call | flops 1500000000 | bytes 51000000 | tf_op jit(solution)/shard_map/layer_forward/pallas_call | solution.py:340
  196.4 20.8 %all-to-all-start.2 = ((bf16[16,32,288]{2,1,0:T(8,128)(2,1)}), bf16[16,32,288]{2,1,0:T(8,128)(2,1)S(1)}, u32[]{:S(2)}, u32[]{:S(2)}) async-start(bf16[16,32,288]{2,1,0:T(8,128)(2,1)} %copy-done.4), calls=%async_computation.2 | async-start | bytes 786432 | tf_op jit(solution)/shard_map/all_to_all | solution.py:1083
  221.6 25.7 %all_gather.12 = bf16[16,32,768]{2,1,0:T(8,128)(2,1)} all-gather(bf16[1,32,768]{2,1,0:T(8,128)(2,1)S(1)} %bitcast.162), channel_id=1, replica_groups=mesh['pair'=2,'dp'=16] {'dp'}, dimensions={0}, use_global_device_ids=true | all-gather | bytes 835584 | tf_op jit(solution)/shard_map/all_gather | solution.py:1078
  250.0 5.5 %fusion.39 = (f32[256]{0:T(256)S(1)}, f32[256,3144]{0,1:T(8,128)S(1)}) fusion(bf16[256,768]{1,0:T(8,128)(2,1)S(1)} %bitcast.147, f32[3144,768]{1,0:T(8,128)} %param.45), kind=kOutput, calls=%fused_computation.125 | convolution fusion | flops 1239490304 | bytes 13272064 | tf_op jit(solution)/shard_map/dot_general | solution.py:55
  264.1 3.6 all-to-all-start.3
  269.1 27.2 %collective-permute-done.24 = f32[352,768]{1,0:T(8,128)} collective-permute-done((f32[352,768]{1,0:T(8,128)}, f32[352,768]{1,0:T(8,128)}, u32[]{:S(2)}, u32[]{:S(2)}) %collective-permute-start.24) | collective-permute-done | bytes 1081376 | tf_op jit(solution)/shard_map/ppermute | solution.py:1035
  300.2 6.7 %upper_backward.1 = (f32[16,1536]{1,0:T(8,128)S(1)}, f32[16,1536]{1,0:T(8,128)S(1)}, f32[16,768]{1,0:T(8,128)S(1)}, bf16[32,4608]{1,0:T(8,128)(2,1)}) custom-call(f32[32,768]{1,0:T(8,128)S(1)} %fusion.25.d_final_ref, f32[16,768]{1,0:T(8,128)S(1)} %reshape.385.vec_ref, f32[32,768]{1,0:T(8,128)S(1)} %get-tuple-element.170.mid_ref, f32[32,3072]{1,0:T(8,128)S(1)} %copy-done.6, ...), custom_call_target="tpu_custom_call" | custom-call | flops 900000000 | bytes 30600000 | tf_op jit(solution)/shard_map/upper_backward/pallas_call | solution.py:560
  317.0 16.4 %lower_backward.1 = (bf16[16,64,768]{2,1,0:T(8,128)(2,1)}, bf16[768,2688]{1,0:T(8,128)(2,1)}, f32[16,768]{1,0:T(8,128)}, f32[8,768]{1,0:T(8,128)}) custom-call(s32[1]{0:T(128)} %bitcast.4.flag_ref.refs_0_, f32[16,768]{1,0:T(8,128)S(1)} %slice.199.d_mid_ref, bf16[16,768]{1,0:T(8,128)(2,1)S(1)} %slice.248.d_attended_ref, ...), custom_call_target="tpu_custom_call" | custom-call | flops 1500000000 | bytes 51000000 | tf_op jit(solution)/shard_map/lower_backward/pallas_call | solution.py:591
  336.6 6.2 %all-to-all-start.4 = ((bf16[16,64,768]{2,1,0:T(8,128)(2,1)}), bf16[16,64,768]{2,1,0:T(8,128)(2,1)S(1)}, u32[]{:S(2)}, u32[]{:S(2)}) async-start(bf16[16,64,768]{2,1,0:T(8,128)(2,1)} %get-tuple-element.186), calls=%async_computation.4 | async-start | bytes 3145728 | tf_op jit(solution)/shard_map/all_to_all | solution.py:1173
  344.9 10.2 %collective-permute-done.31.refs_4_ = bf16[256,768]{1,0:T(8,128)(2,1)} collective-permute-done((bf16[256,768]{1,0:T(8,128)(2,1)}, bf16[256,768]{1,0:T(8,128)(2,1)}, u32[]{:S(2)}, u32[]{:S(2)}) %collective-permute-start.31) | collective-permute-done | bytes 393248 | tf_op jit(solution)/shard_map/ppermute | solution.py:1172
  355.1 4.0 fusion.1
  359.1 23.6 %all-gather.4.cloned.1.call-done = bf16[512,4608]{1,0:T(8,128)(2,1)} async-done(((bf16[32,4608]{1,0:T(8,128)(2,1)}), bf16[512,4608]{1,0:T(8,128)(2,1)}) %all-gather.4.cloned.1.call-update) | async-done | bytes 4718608 | tf_op jit(solution)/shard_map/all_gather | solution.py:1194
  396.2 3.6 all-to-all-start.5
  399.9 3.6 collective-permute-start.32
  403.5 44.5 %all-to-all-done.5 = bf16[8,48,2688]{2,1,0:T(8,128)(2,1)S(1)} async-done(((bf16[8,48,2688]{2,1,0:T(8,128)(2,1)}), bf16[8,48,2688]{2,1,0:T(8,128)(2,1)S(1)}, u32[]{:S(2)}, u32[]{:S(2)}) %all-to-all-start.5) | async-done | bytes 2064416 | tf_op jit(solution)/shard_map/all_to_all | solution.py:1214
  455.2 17.9 %table_gradient.1 = (f32[3144,768]{1,0:T(8,128)}, f32[8,768]{1,0:T(8,128)}) custom-call(s32[1]{0:T(128)} %bitcast.4.flag_ref.refs_0_, bf16[3144,256]{1,0:T(8,128)(2,1)} %bitcast.142, bf16[256,768]{1,0:T(8,128)(2,1)} %bitcast.149, bf16[3144,256]{1,0:T(8,128)(2,1)} %bitcast.62.refs_3_, bf16[256,768]{1,0:T(8,128)(2,1)} %collective-permute-done.31.refs_4_, ...), custom_call_target="tpu_custom_call" | custom-call | flops 1700000000 | bytes 57800000 | tf_op jit(solution)/shard_map/table_gradient/pallas_call | solution.py:886
  476.0 3.6 all-to-all-start.6
  492.5 24.4 %multiply_subtract_fusion = (f32[3144,768]{1,0:T(8,128)}, f32[3144,768]{1,0:T(8,128)}, f32[3144,768]{1,0:T(8,128)}) fusion(f32[3144,768]{1,0:T(8,128)} %param.45, f32[3144,768]{1,0:T(8,128)} %get-tuple-element.202, f32[]{:T(128)} %min_shard_map.3, f32[3144,768]{1,0:T(8,128)} %param.52, f32[3144,768]{1,0:T(8,128)} %param.59), kind=kLoop, calls=%fused_computation.12 | loop fusion | flops 38633472 | bytes 67608576 | tf_op jit(solution)/shard_map/sub | solution.py:138
  517.6 6.3 %small_updates.1 = (f32[64,768]{1,0:T(8,128)}, f32[64,768]{1,0:T(8,128)}, f32[64,768]{1,0:T(8,128)}, f32[48,2304]{1,0:T(8,128)}, f32[48,2304]{1,0:T(8,128)}, /*i...) custom-call(f32[1]{0:T(128)} %bitcast.73.factor_ref, ...), custom_call_target="tpu_custom_call" | custom-call | flops 600000000 | bytes 20400000 | tf_op jit(solution)/shard_map/small_updates/pallas_call | solution.py:940
  (257 shorter events, 126.4 us)
Async XLA Ops:
  14.6 13.9 %all-to-all-start = ((s32[16,1,160]{2,1,0:T(1,128)}), s32[16,1,160]{2,1,0:T(1,128)S(1)}, u32[]{:S(2)}, u32[]{:S(2)}) async-start(s32[16,1,160]{2,1,0:T(1,128)} %copy.72), calls=%async_computation | async-start | bytes 32768 | tf_op jit(solution)/shard_map/all_to_all | solution.py:1009
  31.5 24.3 %collective-permute-start = (bf16[656,768]{1,0:T(8,128)(2,1)}, bf16[656,768]{1,0:T(8,128)(2,1)}, u32[]{:S(2)}, u32[]{:S(2)}) collective-permute-start(bf16[656,768]{1,0:T(8,128)(2,1)} %pack_weights.1), channel_id=1, source_target_pairs={{0,4},{1,5},{4,8},{5,9},{8,12},{9,13},{12,14},{13,15},{14,10},{15,... | collective-permute-start | bytes 3022856 | tf_op jit(solution)/shard_map/ppermute | solution.py:93
  32.0 24.3 %collective-permute-start.1 = (bf16[656,768]{1,0:T(8,128)(2,1)}, bf16[656,768]{1,0:T(8,128)(2,1)}, u32[]{:S(2)}, u32[]{:S(2)}) collective-permute-start(bf16[656,768]{1,0:T(8,128)(2,1)} %pack_weights.1), channel_id=1, source_target_pairs={{4,0},{5,1},{8,4},{9,5},{12,8},{13,9},{14,12},{15,13},{10,14},{11,... | collective-permute-start | bytes 3022856 | tf_op jit(solution)/shard_map/ppermute | solution.py:93
  56.3 23.5 %collective-permute-start.2 = (bf16[656,768]{1,0:T(8,128)(2,1)}, bf16[656,768]{1,0:T(8,128)(2,1)}, u32[]{:S(2)}, u32[]{:S(2)}) collective-permute-start(bf16[656,768]{1,0:T(8,128)(2,1)} %collective-permute-done), channel_id=1, source_target_pairs={{0,4},{1,5},{4,8},{5,9},{8,12},{9,13},{12,14},{13,15},{14,10},{15,... | collective-permute-start | bytes 3022856 | tf_op jit(solution)/shard_map/ppermute | solution.py:93
  56.9 23.2 %collective-permute-start.3 = (bf16[656,768]{1,0:T(8,128)(2,1)}, bf16[656,768]{1,0:T(8,128)(2,1)}, u32[]{:S(2)}, u32[]{:S(2)}) collective-permute-start(bf16[656,768]{1,0:T(8,128)(2,1)} %collective-permute-done.1), channel_id=1, source_target_pairs={{4,0},{5,1},{8,4},{9,5},{12,8},{13,9},{14,12},{15,13},{10,14},{11,... | collective-permute-start | bytes 3022856 | tf_op jit(solution)/shard_map/ppermute | solution.py:93
  80.1 28.9 %collective-permute-start.9 = (bf16[656,768]{1,0:T(8,128)(2,1)}, bf16[656,768]{1,0:T(8,128)(2,1)}, u32[]{:S(2)}, u32[]{:S(2)}) collective-permute-start(bf16[656,768]{1,0:T(8,128)(2,1)} %collective-permute-done.2), channel_id=1, source_target_pairs={{0,4},{1,5},{4,8},{5,9},{8,12},{9,13},{12,14},{13,15},{14,10},{15,... | collective-permute-start | bytes 3022856 | tf_op jit(solution)/shard_map/ppermute | solution.py:93
  80.7 34.8 %collective-permute-start.10 = (bf16[656,768]{1,0:T(8,128)(2,1)}, bf16[656,768]{1,0:T(8,128)(2,1)}, u32[]{:S(2)}, u32[]{:S(2)}) collective-permute-start(bf16[656,768]{1,0:T(8,128)(2,1)} %collective-permute-done.3), channel_id=1, source_target_pairs={{4,0},{5,1},{8,4},{9,5},{12,8},{13,9},{14,12},{15,13},{10,14},{11,... | collective-permute-start | bytes 3022856 | tf_op jit(solution)/shard_map/ppermute | solution.py:93
  82.1 93.4 %all-to-all-start.1 = ((bf16[16,128,768]{2,1,0:T(8,128)(2,1)}), bf16[16,128,768]{2,1,0:T(8,128)(2,1)S(1)}, u32[]{:S(2)}, u32[]{:S(2)}) async-start(bf16[16,128,768]{2,1,0:T(8,128)(2,1)} %get-tuple-element.268), calls=%async_computation.1 | async-start | bytes 6291456 | tf_op jit(solution)/shard_map/all_to_all | solution.py:1052
  86.9 32.1 %collective-permute-start.5 = (bf16[656,768]{1,0:T(8,128)(2,1)}, bf16[656,768]{1,0:T(8,128)(2,1)S(1)}, u32[]{:S(2)}, u32[]{:S(2)}) collective-permute-start(bf16[656,768]{1,0:T(8,128)(2,1)} %collective-permute-done), channel_id=1, source_target_pairs={{0,1},{1,0},{2,3},{3,2},{4,5},{5,4},{6,7},{7,6},{8,9},{9,8},{10,11... | collective-permute-start | bytes 3022856 | tf_op jit(solution)/shard_map/ppermute | solution.py:88
  105.1 16.6 %collective-permute-start.6 = (bf16[656,768]{1,0:T(8,128)(2,1)}, bf16[656,768]{1,0:T(8,128)(2,1)S(1)}, u32[]{:S(2)}, u32[]{:S(2)}) collective-permute-start(bf16[656,768]{1,0:T(8,128)(2,1)} %collective-permute-done.1), channel_id=1, source_target_pairs={{0,1},{1,0},{2,3},{3,2},{4,5},{5,4},{6,7},{7,6},{8,9},{9,8},{10,11... | collective-permute-start | bytes 3022856 | tf_op jit(solution)/shard_map/ppermute | solution.py:88
  109.0 14.2 %collective-permute-start.7 = (bf16[656,768]{1,0:T(8,128)(2,1)}, bf16[656,768]{1,0:T(8,128)(2,1)S(1)}, u32[]{:S(2)}, u32[]{:S(2)}) collective-permute-start(bf16[656,768]{1,0:T(8,128)(2,1)} %collective-permute-done.2), channel_id=1, source_target_pairs={{0,1},{1,0},{2,3},{3,2},{4,5},{5,4},{6,7},{7,6},{8,9},{9,8},{10,11... | collective-permute-start | bytes 3022856 | tf_op jit(solution)/shard_map/ppermute | solution.py:88
  109.0 16.1 %collective-permute-start.8 = (bf16[656,768]{1,0:T(8,128)(2,1)}, bf16[656,768]{1,0:T(8,128)(2,1)S(1)}, u32[]{:S(2)}, u32[]{:S(2)}) collective-permute-start(bf16[656,768]{1,0:T(8,128)(2,1)} %collective-permute-done.3), channel_id=1, source_target_pairs={{0,1},{1,0},{2,3},{3,2},{4,5},{5,4},{6,7},{7,6},{8,9},{9,8},{10,11... | collective-permute-start | bytes 3022856 | tf_op jit(solution)/shard_map/ppermute | solution.py:88
  121.7 45.4 %collective-permute-start.14 = (bf16[656,768]{1,0:T(8,128)(2,1)}, bf16[656,768]{1,0:T(8,128)(2,1)S(1)}, u32[]{:S(2)}, u32[]{:S(2)}) collective-permute-start(bf16[656,768]{1,0:T(8,128)(2,1)} %collective-permute-done.9), channel_id=1, source_target_pairs={{0,1},{1,0},{2,3},{3,2},{4,5},{5,4},{6,7},{7,6},{8,9},{9,8},{10,11... | collective-permute-start | bytes 3022856 | tf_op jit(solution)/shard_map/ppermute | solution.py:88
  123.2 45.3 %collective-permute-start.15 = (bf16[656,768]{1,0:T(8,128)(2,1)}, bf16[656,768]{1,0:T(8,128)(2,1)S(1)}, u32[]{:S(2)}, u32[]{:S(2)}) collective-permute-start(bf16[656,768]{1,0:T(8,128)(2,1)} %collective-permute-done.10), channel_id=1, source_target_pairs={{0,1},{1,0},{2,3},{3,2},{4,5},{5,4},{6,7},{7,6},{8,9},{9,8},{10,11... | collective-permute-start | bytes 3022856 | tf_op jit(solution)/shard_map/ppermute | solution.py:88
  125.1 39.3 %collective-permute-start.16 = (bf16[320,768]{1,0:T(8,128)(2,1)S(1)}, bf16[320,768]{1,0:T(8,128)(2,1)S(1)}, u32[]{:S(2)}, u32[]{:S(2)}) collective-permute-start(bf16[320,768]{1,0:T(8,128)(2,1)S(1)} %slice.149), channel_id=1, source_target_pairs={{0,4},{1,5},{4,8},{5,9},{8,12},{9,13},{12,14},{13,15},{14,10},{15,... | collective-permute-start | bytes 1474568 | tf_op jit(solution)/shard_map/ppermute | solution.py:110
  127.7 39.3 %collective-permute-start.17 = (bf16[336,768]{1,0:T(8,128)(2,1)S(1)}, bf16[336,768]{1,0:T(8,128)(2,1)S(1)}, u32[]{:S(2)}, u32[]{:S(2)}) collective-permute-start(bf16[336,768]{1,0:T(8,128)(2,1)S(1)} %slice.150), channel_id=1, source_target_pairs={{4,0},{5,1},{8,4},{9,5},{12,8},{13,9},{14,12},{15,13},{10,14},{11,... | collective-permute-start | bytes 1548296 | tf_op jit(solution)/shard_map/ppermute | solution.py:111
  194.9 24.1 %collective-permute-start.19 = (bf16[16,768]{1,0:T(8,128)(2,1)}, bf16[16,768]{1,0:T(8,128)(2,1)S(1)}, u32[]{:S(2)}, u32[]{:S(2)}) collective-permute-start(bf16[16,768]{1,0:T(8,128)(2,1)} %get-tuple-element.152), channel_id=1, source_target_pairs={{0,16},{16,0},{1,17},{17,1},{2,18},{18,2},{3,19},{19,3},{4,20},{20... | collective-permute-start | bytes 73736 | tf_op jit(solution)/shard_map/ppermute | solution.py:1065
  196.4 50.9 %all-to-all-start.2 = ((bf16[16,32,288]{2,1,0:T(8,128)(2,1)}), bf16[16,32,288]{2,1,0:T(8,128)(2,1)S(1)}, u32[]{:S(2)}, u32[]{:S(2)}) async-start(bf16[16,32,288]{2,1,0:T(8,128)(2,1)} %copy-done.4), calls=%async_computation.2 | async-start | bytes 786432 | tf_op jit(solution)/shard_map/all_to_all | solution.py:1083
  218.9 28.3 %collective-permute-start.20 = (f32[192,768]{1,0:T(8,128)}, f32[192,768]{1,0:T(8,128)S(1)}, u32[]{:S(2)}, u32[]{:S(2)}) collective-permute-start(f32[192,768]{1,0:T(8,128)} %slice_bitcast_fusion.2), channel_id=1, source_target_pairs={{16,0},{17,1},{18,2},{19,3},{20,4},{21,5},{22,6},{23,7},{24,8},{25... | collective-permute-start | bytes 1769480 | tf_op jit(solution)/shard_map/ppermute | solution.py:1035
  220.2 42.7 %collective-permute-start.23 = (bf16[3,144,768]{2,1,0:T(8,128)(2,1)}, bf16[3,144,768]{2,1,0:T(8,128)(2,1)S(1)}, u32[]{:S(2)}, u32[]{:S(2)}) collective-permute-start(bf16[3,144,768]{2,1,0:T(8,128)(2,1)} %pad_maximum_fusion.4), channel_id=1, source_target_pairs={{16,0},{17,1},{18,2},{19,3},{20,4},{21,5},{22,6},{23,7},{24,8},{25... | collective-permute-start | bytes 1990664 | tf_op jit(solution)/shard_map/ppermute | solution.py:1035
  264.1 32.2 %all-to-all-start.3 = ((bf16[16,36,768]{2,1,0:T(8,128)(2,1)}), bf16[16,36,768]{2,1,0:T(8,128)(2,1)S(1)}, u32[]{:S(2)}, u32[]{:S(2)}) async-start(bf16[16,36,768]{2,1,0:T(8,128)(2,1)} %pad_maximum_fusion.3), calls=%async_computation.3 | async-start | bytes 1966080 | tf_op jit(solution)/shard_map/all_to_all | solution.py:1114
  267.8 114.9 %all-gather.4.cloned.1.call-start = ((), (), s32[]{:S(2)}) async-start(), calls=%async_computation.7 | async-start | bytes 5013504 | tf_op jit(solution)/shard_map/all_gather | solution.py:1194
  267.8 28.5 %collective-permute-start.24 = (f32[352,768]{1,0:T(8,128)}, f32[352,768]{1,0:T(8,128)}, u32[]{:S(2)}, u32[]{:S(2)}) collective-permute-start(f32[352,768]{1,0:T(8,128)} %pad_maximum_fusion.1), channel_id=1, source_target_pairs={{16,0},{17,1},{18,2},{19,3},{20,4},{21,5},{22,6},{23,7},{24,8},{25... | collective-permute-start | bytes 3244040 | tf_op jit(solution)/shard_map/ppermute | solution.py:1035
  336.6 18.5 %collective-permute-start.30 = (bf16[8,48,2688]{2,1,0:T(8,128)(2,1)}, bf16[8,48,2688]{2,1,0:T(8,128)(2,1)}, u32[]{:S(2)}, u32[]{:S(2)}) collective-permute-start(bf16[8,48,2688]{2,1,0:T(8,128)(2,1)} %dynamic-slice_bitcast_fusion), channel_id=1, source_target_pairs={{0,1},{1,0},{2,3},{3,2},{4,5},{5,4},{6,7},{7,6},{8,9},{9,8},{10,11... | collective-permute-start | bytes 6193160 | tf_op jit(solution)/shard_map/ppermute | solution.py:1062
  336.6 58.4 %all-to-all-start.4 = ((bf16[16,64,768]{2,1,0:T(8,128)(2,1)}), bf16[16,64,768]{2,1,0:T(8,128)(2,1)S(1)}, u32[]{:S(2)}, u32[]{:S(2)}) async-start(bf16[16,64,768]{2,1,0:T(8,128)(2,1)} %get-tuple-element.186), calls=%async_computation.4 | async-start | bytes 3145728 | tf_op jit(solution)/shard_map/all_to_all | solution.py:1173
  342.9 52.1 %collective-permute-start.29 = (bf16[256,3144]{0,1:T(8,128)(2,1)S(1)}, bf16[256,3144]{0,1:T(8,128)(2,1)}, u32[]{:S(2)}, u32[]{:S(2)}) collective-permute-start(bf16[256,3144]{0,1:T(8,128)(2,1)S(1)} %copy-done.18), channel_id=1, source_target_pairs={{0,16},{16,0},{1,17},{17,1},{2,18},{18,2},{3,19},{19,3},{4,20},{20... | collective-permute-start | bytes 4829192 | tf_op jit(solution)/shard_map/ppermute | solution.py:1192
  396.2 51.8 %all-to-all-start.5 = ((bf16[8,48,2688]{2,1,0:T(8,128)(2,1)}), bf16[8,48,2688]{2,1,0:T(8,128)(2,1)S(1)}, u32[]{:S(2)}, u32[]{:S(2)}) async-start(bf16[8,48,2688]{2,1,0:T(8,128)(2,1)} %fusion.1), calls=%async_computation.5 | async-start | bytes 4128768 | tf_op jit(solution)/shard_map/all_to_all | solution.py:1214
  399.8 90.1 %all-gather.6.cloned.1.call-start = ((), (), s32[]{:S(2)}) async-start(), calls=%async_computation.8 | async-start | bytes 1671168 | tf_op jit(solution)/shard_map/all_gather | solution.py:1236
  399.9 49.1 %collective-permute-start.32 = (bf16[1024,768]{1,0:T(8,128)(2,1)}, bf16[1024,768]{1,0:T(8,128)(2,1)}, u32[]{:S(2)}, u32[]{:S(2)}) collective-permute-start(bf16[1024,768]{1,0:T(8,128)(2,1)} %bitcast.143), channel_id=1, source_target_pairs={{0,16},{16,0},{1,17},{17,1},{2,18},{18,2},{3,19},{19,3},{4,20},{20... | collective-permute-start | bytes 4718600 | tf_op jit(solution)/shard_map/ppermute | solution.py:1210
  449.0 24.6 %collective-permute-start.33 = (bf16[432,768]{1,0:T(8,128)(2,1)}, bf16[432,768]{1,0:T(8,128)(2,1)S(1)}, u32[]{:S(2)}, u32[]{:S(2)}) collective-permute-start(bf16[432,768]{1,0:T(8,128)(2,1)} %pad_maximum_fusion.5), channel_id=1, source_target_pairs={{16,0},{17,1},{18,2},{19,3},{20,4},{21,5},{22,6},{23,7},{24,8},{25... | collective-permute-start | bytes 1990664 | tf_op jit(solution)/shard_map/ppermute | solution.py:1035
  450.4 23.2 %collective-permute-start.34 = (bf16[48,2688]{1,0:T(8,128)(2,1)S(1)}, bf16[48,2688]{1,0:T(8,128)(2,1)S(1)}, u32[]{:S(2)}, u32[]{:S(2)}) collective-permute-start(bf16[48,2688]{1,0:T(8,128)(2,1)S(1)} %reduce_sum.89.mine_ref), channel_id=1, source_target_pairs={{0,16},{16,0},{1,17},{17,1},{2,18},{18,2},{3,19},{19,3},{4,20},{20... | collective-permute-start | bytes 774152 | tf_op jit(solution)/shard_map/ppermute | solution.py:1242
  491.0 25.9 %collective-permute-start.35 = (bf16[64,768]{1,0:T(8,128)(2,1)S(1)}, bf16[64,768]{1,0:T(8,128)(2,1)S(1)}, u32[]{:S(2)}, u32[]{:S(2)}) collective-permute-start(bf16[64,768]{1,0:T(8,128)(2,1)S(1)} %pad_dynamic-slice_fusion), channel_id=1, source_target_pairs={{0,16},{16,0},{1,17},{17,1},{2,18},{18,2},{3,19},{19,3},{4,20},{20... | collective-permute-start | bytes 294920 | tf_op jit(solution)/shard_map/ppermute | solution.py:1261
  (49 other events, 461.9 us)
Sparse Core Ops, SparseCore 0:
  307.0 75.6 all-gather.3
  449.1 40.6 all-gather.5

commit v5 on v4

--- a/solution.py
+++ b/solution.py
@@ -453,7 +453,8 @@
     *refs,
 ):
     there, near, rest = refs[:count], refs[count : 2 * count], refs[2 * count :]
-    sent_ref, g_attn_ref, g_vec_ref, g_pos_ref, w_ref, sems = rest
+    sent_ref, *outs, g_vec_ref, g_pos_ref, w_ref, sems = rest[:-1]
+    g_attn_ref = outs[0] if len(outs) == 1 else rest[-1]
     length, width = x_ref.shape
     devices, capacity, _ = sent_ref.shape
     slabs, share, _ = w_ref.shape
@@ -550,6 +551,12 @@
                 d * pos_share : (d + 1) * pos_share, k * part : (k + 1) * part
             ]
     g_pos_ref[...] = jnp.zeros(g_pos_ref.shape, wide)
+    core = lax.rem(lax.axis_index("dp"), 2)
+    held = width // devices
+    for k in range(devices // 2):
+        for out, side in zip(outs, (core, 1 - core)):
+            first = pl.multiple_of((2 * k + side) * held, 16)
+            out[k] = g_attn_ref[pl.ds(first, held), :]
 
 
 def run_upper(d_final, vec, kept, whole):
@@ -582,6 +589,10 @@
     width = vec.shape[1]
     capacity = 2 * length // devices
     loose = LONGEST // devices % 16
+    broad = 3 * width + (0 if loose else LANES + LONGEST)
+    outs = [jax.ShapeDtypeStruct((width, broad), low)]
+    if not loose:
+        outs = [jax.ShapeDtypeStruct((devices // 2, width // devices, broad), low)] * 2
     vmem = pl.BlockSpec(memory_space=pltpu.VMEM)
     hbm = pl.BlockSpec(memory_space=pl.ANY)
 
@@ -592,15 +603,16 @@
         functools.partial(lower_kernel, len(there)),
         out_shape=(
             shape((devices, capacity, width), low),
-            shape((width, 3 * width + (0 if loose else LANES + LONGEST)), low),
+            *outs,
             shape((16, width), wide),
             shape((LONGEST if loose else 8, width), wide),
         ),
         in_specs=[pl.BlockSpec(memory_space=pltpu.SMEM)] + [vmem] * 9 + [hbm] * (1 + 2 * len(there)),
-        out_specs=(vmem,) * 4,
+        out_specs=(vmem,) * (3 + len(outs)),
         scratch_shapes=[
             pltpu.VMEM((whole.shape[0], 3 * width // whole.shape[0], width), low),
             pltpu.SemaphoreType.DMA((whole.shape[0],)),
+            pltpu.VMEM((8, LANES) if loose else (width, broad), low),
         ],
         compiler_params=kernel_limit(44),
         cost_estimate=kernel_cost(15),
@@ -1076,7 +1088,7 @@
         ]
     )
     every = lax.all_gather(both.reshape(2 * picks, width), "dp", axis=0)
-    cuts = (0, 3 * length // 8, x_over.shape[0])
+    cuts = (0, 13 * length // 32, x_over.shape[0])
     x_over = [x_over[a:b] for a, b in zip(cuts, cuts[1:])]
     other_final, x_over[0] = tied(other_final, x_over[0])
     x_over[0] = over(x_over[0])
@@ -1154,7 +1166,7 @@
     passed = jnp.where(is_student, passed_last, passed_there)
     x_last = jnp.concatenate([x_embed[1], queries[picks:].astype(wide), vec], axis=0)
     x_last = jnp.where(is_student, x_last, jnp.concatenate(x_over, axis=0))
-    sent, g_attn, g_vecs, g_pos = run_lower(
+    sent, *halves, g_vecs, g_pos = run_lower(
         student_flag,
         (passed[:, :width], passed[:, width:].astype(low), jnp.where(is_student, g_vecs, 0.0)),
         cols[part],
@@ -1178,17 +1190,11 @@
         g_vecs = jnp.pad(g_vecs.T, ((0, 0), (0, LANES - g_vecs.shape[0]))).astype(low)
         parts = g_pos.reshape(devices, pos_share, -1, LONGEST).transpose(0, 2, 1, 3)
         parts = parts.reshape(width, LONGEST).astype(low)
-        shared = jnp.concatenate([g_attn, g_vecs, parts], axis=1)
-    else:
-        shared = g_attn
-    if devices % 2:
-        shared = lax.psum_scatter(shared, "dp", scatter_dimension=0, tiled=True)
-    else:
+        shared = jnp.concatenate([halves[0], g_vecs, parts], axis=1)
         chips = shared.reshape(devices // 2, 2, rows, -1)
-        near_sum = across(lax.dynamic_index_in_dim(chips, 1 - core, 1, keepdims=False))
-        near_sum, rows_other = tied(near_sum, rows_other)
-        mine = lax.dynamic_index_in_dim(chips, core, 1, keepdims=False)
-        chips = (mine.astype(wide) + near_sum.astype(wide)).astype(low)
+        halves = [lax.dynamic_index_in_dim(chips, c, 1, keepdims=False) for c in (core, 1 - core)]
+    near_sum, rows_other = tied(across(halves[1]), rows_other)
+    chips = (halves[0].astype(wide) + near_sum.astype(wide)).astype(low)
     d_low_other = lax.ppermute(d_low_sent, "pair", swap)
 
     rights = lax.all_gather(rights, "dp", axis=0, tiled=True)
@@ -1252,7 +1258,6 @@
     grad_norm = jnp.sqrt(jnp.sum(totals[devices:, 0, 0]))
     kl_mean = jnp.sum(totals[:, 0, 1]) / total_rows
     factor = jnp.minimum(1.0, clip_limit / (grad_norm + 1e-06))
-    factor, pos_near = tied(factor, pos_near)
     table_out = adam_update(table, table_m, table_v, g_table, factor)
     products = jnp.where(is_student, products, products_there).astype(wide)
     g_mlp_out, g_attn_out = products[:fold_rows], products[fold_rows + 4 * rows :]
@@ -1261,12 +1266,13 @@
     g_pos = pos_near.astype(wide) + lax.ppermute(pos_near, "pair", swap).astype(wide)
     g_attn_in = shared[:, : 3 * width]
     g_vecs = shared[:, 3 * width : 3 * width + vec_count].T
-    smalls = (g_pos, g_attn_in, g_attn_out, g_mlp_in, g_mlp_out, g_vecs)
-    masters = (pos_table, attn_in, attn_out, mlp_in, mlp_out, vectors)
-    firsts = (pos_m, attn_in_m, attn_out_m, mlp_in_m, mlp_out_m, vectors_m)
-    seconds = (pos_v, attn_in_v, attn_out_v, mlp_in_v, mlp_out_v, vectors_v)
+    smalls = (g_attn_in, g_attn_out, g_mlp_in, g_mlp_out, g_vecs)
+    masters = (attn_in, attn_out, mlp_in, mlp_out, vectors)
+    firsts = (attn_in_m, attn_out_m, mlp_in_m, mlp_out_m, vectors_m)
+    seconds = (attn_in_v, attn_out_v, mlp_in_v, mlp_out_v, vectors_v)
     small_out = run_adam(factor, list(zip(masters, firsts, seconds, smalls)))
-    return (*table_out, *small_out, grad_norm, kl_mean)
+    pos_out = adam_update(pos_table, pos_m, pos_v, g_pos, factor)
+    return (*table_out, *pos_out, *small_out, grad_norm, kl_mean)
 
 
 def solution(mesh):

time: 542 us -> 536 us (0.989)
    sub x1 -> x2, other arithmetic: 24.4 us -> 25.5 us  [adam_update(): master - learn_rate * (fixed_one / (jnp.sqrt(fixed_two) + adam_eps) + dec...]
    unnamed x79 -> x83, local copies, waits for them, and re-layouts: 12.4 us -> 11.5 us
  transfers between devices with their start and end apart: 45 -> 45, of which waited for: 21 -> 19; matrix products, arithmetic and copies ran while one was open for 20% -> 19% of each run, Pallas kernels for 7% -> 8%
where the time goes in v5:
time: 536 us; the launch traced here: 527 us
  waiting for transfers between devices  200 us (37%)
  starting transfers between devices  85.5 us (16%)
  Pallas kernels  72.7 us (14%)
  local copies, waits for them, and re-layouts  59.2 us (11%)
  other arithmetic  44.2 us (8%)
  blocking collectives  25.6 us (5%)
  between operations  21.3 us (4%)
  matrix products  18 us (3%)
    all_to_all x1, waiting for transfers between devices, shards(): lax.all_to_all(chips, 'dp', split_axis=0, concat_axis=0, axis_index_group...  44.6 us
    ppermute x10, waiting for transfers between devices, over(): return lax.ppermute(value, 'pair', to_teacher)  38.8 us
    ppermute x1, waiting for transfers between devices, ring_gather(): first = lax.ppermute(ahead[:half_rows], 'dp', onward)  34.1 us
    ppermute x3, waiting for transfers between devices, step(): lax.ppermute(ahead, 'dp', onward)  27.8 us
    all_gather x1, waiting for transfers between devices, shards(): rights = lax.all_gather(rights, 'dp', axis=0, tiled=True)  26 us
    all_gather x1, blocking collectives, shards(): every = lax.all_gather(both.reshape(2 * picks, width), 'dp', axis=0)  25.6 us
    sub x2, other arithmetic, adam_update(): master - learn_rate * (fixed_one / (jnp.sqrt(fixed_two) + adam_eps) + dec...  25.5 us
    all_to_all x1, starting transfers between devices, shards(): lefts = lax.all_to_all(lefts, 'dp', split_axis=0, concat_axis=0, tiled=True)  20.8 us
  transfers between devices with their start and end apart: 45, of which 19 were waited for; matrix products, arithmetic and copies ran while one was open for 19% of the time, Pallas kernels for 8%

profile of v5, /device:TPU:0, one launch (start us, length us, event | category | flops | bytes accessed | tf_op | source)
XLA Modules:
  0.0 526.8 jit_solution(2129147292428628761)
XLA Ops:
  8.9 4.3 route_tokens.1
  14.6 7.4 %all-to-all-start = ((s32[16,1,160]{2,1,0:T(1,128)}), s32[16,1,160]{2,1,0:T(1,128)S(1)}, u32[]{:S(2)}, u32[]{:S(2)}) async-start(s32[16,1,160]{2,1,0:T(1,128)} %copy.72), calls=%async_computation | async-start | bytes 32768 | tf_op jit(solution)/shard_map/all_to_all | solution.py:1021
  22.0 6.5 %all-to-all-done = s32[16,1,160]{2,1,0:T(1,128)S(1)} async-done(((s32[16,1,160]{2,1,0:T(1,128)}), s32[16,1,160]{2,1,0:T(1,128)S(1)}, u32[]{:S(2)}, u32[]{:S(2)}) %all-to-all-start) | async-done | bytes 10272 | tf_op jit(solution)/shard_map/all_to_all | solution.py:1021
  34.2 15.2 %conditional.1 = (bf16[16,128,768]{2,1,0:T(8,128)(2,1)S(1)}) conditional(s32[]{:T(128)} %convert_element_type.93, (s32[16,128]{1,0:T(8,128)S(1)}, bf16[3144,768]{1,0:T(8,128)(2,1)}) %tuple.34, (s32[16,128]{1,0:T(8,128)S(1)}, f32[3144,768]{1,0:T(8,128)}) %tuple.35), branch_computations={%region_0.1_spmd, %region_1.0_spmd} | conditional | flops 1593344 | bytes 12619784 | solution.py:1040
  34.2 13.1 %gather_fusion = bf16[2048,768]{1,0:T(8,128)(2,1)} fusion(bf16[3144,768]{1,0:T(8,128)(2,1)} %get-tuple-element.12, s32[2048]{0:T(1024)S(1)} %bitcast_clamp_fusion), kind=kCustom, calls=%fused_computation | custom fusion | bytes 6299648 | tf_op jit(solution)/shard_map/cond/branch_0_fun/jit(_take)/gather | solution.py:1043
  49.4 6.4 %collective-permute-done = bf16[656,768]{1,0:T(8,128)(2,1)} collective-permute-done((bf16[656,768]{1,0:T(8,128)(2,1)}, bf16[656,768]{1,0:T(8,128)(2,1)}, u32[]{:S(2)}, u32[]{:S(2)}) %collective-permute-start) | collective-permute-done | bytes 1007648 | tf_op jit(solution)/shard_map/ppermute | solution.py:93
  58.4 21.4 %collective-permute-done.2 = bf16[656,768]{1,0:T(8,128)(2,1)} collective-permute-done((bf16[656,768]{1,0:T(8,128)(2,1)}, bf16[656,768]{1,0:T(8,128)(2,1)}, u32[]{:S(2)}, u32[]{:S(2)}) %collective-permute-start.2) | collective-permute-done | bytes 1007648 | tf_op jit(solution)/shard_map/ppermute | solution.py:93
  82.1 3.7 all-to-all-start.1
  96.3 4.0 collective-permute-done.11
  105.1 3.9 collective-permute-done.13
  109.5 6.0 %collective-permute-done.10 = bf16[656,768]{1,0:T(8,128)(2,1)} collective-permute-done((bf16[656,768]{1,0:T(8,128)(2,1)}, bf16[656,768]{1,0:T(8,128)(2,1)}, u32[]{:S(2)}, u32[]{:S(2)}) %collective-permute-start.10) | collective-permute-done | bytes 1007648 | tf_op jit(solution)/shard_map/ppermute | solution.py:93
  130.3 34.1 %collective-permute-done.16 = bf16[320,768]{1,0:T(8,128)(2,1)S(1)} collective-permute-done((bf16[320,768]{1,0:T(8,128)(2,1)S(1)}, bf16[320,768]{1,0:T(8,128)(2,1)S(1)}, u32[]{:S(2)}, u32[]{:S(2)}) %collective-permute-start.16) | collective-permute-done | bytes 491552 | tf_op jit(solution)/shard_map/ppermute | solution.py:110
  169.8 5.6 %copy-done.16 = bf16[16,656,768]{2,1,0:T(8,128)(2,1)} copy-done((bf16[16,656,768]{2,1,0:T(8,128)(2,1)}, bf16[16,656,768]{2,1,0:T(8,128)(2,1)S(1)}, u32[]{:S(2)}) %copy-start.16) | copy-done | bytes 16121880
  177.3 15.2 %layer_forward.1 = (bf16[16,768]{1,0:T(8,128)(2,1)}, bf16[16,768]{1,0:T(8,128)(2,1)S(1)}, f32[32,768]{1,0:T(8,128)S(1)}, f32[2,512,768]{2,1,0:T(8,128)S(1)}, bf1...) custom-call(s32[1]{0:T(128)} %bitcast.4.flag_ref.refs_0_, ...), custom_call_target="tpu_custom_call" | custom-call | flops 1500000000 | bytes 51000000 | tf_op jit(solution)/shard_map/layer_forward/pallas_call | solution.py:340
  196.4 20.8 %all-to-all-start.2 = ((bf16[16,32,288]{2,1,0:T(8,128)(2,1)}), bf16[16,32,288]{2,1,0:T(8,128)(2,1)S(1)}, u32[]{:S(2)}, u32[]{:S(2)}) async-start(bf16[16,32,288]{2,1,0:T(8,128)(2,1)} %copy-done.7), calls=%async_computation.2 | async-start | bytes 786432 | tf_op jit(solution)/shard_map/all_to_all | solution.py:1095
  221.0 25.6 %all_gather.12 = bf16[16,32,768]{2,1,0:T(8,128)(2,1)} all-gather(bf16[1,32,768]{2,1,0:T(8,128)(2,1)S(1)} %bitcast.153), channel_id=1, replica_groups=mesh['pair'=2,'dp'=16] {'dp'}, dimensions={0}, use_global_device_ids=true | all-gather | bytes 835584 | tf_op jit(solution)/shard_map/all_gather | solution.py:1090
  248.5 5.5 %fusion.40 = (f32[256]{0:T(256)S(1)}, f32[256,3144]{0,1:T(8,128)S(1)}) fusion(bf16[256,768]{1,0:T(8,128)(2,1)S(1)} %bitcast.137, f32[3144,768]{1,0:T(8,128)} %param.45), kind=kOutput, calls=%fused_computation.127 | convolution fusion | flops 1239490304 | bytes 13272064 | tf_op jit(solution)/shard_map/dot_general | solution.py:55
  262.6 3.6 all-to-all-start.3
  267.6 27.1 %collective-permute-done.24 = f32[336,768]{1,0:T(8,128)} collective-permute-done((f32[336,768]{1,0:T(8,128)}, f32[336,768]{1,0:T(8,128)}, u32[]{:S(2)}, u32[]{:S(2)}) %collective-permute-start.24) | collective-permute-done | bytes 1032224 | tf_op jit(solution)/shard_map/ppermute | solution.py:1047
  298.5 6.7 %upper_backward.1 = (f32[16,1536]{1,0:T(8,128)S(1)}, f32[16,1536]{1,0:T(8,128)S(1)}, f32[16,768]{1,0:T(8,128)S(1)}, bf16[32,4608]{1,0:T(8,128)(2,1)}) custom-call(f32[32,768]{1,0:T(8,128)S(1)} %fusion.25.d_final_ref, f32[16,768]{1,0:T(8,128)S(1)} %reshape.379.vec_ref, f32[32,768]{1,0:T(8,128)S(1)} %get-tuple-element.166.mid_ref, f32[32,3072]{1,0:T(8,128)S(1)} %copy-done.9, ...), custom_call_target="tpu_custom_call" | custom-call | flops 900000000 | bytes 30600000 | tf_op jit(solution)/shard_map/upper_backward/pallas_call | solution.py:567
  310.2 3.5 multiply_reduce_fusion
  315.4 17.0 %lower_backward.1 = (bf16[16,64,768]{2,1,0:T(8,128)(2,1)S(1)}, bf16[8,48,2688]{2,1,0:T(8,128)(2,1)S(1)}, bf16[8,48,2688]{2,1,0:T(8,128)(2,1)}, f32[16,768]{1,0:T(8,128)}, f32[8,768]{1,0:T(8,128)}) custom-call(s32[1]{0:T(128)} %bitcast.4.flag_ref.refs_0_, f32[16,768]{1,0:T(8,128)S(1)} %slice.199.d_mid_ref, bf16[16,768]{1,0:T(8,128)(2,1)S(1)} %slice.248.d_attended_ref, ...), custom_call_target="tpu_custom_call" | custom-call | flops 1500000000 | bytes 51000000 | tf_op jit(solution)/shard_map/lower_backward/pallas_call | solution.py:602
  333.5 6.3 %all-to-all-start.4 = ((bf16[16,64,768]{2,1,0:T(8,128)(2,1)}), bf16[16,64,768]{2,1,0:T(8,128)(2,1)}, u32[]{:S(2)}, u32[]{:S(2)}) async-start(bf16[16,64,768]{2,1,0:T(8,128)(2,1)} %copy-done.2), calls=%async_computation.4 | async-start | bytes 3145728 | tf_op jit(solution)/shard_map/all_to_all | solution.py:1185
  341.9 10.1 %collective-permute-done.31.refs_4_ = bf16[256,768]{1,0:T(8,128)(2,1)S(1)} collective-permute-done((bf16[256,768]{1,0:T(8,128)(2,1)}, bf16[256,768]{1,0:T(8,128)(2,1)S(1)}, u32[]{:S(2)}, u32[]{:S(2)}) %collective-permute-start.31) | collective-permute-done | bytes 393248 | tf_op jit(solution)/shard_map/ppermute | solution.py:1184
  352.0 3.6 add_convert_fusion
  355.6 26.0 %all-gather.4.cloned.1.call-done = bf16[512,4608]{1,0:T(8,128)(2,1)} async-done(((bf16[32,4608]{1,0:T(8,128)(2,1)}), bf16[512,4608]{1,0:T(8,128)(2,1)}) %all-gather.4.cloned.1.call-update) | async-done | bytes 4718608 | tf_op jit(solution)/shard_map/all_gather | solution.py:1200
  391.2 3.6 all-to-all-start.5
  394.9 3.5 collective-permute-start.32
  398.4 44.6 %all-to-all-done.5 = bf16[8,48,2688]{2,1,0:T(8,128)(2,1)S(1)} async-done(((bf16[8,48,2688]{2,1,0:T(8,128)(2,1)}), bf16[8,48,2688]{2,1,0:T(8,128)(2,1)S(1)}, u32[]{:S(2)}, u32[]{:S(2)}) %all-to-all-start.5) | async-done | bytes 2064416 | tf_op jit(solution)/shard_map/all_to_all | solution.py:1220
  450.1 17.8 %table_gradient.1 = (f32[3144,768]{1,0:T(8,128)}, f32[8,768]{1,0:T(8,128)}) custom-call(s32[1]{0:T(128)} %bitcast.4.flag_ref.refs_0_, bf16[3144,256]{1,0:T(8,128)(2,1)} %bitcast.136, bf16[256,768]{1,0:T(8,128)(2,1)} %bitcast.139, bf16[3144,256]{1,0:T(8,128)(2,1)} %bitcast.62.refs_3_, bf16[256,768]{1,0:T(8,128)(2,1)} %copy-done.27, ...), custom_call_target="tpu_custom_call" | custom-call | flops 1700000000 | bytes 57800000 | tf_op jit(solution)/shard_map/table_gradient/pallas_call | solution.py:898
  482.1 24.5 %multiply_subtract_fusion = (f32[3144,768]{1,0:T(8,128)}, f32[3144,768]{1,0:T(8,128)}, f32[3144,768]{1,0:T(8,128)}) fusion(f32[3144,768]{1,0:T(8,128)} %param.45, f32[3144,768]{1,0:T(8,128)} %get-tuple-element.199, f32[]{:T(128)} %min_shard_map.3, f32[3144,768]{1,0:T(8,128)} %param.52, f32[3144,768]{1,0:T(8,128)} %param.59), kind=kLoop, calls=%fused_computation.12 | loop fusion | flops 38633472 | bytes 67608576 | tf_op jit(solution)/shard_map/sub | solution.py:138
  509.8 6.4 %small_updates.1 = (f32[48,2304]{1,0:T(8,128)}, f32[48,2304]{1,0:T(8,128)}, f32[48,2304]{1,0:T(8,128)}, f32[48,768]{1,0:T(8,128)}, f32[48,768]{1,0:T(8,128)}, /*...) custom-call(f32[1]{0:T(128)} %bitcast.70.factor_ref, ...), custom_call_target="tpu_custom_call" | custom-call | flops 600000000 | bytes 20400000 | tf_op jit(solution)/shard_map/small_updates/pallas_call | solution.py:952
  (260 shorter events, 117.4 us)
Async XLA Ops:
  14.6 13.9 %all-to-all-start = ((s32[16,1,160]{2,1,0:T(1,128)}), s32[16,1,160]{2,1,0:T(1,128)S(1)}, u32[]{:S(2)}, u32[]{:S(2)}) async-start(s32[16,1,160]{2,1,0:T(1,128)} %copy.72), calls=%async_computation | async-start | bytes 32768 | tf_op jit(solution)/shard_map/all_to_all | solution.py:1021
  31.5 24.3 %collective-permute-start = (bf16[656,768]{1,0:T(8,128)(2,1)}, bf16[656,768]{1,0:T(8,128)(2,1)}, u32[]{:S(2)}, u32[]{:S(2)}) collective-permute-start(bf16[656,768]{1,0:T(8,128)(2,1)} %pack_weights.1), channel_id=1, source_target_pairs={{0,4},{1,5},{4,8},{5,9},{8,12},{9,13},{12,14},{13,15},{14,10},{15,... | collective-permute-start | bytes 3022856 | tf_op jit(solution)/shard_map/ppermute | solution.py:93
  32.0 24.3 %collective-permute-start.1 = (bf16[656,768]{1,0:T(8,128)(2,1)}, bf16[656,768]{1,0:T(8,128)(2,1)}, u32[]{:S(2)}, u32[]{:S(2)}) collective-permute-start(bf16[656,768]{1,0:T(8,128)(2,1)} %pack_weights.1), channel_id=1, source_target_pairs={{4,0},{5,1},{8,4},{9,5},{12,8},{13,9},{14,12},{15,13},{10,14},{11,... | collective-permute-start | bytes 3022856 | tf_op jit(solution)/shard_map/ppermute | solution.py:93
  56.3 23.5 %collective-permute-start.2 = (bf16[656,768]{1,0:T(8,128)(2,1)}, bf16[656,768]{1,0:T(8,128)(2,1)}, u32[]{:S(2)}, u32[]{:S(2)}) collective-permute-start(bf16[656,768]{1,0:T(8,128)(2,1)} %collective-permute-done), channel_id=1, source_target_pairs={{0,4},{1,5},{4,8},{5,9},{8,12},{9,13},{12,14},{13,15},{14,10},{15,... | collective-permute-start | bytes 3022856 | tf_op jit(solution)/shard_map/ppermute | solution.py:93
  56.9 23.2 %collective-permute-start.3 = (bf16[656,768]{1,0:T(8,128)(2,1)}, bf16[656,768]{1,0:T(8,128)(2,1)}, u32[]{:S(2)}, u32[]{:S(2)}) collective-permute-start(bf16[656,768]{1,0:T(8,128)(2,1)} %collective-permute-done.1), channel_id=1, source_target_pairs={{4,0},{5,1},{8,4},{9,5},{12,8},{13,9},{14,12},{15,13},{10,14},{11,... | collective-permute-start | bytes 3022856 | tf_op jit(solution)/shard_map/ppermute | solution.py:93
  80.1 13.6 %collective-permute-start.4 = (bf16[656,768]{1,0:T(8,128)(2,1)}, bf16[656,768]{1,0:T(8,128)(2,1)}, u32[]{:S(2)}, u32[]{:S(2)}) collective-permute-start(bf16[656,768]{1,0:T(8,128)(2,1)} %pack_weights.1), channel_id=1, source_target_pairs={{0,1},{1,0},{2,3},{3,2},{4,5},{5,4},{6,7},{7,6},{8,9},{9,8},{10,11... | collective-permute-start | bytes 3022856 | tf_op jit(solution)/shard_map/ppermute | solution.py:88
  80.1 28.9 %collective-permute-start.9 = (bf16[656,768]{1,0:T(8,128)(2,1)}, bf16[656,768]{1,0:T(8,128)(2,1)}, u32[]{:S(2)}, u32[]{:S(2)}) collective-permute-start(bf16[656,768]{1,0:T(8,128)(2,1)} %collective-permute-done.2), channel_id=1, source_target_pairs={{0,4},{1,5},{4,8},{5,9},{8,12},{9,13},{12,14},{13,15},{14,10},{15,... | collective-permute-start | bytes 3022856 | tf_op jit(solution)/shard_map/ppermute | solution.py:93
  80.7 34.8 %collective-permute-start.10 = (bf16[656,768]{1,0:T(8,128)(2,1)}, bf16[656,768]{1,0:T(8,128)(2,1)}, u32[]{:S(2)}, u32[]{:S(2)}) collective-permute-start(bf16[656,768]{1,0:T(8,128)(2,1)} %collective-permute-done.3), channel_id=1, source_target_pairs={{4,0},{5,1},{8,4},{9,5},{12,8},{13,9},{14,12},{15,13},{10,14},{11,... | collective-permute-start | bytes 3022856 | tf_op jit(solution)/shard_map/ppermute | solution.py:93
  82.1 93.4 %all-to-all-start.1 = ((bf16[16,128,768]{2,1,0:T(8,128)(2,1)}), bf16[16,128,768]{2,1,0:T(8,128)(2,1)S(1)}, u32[]{:S(2)}, u32[]{:S(2)}) async-start(bf16[16,128,768]{2,1,0:T(8,128)(2,1)} %copy-done.21), calls=%async_computation.1 | async-start | bytes 6291456 | tf_op jit(solution)/shard_map/all_to_all | solution.py:1064
  86.9 32.1 %collective-permute-start.5 = (bf16[656,768]{1,0:T(8,128)(2,1)}, bf16[656,768]{1,0:T(8,128)(2,1)S(1)}, u32[]{:S(2)}, u32[]{:S(2)}) collective-permute-start(bf16[656,768]{1,0:T(8,128)(2,1)} %collective-permute-done), channel_id=1, source_target_pairs={{0,1},{1,0},{2,3},{3,2},{4,5},{5,4},{6,7},{7,6},{8,9},{9,8},{10,11... | collective-permute-start | bytes 3022856 | tf_op jit(solution)/shard_map/ppermute | solution.py:88
  105.1 16.6 %collective-permute-start.6 = (bf16[656,768]{1,0:T(8,128)(2,1)}, bf16[656,768]{1,0:T(8,128)(2,1)S(1)}, u32[]{:S(2)}, u32[]{:S(2)}) collective-permute-start(bf16[656,768]{1,0:T(8,128)(2,1)} %collective-permute-done.1), channel_id=1, source_target_pairs={{0,1},{1,0},{2,3},{3,2},{4,5},{5,4},{6,7},{7,6},{8,9},{9,8},{10,11... | collective-permute-start | bytes 3022856 | tf_op jit(solution)/shard_map/ppermute | solution.py:88
  109.0 14.2 %collective-permute-start.7 = (bf16[656,768]{1,0:T(8,128)(2,1)}, bf16[656,768]{1,0:T(8,128)(2,1)S(1)}, u32[]{:S(2)}, u32[]{:S(2)}) collective-permute-start(bf16[656,768]{1,0:T(8,128)(2,1)} %collective-permute-done.2), channel_id=1, source_target_pairs={{0,1},{1,0},{2,3},{3,2},{4,5},{5,4},{6,7},{7,6},{8,9},{9,8},{10,11... | collective-permute-start | bytes 3022856 | tf_op jit(solution)/shard_map/ppermute | solution.py:88
  109.0 16.1 %collective-permute-start.8 = (bf16[656,768]{1,0:T(8,128)(2,1)}, bf16[656,768]{1,0:T(8,128)(2,1)S(1)}, u32[]{:S(2)}, u32[]{:S(2)}) collective-permute-start(bf16[656,768]{1,0:T(8,128)(2,1)} %collective-permute-done.3), channel_id=1, source_target_pairs={{0,1},{1,0},{2,3},{3,2},{4,5},{5,4},{6,7},{7,6},{8,9},{9,8},{10,11... | collective-permute-start | bytes 3022856 | tf_op jit(solution)/shard_map/ppermute | solution.py:88
  121.7 45.4 %collective-permute-start.14 = (bf16[656,768]{1,0:T(8,128)(2,1)}, bf16[656,768]{1,0:T(8,128)(2,1)S(1)}, u32[]{:S(2)}, u32[]{:S(2)}) collective-permute-start(bf16[656,768]{1,0:T(8,128)(2,1)} %collective-permute-done.9), channel_id=1, source_target_pairs={{0,1},{1,0},{2,3},{3,2},{4,5},{5,4},{6,7},{7,6},{8,9},{9,8},{10,11... | collective-permute-start | bytes 3022856 | tf_op jit(solution)/shard_map/ppermute | solution.py:88
  123.2 45.3 %collective-permute-start.15 = (bf16[656,768]{1,0:T(8,128)(2,1)}, bf16[656,768]{1,0:T(8,128)(2,1)S(1)}, u32[]{:S(2)}, u32[]{:S(2)}) collective-permute-start(bf16[656,768]{1,0:T(8,128)(2,1)} %collective-permute-done.10), channel_id=1, source_target_pairs={{0,1},{1,0},{2,3},{3,2},{4,5},{5,4},{6,7},{7,6},{8,9},{9,8},{10,11... | collective-permute-start | bytes 3022856 | tf_op jit(solution)/shard_map/ppermute | solution.py:88
  125.1 39.3 %collective-permute-start.16 = (bf16[320,768]{1,0:T(8,128)(2,1)S(1)}, bf16[320,768]{1,0:T(8,128)(2,1)S(1)}, u32[]{:S(2)}, u32[]{:S(2)}) collective-permute-start(bf16[320,768]{1,0:T(8,128)(2,1)S(1)} %slice.149), channel_id=1, source_target_pairs={{0,4},{1,5},{4,8},{5,9},{8,12},{9,13},{12,14},{13,15},{14,10},{15,... | collective-permute-start | bytes 1474568 | tf_op jit(solution)/shard_map/ppermute | solution.py:110
  127.7 39.3 %collective-permute-start.17 = (bf16[336,768]{1,0:T(8,128)(2,1)S(1)}, bf16[336,768]{1,0:T(8,128)(2,1)S(1)}, u32[]{:S(2)}, u32[]{:S(2)}) collective-permute-start(bf16[336,768]{1,0:T(8,128)(2,1)S(1)} %slice.150), channel_id=1, source_target_pairs={{4,0},{5,1},{8,4},{9,5},{12,8},{13,9},{14,12},{15,13},{10,14},{11,... | collective-permute-start | bytes 1548296 | tf_op jit(solution)/shard_map/ppermute | solution.py:111
  194.9 23.4 %collective-permute-start.19 = (bf16[16,768]{1,0:T(8,128)(2,1)}, bf16[16,768]{1,0:T(8,128)(2,1)S(1)}, u32[]{:S(2)}, u32[]{:S(2)}) collective-permute-start(bf16[16,768]{1,0:T(8,128)(2,1)} %get-tuple-element.148), channel_id=1, source_target_pairs={{0,16},{16,0},{1,17},{17,1},{2,18},{18,2},{3,19},{19,3},{4,20},{20... | collective-permute-start | bytes 73736 | tf_op jit(solution)/shard_map/ppermute | solution.py:1077
  196.4 50.1 %all-to-all-start.2 = ((bf16[16,32,288]{2,1,0:T(8,128)(2,1)}), bf16[16,32,288]{2,1,0:T(8,128)(2,1)S(1)}, u32[]{:S(2)}, u32[]{:S(2)}) async-start(bf16[16,32,288]{2,1,0:T(8,128)(2,1)} %copy-done.7), calls=%async_computation.2 | async-start | bytes 786432 | tf_op jit(solution)/shard_map/all_to_all | solution.py:1095
  218.3 28.2 %collective-permute-start.20 = (f32[208,768]{1,0:T(8,128)}, f32[208,768]{1,0:T(8,128)}, u32[]{:S(2)}, u32[]{:S(2)}) collective-permute-start(f32[208,768]{1,0:T(8,128)} %slice_bitcast_fusion.2), channel_id=1, source_target_pairs={{16,0},{17,1},{18,2},{19,3},{20,4},{21,5},{22,6},{23,7},{24,8},{25... | collective-permute-start | bytes 1916936 | tf_op jit(solution)/shard_map/ppermute | solution.py:1047
  219.6 41.8 %collective-permute-start.23 = (bf16[3,144,768]{2,1,0:T(8,128)(2,1)}, bf16[3,144,768]{2,1,0:T(8,128)(2,1)S(1)}, u32[]{:S(2)}, u32[]{:S(2)}) collective-permute-start(bf16[3,144,768]{2,1,0:T(8,128)(2,1)} %pad_maximum_fusion.4), channel_id=1, source_target_pairs={{16,0},{17,1},{18,2},{19,3},{20,4},{21,5},{22,6},{23,7},{24,8},{25... | collective-permute-start | bytes 1990664 | tf_op jit(solution)/shard_map/ppermute | solution.py:1047
  262.6 32.1 %all-to-all-start.3 = ((bf16[16,36,768]{2,1,0:T(8,128)(2,1)}), bf16[16,36,768]{2,1,0:T(8,128)(2,1)S(1)}, u32[]{:S(2)}, u32[]{:S(2)}) async-start(bf16[16,36,768]{2,1,0:T(8,128)(2,1)} %pad_maximum_fusion.3), calls=%async_computation.3 | async-start | bytes 1966080 | tf_op jit(solution)/shard_map/all_to_all | solution.py:1126
  266.3 115.3 %all-gather.4.cloned.1.call-start = ((), (), s32[]{:S(2)}) async-start(), calls=%async_computation.7 | async-start | bytes 5013504 | tf_op jit(solution)/shard_map/all_gather | solution.py:1200
  266.3 28.4 %collective-permute-start.24 = (f32[336,768]{1,0:T(8,128)}, f32[336,768]{1,0:T(8,128)}, u32[]{:S(2)}, u32[]{:S(2)}) collective-permute-start(f32[336,768]{1,0:T(8,128)} %pad_maximum_fusion.1), channel_id=1, source_target_pairs={{16,0},{17,1},{18,2},{19,3},{20,4},{21,5},{22,6},{23,7},{24,8},{25... | collective-permute-start | bytes 3096584 | tf_op jit(solution)/shard_map/ppermute | solution.py:1047
  333.5 18.5 %collective-permute-start.30 = (bf16[8,48,2688]{2,1,0:T(8,128)(2,1)}, bf16[8,48,2688]{2,1,0:T(8,128)(2,1)}, u32[]{:S(2)}, u32[]{:S(2)}) collective-permute-start(bf16[8,48,2688]{2,1,0:T(8,128)(2,1)} %get-tuple-element.188), channel_id=1, source_target_pairs={{0,1},{1,0},{2,3},{3,2},{4,5},{5,4},{6,7},{7,6},{8,9},{9,8},{10,11... | collective-permute-start | bytes 6193160 | tf_op jit(solution)/shard_map/ppermute | solution.py:1074
  333.5 57.6 %all-to-all-start.4 = ((bf16[16,64,768]{2,1,0:T(8,128)(2,1)}), bf16[16,64,768]{2,1,0:T(8,128)(2,1)}, u32[]{:S(2)}, u32[]{:S(2)}) async-start(bf16[16,64,768]{2,1,0:T(8,128)(2,1)} %copy-done.2), calls=%async_computation.4 | async-start | bytes 3145728 | tf_op jit(solution)/shard_map/all_to_all | solution.py:1185
  339.9 51.3 %collective-permute-start.29 = (bf16[256,3144]{0,1:T(8,128)(2,1)}, bf16[256,3144]{0,1:T(8,128)(2,1)}, u32[]{:S(2)}, u32[]{:S(2)}) collective-permute-start(bf16[256,3144]{0,1:T(8,128)(2,1)} %get-tuple-element.185), channel_id=1, source_target_pairs={{0,16},{16,0},{1,17},{17,1},{2,18},{18,2},{3,19},{19,3},{4,20},{20... | collective-permute-start | bytes 4829192 | tf_op jit(solution)/shard_map/ppermute | solution.py:1198
  391.2 51.8 %all-to-all-start.5 = ((bf16[8,48,2688]{2,1,0:T(8,128)(2,1)}), bf16[8,48,2688]{2,1,0:T(8,128)(2,1)S(1)}, u32[]{:S(2)}, u32[]{:S(2)}) async-start(bf16[8,48,2688]{2,1,0:T(8,128)(2,1)} %add_convert_fusion), calls=%async_computation.5 | async-start | bytes 4128768 | tf_op jit(solution)/shard_map/all_to_all | solution.py:1220
  394.8 111.8 %all-gather.6.cloned.1.call-start = ((), (), s32[]{:S(2)}) async-start(), calls=%async_computation.8 | async-start | bytes 1671168 | tf_op jit(solution)/shard_map/all_gather | solution.py:1242
  394.9 48.4 %collective-permute-start.32 = (bf16[1024,768]{1,0:T(8,128)(2,1)}, bf16[1024,768]{1,0:T(8,128)(2,1)}, u32[]{:S(2)}, u32[]{:S(2)}) collective-permute-start(bf16[1024,768]{1,0:T(8,128)(2,1)} %bitcast.57.refs_7_), channel_id=1, source_target_pairs={{0,16},{16,0},{1,17},{17,1},{2,18},{18,2},{3,19},{19,3},{4,20},{20... | collective-permute-start | bytes 4718600 | tf_op jit(solution)/shard_map/ppermute | solution.py:1216
  443.3 24.7 %collective-permute-start.33 = (bf16[432,768]{1,0:T(8,128)(2,1)S(1)}, bf16[432,768]{1,0:T(8,128)(2,1)S(1)}, u32[]{:S(2)}, u32[]{:S(2)}) collective-permute-start(bf16[432,768]{1,0:T(8,128)(2,1)S(1)} %pad_maximum_fusion.5), channel_id=1, source_target_pairs={{16,0},{17,1},{18,2},{19,3},{20,4},{21,5},{22,6},{23,7},{24,8},{25... | collective-permute-start | bytes 1990664 | tf_op jit(solution)/shard_map/ppermute | solution.py:1047
  444.7 23.3 %collective-permute-start.34 = (bf16[48,2688]{1,0:T(8,128)(2,1)S(1)}, bf16[48,2688]{1,0:T(8,128)(2,1)S(1)}, u32[]{:S(2)}, u32[]{:S(2)}) collective-permute-start(bf16[48,2688]{1,0:T(8,128)(2,1)S(1)} %reduce_sum.89.mine_ref), channel_id=1, source_target_pairs={{0,16},{16,0},{1,17},{17,1},{2,18},{18,2},{3,19},{19,3},{4,20},{20... | collective-permute-start | bytes 774152 | tf_op jit(solution)/shard_map/ppermute | solution.py:1248
  (51 other events, 577.3 us)
Sparse Core Ops, SparseCore 0:
  305.4 76.1 all-gather.3
  450.2 38.0 all-gather.5
